TPU v7x, 32 devices: a whole 2x2x4 slice. The times are simulated.
32 devices in a mesh: energy: 4 (over x, core), atom: 8 (over z, y).
Axes of the slice: x: 2, y: 2, z: 4, core: 2. Of those that a mesh axis runs over, the one named last changes fastest.
Arguments:
- green: float32 [2, 8, 16, 128, 128], P(None, 'energy', 'atom'), may hold values from -6 to 6
- coupling: float32 [16, 6, 128, 128], P('atom'), may hold values from -0.5 to 0.5
- phonon: float32 [16, 6, 4], P('atom'), may hold values from 0.2 to 2
- neighbours: int32 [16, 6], P('atom'), may hold values from 0 to 15, as said below
Outputs:
- self_energy: float32 [2, 8, 16, 128, 128], P(None, 'energy', 'atom')
- rates: float32 [16, 128], P('atom')
Inputs may be any that keep to these rules, and one draw needn't show every extreme that they name: `neighbours`: each entry lies within 2 of its row's index and within 0 to 15; offsets +2 and -2 both occur.
All inputs are finite; a program needn't handle non-finite values.
Results may differ from a plain program's by a relative error of at most 0.000071.
Values sent between devices are 32-bit elements; how exact they have to be, the bound alone decides.
No kernel may reach another device: no remote copies, remote signals or barrier semaphores. Data moves between devices by JAX's collectives and lax.ppermute only.
A program may use at most 64 MiB of HBM per device.

v0:
```python
import functools

import jax
import jax.numpy as jnp
from jax import lax
from jax.experimental import pallas as pl
from jax.experimental.pallas import tpu as pltpu
from jax.sharding import PartitionSpec as P

SHIFTS = (-2, -1, 1, 2)
REACH = max(SHIFTS)
OWN, PAIR, FAR = 0, 1, 2
FEW = 4
VMEM = pl.BlockSpec(memory_space=pltpu.VMEM)
SMEM = pl.BlockSpec(memory_space=pltpu.SMEM)
ANY = pl.BlockSpec(memory_space=pl.ANY)


def halves(x):
    high = x.astype(jnp.bfloat16)
    return high, (x - high.astype(jnp.float32)).astype(jnp.bfloat16)


def swap(x, axis, first, close=False):
    size = lax.axis_size(axis)
    pairs = [(i, i + 1) for i in range(first, size - 1, 2)]
    if close and first == 1 and size % 2 == 0:
        pairs.append((0, size - 1))
    return lax.ppermute(x, axis, pairs + [(j, i) for i, j in pairs])


def exchange(x, partner, spare):
    energies, atoms = lax.axis_size("energy"), lax.axis_size("atom")
    perm = []
    for e in range(energies):
        for a in range(atoms):
            to_e, to_a = partner(e, a)
            if not (0 <= to_e < energies and 0 <= to_a < atoms):
                to_e, to_a = spare(e, a)
            if 0 <= to_e < energies and 0 <= to_a < atoms:
                perm.append((e * atoms + a, to_e * atoms + to_a))
    return lax.ppermute(x, ("energy", "atom"), perm)


def cross_swap(x):
    step = 2 if lax.axis_size("atom") % 4 == 0 else 1
    return exchange(x, lambda e, a: (e + 1 if e % 2 else e - 1, a), lambda e, a: (e, a ^ step))


def forward(x, axis):
    size = lax.axis_size(axis)
    ups = [(i, min(i + 2, size - 1)) for i in range(0, size, 2)]
    downs = [(i, max(i - 2, 0)) for i in range(1, size, 2)]
    return lax.ppermute(x, axis, [(i, j) for i, j in ups + downs if i != j])


def put_blocks(blocks, c, green):
    orb = green.shape[-1]
    for e in range(green.shape[0]):
        for a in range(green.shape[1]):
            high, low = halves(green[e, a])
            blocks[c, a, e, :, :orb] = high
            blocks[c, a, e, :, orb:] = low


def add_pairs(group, neighbours, phonon, coupling, blocks, totals, picked, size):
    atoms, slots, orb = coupling.shape[0], coupling.shape[1], coupling.shape[-1]
    e_local = blocks.shape[2]
    index = lax.axis_index("atom")
    base = index * atoms
    if group != OWN:
        upper = (index & 1) == (0 if group == PAIR else 1)
        base += jnp.where(upper, atoms, -atoms)

    found = jnp.int32(0)
    for a in range(atoms):
        for j in range(slots):
            picked[found] = a * slots + j
            b = neighbours[a, j] - base
            found += ((b >= 0) & (b < atoms)).astype(jnp.int32)

    def batch(step, _):
        pairs = []
        for u in range(size):
            at = step * size + u
            item = picked[jnp.minimum(at, found - 1)]
            a = item // slots
            j = item - a * slots
            high, low = halves(coupling[a, j])
            left = jnp.concatenate([high, low], 1)
            right = jnp.concatenate(
                [jnp.concatenate([high, high], 1), jnp.concatenate([low, low], 1)], 0
            )
            pairs.append((a, j, neighbours[a, j] - base, jnp.where(at < found, 1.0, 0.0), left, right))
        inners = []
        for a, j, b, live, left, right in pairs:
            for c in range(len(totals)):
                near = blocks[c, b].reshape(e_local * orb, 2 * orb)
                inner = lax.dot_general(
                    near, right, (((1,), (1,)), ((), ())), preferred_element_type=jnp.float32
                )
                inners.append(inner[:, :orb] + inner[:, orb:])
        results = []
        for a, j, b, live, left, right in pairs:
            for total in totals:
                inner = inners.pop(0)
                sums = [None] * (e_local + 2 * REACH)
                for e in range(e_local):
                    high, low = halves(inner[e * orb : (e + 1) * orb])
                    both = jnp.concatenate([high, low], 1)
                    outer = jnp.dot(
                        left, jnp.concatenate([both, both], 0), preferred_element_type=jnp.float32
                    )
                    outer = outer[:, :orb] + outer[:, orb:]
                    for k, s in enumerate(SHIFTS):
                        d = e - s + REACH
                        term = (phonon[a, k, j] * live) * outer
                        sums[d] = term if sums[d] is None else sums[d] + term
                results.append((total, a, sums))
        for total, a, sums in results:
            for d, value in enumerate(sums):
                if value is not None:
                    total[d, a] += value

    lax.fori_loop(0, (found + size - 1) // size, batch, None)


def fetch_kernel(green, coupling, phonon, neighbours, *rest):
    *results, sems = rest
    sources = [green.at[0], green.at[1], green, coupling, phonon, neighbours]
    copies = [
        pltpu.make_async_copy(source, result, sems.at[i])
        for i, (source, result) in enumerate(zip(sources, results))
    ]
    for copy in copies:
        copy.start()
    for copy in copies:
        copy.wait()


def own_kernel(neighbours, phonon, coupling, green0, green1, total0, total1, blocks, picked):
    for c, (green, total) in enumerate(((green0, total0), (green1, total1))):
        put_blocks(blocks, c, green)
        total[...] = jnp.zeros_like(total)
    add_pairs(OWN, neighbours, phonon, coupling, blocks, (total0, total1), picked, 2)


def pair_kernel(neighbours, phonon, coupling, ahead, before, total, blocks, picked):
    total[...] = before[...]
    put_blocks(blocks, 0, ahead)
    add_pairs(PAIR, neighbours, phonon, coupling, blocks, (total,), picked, 4)


def turn_kernel(
    size, neighbours, phonon, coupling, ahead, before, green, by_core, by_cross,
    total, turned, blocks, picked,
):
    e_local, a_local = green.shape[1], green.shape[2]
    core, cross = partner_energies(turned.shape[1])
    has_core, has_cross = has_partners(size)
    for c in range(2):
        for a in range(a_local):
            for e in range(e_local):
                turned[c, REACH + e, a] = green[c, e, a].T
            for e in range(REACH):
                turned[c, core + e, a] = by_core[c, e, a].T * has_core
                turned[c, cross + e, a] = by_cross[c, e, a].T * has_cross
    pair_kernel(neighbours, phonon, coupling, ahead, before, total, blocks, picked)


def partner_energies(spread):
    odd = lax.axis_index("energy") & 1
    return jnp.where(odd == 0, spread - REACH, 0), jnp.where(odd == 0, 0, spread - REACH)


def has_partners(size):
    me = lax.axis_index("energy")
    above, below = jnp.where(me < size - 1, 1.0, 0.0), jnp.where(me > 0, 1.0, 0.0)
    odd = me & 1
    return jnp.where(odd == 0, above, below), jnp.where(odd == 0, below, above)


def finish(total, core, cross):
    to_core, to_cross = partner_energies(total.shape[0])
    for e in range(REACH):
        core[e] = total[to_core + e]
        cross[e] = total[to_cross + e]


def rate_sums(total, turned, c, a):
    sums = total[0, a] * turned[c, 0, a]
    for d in range(1, total.shape[0]):
        sums += total[d, a] * turned[c, d, a]
    return sums


def far_kernel(
    neighbours, phonon, coupling, across, before, turned, total, core, cross, partial, blocks, picked
):
    add_far(neighbours, phonon, coupling, across, before, total, blocks, picked)
    finish(total, core, cross)
    for a in range(partial.shape[0]):
        partial[a] = rate_sums(total, turned, 0, a)


def add_far(neighbours, phonon, coupling, across, before, total, blocks, picked):
    total[...] = before[...]
    put_blocks(blocks, 0, across)
    add_pairs(FAR, neighbours, phonon, coupling, blocks, (total,), picked, 4)


def last_kernel(
    scale, neighbours, phonon, coupling, across, before, turned, partial,
    total, core, cross, rate, blocks, picked,
):
    add_far(neighbours, phonon, coupling, across, before, total, blocks, picked)
    finish(total, core, cross)
    for a in range(partial.shape[0]):
        sums = partial[a] - rate_sums(total, turned, 1, a)
        rate[a : a + 1, :] = jnp.sum(sums.T, axis=0, keepdims=True) * scale


def addends(x, axis):
    size = lax.axis_size(axis)
    if size > FEW:
        return [lax.psum(x, axis)]
    turns = [[(i, (i + k) % size) for i in range(size)] for k in range(1, size)]
    return [x] + [lax.ppermute(x, axis, turn) for turn in turns]


def end_kernel(size, total0, total1, cross0, core0, cross1, core1, *rest):
    *rates, out, rate = rest
    e_local = out.shape[1]
    has_core, has_cross = has_partners(size)
    for c, (total, cross, core) in enumerate(((total0, cross0, core0), (total1, cross1, core1))):
        for e in range(e_local):
            out[c, e] = total[REACH + e] + core[e] * has_core + cross[e] * has_cross
    rate[...] = sum(r[...] for r in rates)


def per_device(green, coupling, phonon, neighbours):
    _, e_local, a_local, orb, _ = green.shape
    energies = lax.axis_size("energy")
    points = e_local * energies
    spread = (e_local + 2 * REACH, a_local, orb, orb)
    edge = (REACH, a_local, orb, orb)

    def call(kernel, out, operands, parts=1):
        return pl.pallas_call(
            kernel,
            out_shape=[jax.ShapeDtypeStruct(shape, jnp.float32) for shape in out],
            in_specs=[SMEM, SMEM] + [VMEM] * (1 + len(operands)),
            out_specs=[VMEM] * len(out),
            scratch_shapes=[
                pltpu.VMEM((parts, a_local, e_local, orb, 2 * orb), jnp.bfloat16),
                pltpu.SMEM((a_local * neighbours.shape[1] + 1,), jnp.int32),
            ],
            compiler_params=pltpu.CompilerParams(vmem_limit_bytes=24 * 2**20),
            cost_estimate=pl.CostEstimate(flops=10**6, bytes_accessed=10**4, transcendentals=0),
        )(neighbours, phonon, coupling, *operands)

    sources = (green, coupling, jnp.swapaxes(phonon, 1, 2), neighbours)
    green0, green1, green, coupling, phonon, neighbours = pl.pallas_call(
        fetch_kernel,
        out_shape=[jax.ShapeDtypeStruct(green.shape[1:], green.dtype)] * 2
        + [jax.ShapeDtypeStruct(x.shape, x.dtype) for x in sources],
        in_specs=[ANY] * 4,
        out_specs=[VMEM] * 6,
        scratch_shapes=[pltpu.SemaphoreType.DMA((6,))],
        compiler_params=pltpu.CompilerParams(vmem_limit_bytes=24 * 2**20),
    )(*(pltpu.with_memory_space_constraint(x, pltpu.HBM) for x in sources))
    ahead1 = swap(green1, "atom", 0)
    ahead0 = swap(green0, "atom", 0)
    by_core, by_cross = swap(green, "energy", 0), swap(green, "energy", 1, close=True)
    total0, total1 = call(own_kernel, [spread] * 2, (green0, green1), parts=2)
    ahead0, total0, total1 = lax.optimization_barrier((ahead0, total0, total1))
    across0 = forward(ahead0, "atom")
    (total0,) = call(pair_kernel, [spread], (ahead0, total0))
    green1, total0 = lax.optimization_barrier((green1, total0))
    across1 = swap(green1, "atom", 1)
    total1, turned = call(
        functools.partial(turn_kernel, energies),
        [spread, (2,) + spread],
        (ahead1, total1, green, by_core, by_cross),
    )
    total0, core0, cross0, partial = call(
        far_kernel, [spread, edge, edge, (a_local, orb, orb)], (across0, total0, turned)
    )
    core0, cross0 = swap(core0, "energy", 0), cross_swap(cross0)
    total1, core1, cross1, rate = call(
        functools.partial(last_kernel, 1.0 / (4.0 * points)),
        [spread, edge, edge, (a_local, orb)],
        (across1, total1, turned, partial),
    )
    core1, cross1 = swap(core1, "energy", 0), cross_swap(cross1)
    cross0, core0, rate = lax.optimization_barrier((cross0, core0, rate))
    rates = addends(rate, "energy")
    return pl.pallas_call(
        functools.partial(end_kernel, energies),
        out_shape=[
            jax.ShapeDtypeStruct(green.shape, jnp.float32),
            jax.ShapeDtypeStruct((a_local, orb), jnp.float32),
        ],
        in_specs=[VMEM] * (6 + len(rates)),
        out_specs=[VMEM] * 2,
        compiler_params=pltpu.CompilerParams(vmem_limit_bytes=24 * 2**20),
        cost_estimate=pl.CostEstimate(flops=10**6, bytes_accessed=2 * 10**6, transcendentals=0),
    )(total0, total1, cross0, core0, cross1, core1, *rates)


def solution(mesh):
    return jax.shard_map(
        per_device,
        mesh=mesh,
        in_specs=(
            P(None, "energy", "atom", None, None),
            P("atom", None, None, None),
            P("atom", None, None),
            P("atom", None),
        ),
        out_specs=(P(None, "energy", "atom", None, None), P("atom", None)),
        check_vma=False,
    )
```

profile of v0, /device:TPU:0, one launch (start us, length us, event | category | flops | bytes accessed | tf_op | source)
XLA Modules:
  0.0 35.4 jit_solution(9323327546548901992)
XLA Ops:
  0.6 1.5 %shard_map.59 = (f32[2,2,128,128]{3,2,1,0:T(8,128)S(1)}, f32[2,2,128,128]{3,2,1,0:T(8,128)S(1)}, f32[2,2,2,128,128]{4,3,2,1,0:T(8,128)S(1)}, f32[2,6,128,128]{3,...) custom-call(f32[2,2,2,128,128]{4,3,2,1,0:T(8,128)} %green.1, f32[2,6,128,128]{3,2,1,0:T(8,128)} %coupling.1, ...), custom_call_target="tpu_custom_call" | custom-call | tf_op jit(solution)/shard_map/pallas_call | solution.py:263
  2.2 3.0 %collective-permute-start = (f32[2,2,128,128]{3,2,1,0:T(8,128)S(1)}, f32[2,2,128,128]{3,2,1,0:T(8,128)S(1)}, u32[]{:S(2)}, u32[]{:S(2)}) collective-permute-start(f32[2,2,128,128]{3,2,1,0:T(8,128)S(1)} %get-tuple-element.31.green0), channel_id=1, source_target_pairs={{0,1},{2,3},{4,5},{6,7},{1,0},{3,2},{5,4},{7,6},{8,9},{10,11},{12,... | collective-permute-start | bytes 786440 | tf_op jit(solution)/shard_map/ppermute | solution.py:29
  5.2 0.7 %collective-permute-start.4 = (f32[2,2,2,128,128]{4,3,2,1,0:T(8,128)S(1)}, f32[2,2,2,128,128]{4,3,2,1,0:T(8,128)S(1)}, u32[]{:S(2)}, u32[]{:S(2)}) collective-permute-start(f32[2,2,2,128,128]{4,3,2,1,0:T(8,128)S(1)} %get-tuple-element.39.green), channel_id=1, source_target_pairs={{8,16},{0,24},{16,8},{24,0},{9,17},{1,25},{17,9},{25,1},{10,18},{2... | collective-permute-start | bytes 1572872 | tf_op jit(solution)/shard_map/ppermute | solution.py:29
  5.8 1.0 %collective-permute-start.3 = (f32[2,2,2,128,128]{4,3,2,1,0:T(8,128)S(1)}, f32[2,2,2,128,128]{4,3,2,1,0:T(8,128)S(1)}, u32[]{:S(2)}, u32[]{:S(2)}) collective-permute-start(f32[2,2,2,128,128]{4,3,2,1,0:T(8,128)S(1)} %get-tuple-element.39.green), channel_id=1, source_target_pairs={{0,8},{16,24},{8,0},{24,16},{1,9},{17,25},{9,1},{25,17},{2,10},{18... | collective-permute-start | bytes 1572872 | tf_op jit(solution)/shard_map/ppermute | solution.py:29
  6.8 0.5 %collective-permute-start.2 = (f32[2,2,128,128]{3,2,1,0:T(8,128)S(1)}, f32[2,2,128,128]{3,2,1,0:T(8,128)S(1)}, u32[]{:S(2)}, u32[]{:S(2)}) collective-permute-start(f32[2,2,128,128]{3,2,1,0:T(8,128)S(1)} %get-tuple-element.42.green1), channel_id=1, source_target_pairs={{0,1},{2,3},{4,5},{6,7},{1,0},{3,2},{5,4},{7,6},{8,9},{10,11},{12,... | collective-permute-start | bytes 786440 | tf_op jit(solution)/shard_map/ppermute | solution.py:29
  7.3 3.8 %shard_map.60 = (f32[6,2,128,128]{3,2,1,0:T(8,128)S(1)}, f32[6,2,128,128]{3,2,1,0:T(8,128)S(1)}) custom-call(s32[2,6]{1,0:T(2,128)S(1)} %get-tuple-element.28.neighbours, f32[2,4,6]{2,1,0:T(4,128)S(1)} %get-tuple-element.29.phonon, f32[2,6,128,128]{3,2,1,0:T(8,128)S(1)} %get-tuple-element.30.coupling, f32[2,2,128,128]{3,2,1,0:T(8,128)S(1)} %get-tuple-element.31.green0, ...), custom_call_target="tpu_custom_call" | custom-call | flops 1000000 | bytes 10000 | tf_op jit(solution)/shard_map/pallas_call | solution.py:249
  11.2 1.2 %collective-permute-done.ahead = f32[2,2,128,128]{3,2,1,0:T(8,128)S(1)} collective-permute-done((f32[2,2,128,128]{3,2,1,0:T(8,128)S(1)}, f32[2,2,128,128]{3,2,1,0:T(8,128)S(1)}, u32[]{:S(2)}, u32[]{:S(2)}) %collective-permute-start) | collective-permute-done | bytes 262176 | tf_op jit(solution)/shard_map/ppermute | solution.py:29
  12.3 2.1 %collective-permute-start.1 = (f32[2,2,128,128]{3,2,1,0:T(8,128)S(1)}, f32[2,2,128,128]{3,2,1,0:T(8,128)S(1)}, u32[]{:S(2)}, u32[]{:S(2)}) collective-permute-start(f32[2,2,128,128]{3,2,1,0:T(8,128)S(1)} %collective-permute-done.ahead), channel_id=1, source_target_pairs={{0,2},{2,4},{4,6},{6,7},{1,0},{3,1},{5,3},{7,5},{8,10},{10,12},{12... | collective-permute-start | bytes 786440 | tf_op jit(solution)/shard_map/ppermute | solution.py:54
  14.4 1.3 %shard_map.61.before = f32[6,2,128,128]{3,2,1,0:T(8,128)S(1)} custom-call(s32[2,6]{1,0:T(2,128)S(1)} %get-tuple-element.28.neighbours, f32[2,4,6]{2,1,0:T(4,128)S(1)} %get-tuple-element.29.phonon, f32[2,6,128,128]{3,2,1,0:T(8,128)S(1)} %get-tuple-element.30.coupling, f32[2,2,128,128]{3,2,1,0:T(8,128)S(1)} %collective-permute-done.ahead, ...), custom_call_target="tpu_custom_call" | custom-call | flops 1000000 | bytes 10000 | tf_op jit(solution)/shard_map/pallas_call | solution.py:249
  15.8 0.7 %collective-permute-start.5 = (f32[2,2,128,128]{3,2,1,0:T(8,128)S(1)}, f32[2,2,128,128]{3,2,1,0:T(8,128)S(1)}, u32[]{:S(2)}, u32[]{:S(2)}) collective-permute-start(f32[2,2,128,128]{3,2,1,0:T(8,128)S(1)} %get-tuple-element.42.green1), channel_id=1, source_target_pairs={{1,2},{3,4},{5,6},{2,1},{4,3},{6,5},{9,10},{11,12},{13,14},{10,9},... | collective-permute-start | bytes 786440 | tf_op jit(solution)/shard_map/ppermute | solution.py:29
  16.5 1.5 %collective-permute-done.2.ahead = f32[2,2,128,128]{3,2,1,0:T(8,128)S(1)} collective-permute-done((f32[2,2,128,128]{3,2,1,0:T(8,128)S(1)}, f32[2,2,128,128]{3,2,1,0:T(8,128)S(1)}, u32[]{:S(2)}, u32[]{:S(2)}) %collective-permute-start.2) | collective-permute-done | bytes 262176 | tf_op jit(solution)/shard_map/ppermute | solution.py:29
  17.9 1.4 %collective-permute-done.4.by_cross = f32[2,2,2,128,128]{4,3,2,1,0:T(8,128)S(1)} collective-permute-done((f32[2,2,2,128,128]{4,3,2,1,0:T(8,128)S(1)}, f32[2,2,2,128,128]{4,3,2,1,0:T(8,128)S(1)}, u32[]{:S(2)}, u32[]{:S(2)}) %collective-permute-start.4) | collective-permute-done | bytes 524320 | tf_op jit(solution)/shard_map/ppermute | solution.py:29
  19.4 0.0 collective-permute-done.3.by_core
  19.4 1.7 %shard_map.62 = (f32[6,2,128,128]{3,2,1,0:T(8,128)S(1)}, f32[2,6,2,128,128]{4,3,2,1,0:T(8,128)S(1)}) custom-call(s32[2,6]{1,0:T(2,128)S(1)} %get-tuple-element.28.neighbours, f32[2,4,6]{2,1,0:T(4,128)S(1)} %get-tuple-element.29.phonon, f32[2,6,128,128]{3,2,1,0:T(8,128)S(1)} %get-tuple-element.30.coupling, ...), custom_call_target="tpu_custom_call" | custom-call | flops 1000000 | bytes 10000 | tf_op jit(solution)/shard_map/pallas_call | solution.py:249
  21.1 1.6 %collective-permute-done.1.across = f32[2,2,128,128]{3,2,1,0:T(8,128)S(1)} collective-permute-done((f32[2,2,128,128]{3,2,1,0:T(8,128)S(1)}, f32[2,2,128,128]{3,2,1,0:T(8,128)S(1)}, u32[]{:S(2)}, u32[]{:S(2)}) %collective-permute-start.1) | collective-permute-done | bytes 262176 | tf_op jit(solution)/shard_map/ppermute | solution.py:54
  22.7 0.9 %shard_map.63 = (f32[6,2,128,128]{3,2,1,0:T(8,128)S(1)}, f32[2,2,128,128]{3,2,1,0:T(8,128)S(1)}, f32[2,2,128,128]{3,2,1,0:T(8,128)S(1)}, f32[2,128,128]{2,1,0:T(8,128)S(1)}) custom-call(s32[2,6]{1,0:T(2,128)S(1)} %get-tuple-element.28.neighbours, f32[2,4,6]{2,1,0:T(4,128)S(1)} %get-tuple-element.29.phonon, ...), custom_call_target="tpu_custom_call" | custom-call | flops 1000000 | bytes 10000 | tf_op jit(solution)/shard_map/pallas_call | solution.py:249
  23.6 0.7 %collective-permute-start.6 = (f32[2,2,128,128]{3,2,1,0:T(8,128)S(1)}, f32[2,2,128,128]{3,2,1,0:T(8,128)S(1)}, u32[]{:S(2)}, u32[]{:S(2)}) collective-permute-start(f32[2,2,128,128]{3,2,1,0:T(8,128)S(1)} %get-tuple-element.46), channel_id=1, source_target_pairs={{0,2},{1,3},{2,0},{3,1},{4,6},{5,7},{6,4},{7,5},{8,16},{9,17},{10,... | collective-permute-start | bytes 786440 | tf_op jit(solution)/shard_map/ppermute | solution.py:42
  24.2 1.2 %collective-permute-start.7 = (f32[2,2,128,128]{3,2,1,0:T(8,128)S(1)}, f32[2,2,128,128]{3,2,1,0:T(8,128)S(1)}, u32[]{:S(2)}, u32[]{:S(2)}) collective-permute-start(f32[2,2,128,128]{3,2,1,0:T(8,128)S(1)} %get-tuple-element.47), channel_id=1, source_target_pairs={{0,8},{16,24},{8,0},{24,16},{1,9},{17,25},{9,1},{25,17},{2,10},{18... | collective-permute-start | bytes 786440 | tf_op jit(solution)/shard_map/ppermute | solution.py:29
  25.5 0.0 collective-permute-done.5.across
  25.5 0.9 %shard_map.64 = (f32[6,2,128,128]{3,2,1,0:T(8,128)S(1)}, f32[2,2,128,128]{3,2,1,0:T(8,128)S(1)}, f32[2,2,128,128]{3,2,1,0:T(8,128)S(1)}, f32[2,128]{1,0:T(2,128)S(1)}) custom-call(s32[2,6]{1,0:T(2,128)S(1)} %get-tuple-element.28.neighbours, f32[2,4,6]{2,1,0:T(4,128)S(1)} %get-tuple-element.29.phonon, f32[2,6,128,128]{3,2,1,0:T(8,128)S(1)} %get-tuple-element.30.coupling, ...), custom_call_target="tpu_custom_call" | custom-call | flops 1000000 | bytes 10000 | tf_op jit(solution)/shard_map/pallas_call | solution.py:249
  26.3 1.8 %collective-permute-start.8 = (f32[2,2,128,128]{3,2,1,0:T(8,128)S(1)}, f32[2,2,128,128]{3,2,1,0:T(8,128)S(1)}, u32[]{:S(2)}, u32[]{:S(2)}) collective-permute-start(f32[2,2,128,128]{3,2,1,0:T(8,128)S(1)} %get-tuple-element.51), channel_id=1, source_target_pairs={{0,2},{1,3},{2,0},{3,1},{4,6},{5,7},{6,4},{7,5},{8,16},{9,17},{10,... | collective-permute-start | bytes 786440 | tf_op jit(solution)/shard_map/ppermute | solution.py:42
  28.1 0.0 collective-permute-start.9
  28.1 1.9 %collective-permute-done.6.cross0 = f32[2,2,128,128]{3,2,1,0:T(8,128)S(1)} collective-permute-done((f32[2,2,128,128]{3,2,1,0:T(8,128)S(1)}, f32[2,2,128,128]{3,2,1,0:T(8,128)S(1)}, u32[]{:S(2)}, u32[]{:S(2)}) %collective-permute-start.6) | collective-permute-done | bytes 262176 | tf_op jit(solution)/shard_map/ppermute | solution.py:42
  30.0 0.0 collective-permute-done.7.core0
  30.0 0.0 collective-permute-start.12
  30.0 1.4 %collective-permute-start.11 = (f32[2,128]{1,0:T(2,128)S(1)}, f32[2,128]{1,0:T(2,128)S(1)}, u32[]{:S(2)}, u32[]{:S(2)}) collective-permute-start(f32[2,128]{1,0:T(2,128)S(1)} %get-tuple-element.53.rest_0_), channel_id=1, source_target_pairs={{0,16},{8,24},{16,0},{24,8},{1,17},{9,25},{17,1},{25,9},{2,18},{10... | collective-permute-start | bytes 3080 | tf_op jit(solution)/shard_map/ppermute | solution.py:228
  31.5 0.0 collective-permute-start.10
  31.5 1.4 %collective-permute-done.8.cross1 = f32[2,2,128,128]{3,2,1,0:T(8,128)S(1)} collective-permute-done((f32[2,2,128,128]{3,2,1,0:T(8,128)S(1)}, f32[2,2,128,128]{3,2,1,0:T(8,128)S(1)}, u32[]{:S(2)}, u32[]{:S(2)}) %collective-permute-start.8) | collective-permute-done | bytes 262176 | tf_op jit(solution)/shard_map/ppermute | solution.py:42
  32.8 0.0 collective-permute-done.9.core1
  32.8 0.0 collective-permute-done.12.rest_3_
  32.8 0.8 %collective-permute-done.11.rest_2_ = f32[2,128]{1,0:T(2,128)S(1)} collective-permute-done((f32[2,128]{1,0:T(2,128)S(1)}, f32[2,128]{1,0:T(2,128)S(1)}, u32[]{:S(2)}, u32[]{:S(2)}) %collective-permute-start.11) | collective-permute-done | bytes 1056 | tf_op jit(solution)/shard_map/ppermute | solution.py:228
  33.6 0.9 %collective-permute-done.10.rest_1_ = f32[2,128]{1,0:T(2,128)S(1)} collective-permute-done((f32[2,128]{1,0:T(2,128)S(1)}, f32[2,128]{1,0:T(2,128)S(1)}, u32[]{:S(2)}, u32[]{:S(2)}) %collective-permute-start.10) | collective-permute-done | bytes 1056 | tf_op jit(solution)/shard_map/ppermute | solution.py:228
  34.5 0.9 %shard_map.65 = (f32[2,2,2,128,128]{4,3,2,1,0:T(8,128)}, f32[2,128]{1,0:T(2,128)}) custom-call(f32[6,2,128,128]{3,2,1,0:T(8,128)S(1)} %get-tuple-element.41.total0, f32[6,2,128,128]{3,2,1,0:T(8,128)S(1)} %get-tuple-element.45.total1, f32[2,2,128,128]{3,2,1,0:T(8,128)S(1)} %collective-permute-done.6.cross0, ...), custom_call_target="tpu_custom_call" | custom-call | flops 1000000 | bytes 2000000 | tf_op jit(solution)/shard_map/pallas_call | solution.py:298
Async XLA Ops:
  2.2 10.2 %collective-permute-start = (f32[2,2,128,128]{3,2,1,0:T(8,128)S(1)}, f32[2,2,128,128]{3,2,1,0:T(8,128)S(1)}, u32[]{:S(2)}, u32[]{:S(2)}) collective-permute-start(f32[2,2,128,128]{3,2,1,0:T(8,128)S(1)} %get-tuple-element.31.green0), channel_id=1, source_target_pairs={{0,1},{2,3},{4,5},{6,7},{1,0},{3,2},{5,4},{7,6},{8,9},{10,11},{12,... | collective-permute-start | bytes 786440 | tf_op jit(solution)/shard_map/ppermute | solution.py:29
  5.2 14.2 %collective-permute-start.4 = (f32[2,2,2,128,128]{4,3,2,1,0:T(8,128)S(1)}, f32[2,2,2,128,128]{4,3,2,1,0:T(8,128)S(1)}, u32[]{:S(2)}, u32[]{:S(2)}) collective-permute-start(f32[2,2,2,128,128]{4,3,2,1,0:T(8,128)S(1)} %get-tuple-element.39.green), channel_id=1, source_target_pairs={{8,16},{0,24},{16,8},{24,0},{9,17},{1,25},{17,9},{25,1},{10,18},{2... | collective-permute-start | bytes 1572872 | tf_op jit(solution)/shard_map/ppermute | solution.py:29
  5.8 13.5 %collective-permute-start.3 = (f32[2,2,2,128,128]{4,3,2,1,0:T(8,128)S(1)}, f32[2,2,2,128,128]{4,3,2,1,0:T(8,128)S(1)}, u32[]{:S(2)}, u32[]{:S(2)}) collective-permute-start(f32[2,2,2,128,128]{4,3,2,1,0:T(8,128)S(1)} %get-tuple-element.39.green), channel_id=1, source_target_pairs={{0,8},{16,24},{8,0},{24,16},{1,9},{17,25},{9,1},{25,17},{2,10},{18... | collective-permute-start | bytes 1572872 | tf_op jit(solution)/shard_map/ppermute | solution.py:29
  6.8 11.1 %collective-permute-start.2 = (f32[2,2,128,128]{3,2,1,0:T(8,128)S(1)}, f32[2,2,128,128]{3,2,1,0:T(8,128)S(1)}, u32[]{:S(2)}, u32[]{:S(2)}) collective-permute-start(f32[2,2,128,128]{3,2,1,0:T(8,128)S(1)} %get-tuple-element.42.green1), channel_id=1, source_target_pairs={{0,1},{2,3},{4,5},{6,7},{1,0},{3,2},{5,4},{7,6},{8,9},{10,11},{12,... | collective-permute-start | bytes 786440 | tf_op jit(solution)/shard_map/ppermute | solution.py:29
  12.3 10.4 %collective-permute-start.1 = (f32[2,2,128,128]{3,2,1,0:T(8,128)S(1)}, f32[2,2,128,128]{3,2,1,0:T(8,128)S(1)}, u32[]{:S(2)}, u32[]{:S(2)}) collective-permute-start(f32[2,2,128,128]{3,2,1,0:T(8,128)S(1)} %collective-permute-done.ahead), channel_id=1, source_target_pairs={{0,2},{2,4},{4,6},{6,7},{1,0},{3,1},{5,3},{7,5},{8,10},{10,12},{12... | collective-permute-start | bytes 786440 | tf_op jit(solution)/shard_map/ppermute | solution.py:54
  15.8 9.7 %collective-permute-start.5 = (f32[2,2,128,128]{3,2,1,0:T(8,128)S(1)}, f32[2,2,128,128]{3,2,1,0:T(8,128)S(1)}, u32[]{:S(2)}, u32[]{:S(2)}) collective-permute-start(f32[2,2,128,128]{3,2,1,0:T(8,128)S(1)} %get-tuple-element.42.green1), channel_id=1, source_target_pairs={{1,2},{3,4},{5,6},{2,1},{4,3},{6,5},{9,10},{11,12},{13,14},{10,9},... | collective-permute-start | bytes 786440 | tf_op jit(solution)/shard_map/ppermute | solution.py:29
  23.6 6.4 %collective-permute-start.6 = (f32[2,2,128,128]{3,2,1,0:T(8,128)S(1)}, f32[2,2,128,128]{3,2,1,0:T(8,128)S(1)}, u32[]{:S(2)}, u32[]{:S(2)}) collective-permute-start(f32[2,2,128,128]{3,2,1,0:T(8,128)S(1)} %get-tuple-element.46), channel_id=1, source_target_pairs={{0,2},{1,3},{2,0},{3,1},{4,6},{5,7},{6,4},{7,5},{8,16},{9,17},{10,... | collective-permute-start | bytes 786440 | tf_op jit(solution)/shard_map/ppermute | solution.py:42
  24.2 5.8 %collective-permute-start.7 = (f32[2,2,128,128]{3,2,1,0:T(8,128)S(1)}, f32[2,2,128,128]{3,2,1,0:T(8,128)S(1)}, u32[]{:S(2)}, u32[]{:S(2)}) collective-permute-start(f32[2,2,128,128]{3,2,1,0:T(8,128)S(1)} %get-tuple-element.47), channel_id=1, source_target_pairs={{0,8},{16,24},{8,0},{24,16},{1,9},{17,25},{9,1},{25,17},{2,10},{18... | collective-permute-start | bytes 786440 | tf_op jit(solution)/shard_map/ppermute | solution.py:29
  26.3 6.5 %collective-permute-start.8 = (f32[2,2,128,128]{3,2,1,0:T(8,128)S(1)}, f32[2,2,128,128]{3,2,1,0:T(8,128)S(1)}, u32[]{:S(2)}, u32[]{:S(2)}) collective-permute-start(f32[2,2,128,128]{3,2,1,0:T(8,128)S(1)} %get-tuple-element.51), channel_id=1, source_target_pairs={{0,2},{1,3},{2,0},{3,1},{4,6},{5,7},{6,4},{7,5},{8,16},{9,17},{10,... | collective-permute-start | bytes 786440 | tf_op jit(solution)/shard_map/ppermute | solution.py:42
  28.1 4.7 %collective-permute-start.9 = (f32[2,2,128,128]{3,2,1,0:T(8,128)S(1)}, f32[2,2,128,128]{3,2,1,0:T(8,128)S(1)}, u32[]{:S(2)}, u32[]{:S(2)}) collective-permute-start(f32[2,2,128,128]{3,2,1,0:T(8,128)S(1)} %get-tuple-element.52), channel_id=1, source_target_pairs={{0,8},{16,24},{8,0},{24,16},{1,9},{17,25},{9,1},{25,17},{2,10},{18... | collective-permute-start | bytes 786440 | tf_op jit(solution)/shard_map/ppermute | solution.py:29
  30.0 2.8 %collective-permute-start.12 = (f32[2,128]{1,0:T(2,128)S(1)}, f32[2,128]{1,0:T(2,128)S(1)}, u32[]{:S(2)}, u32[]{:S(2)}) collective-permute-start(f32[2,128]{1,0:T(2,128)S(1)} %get-tuple-element.53.rest_0_), channel_id=1, source_target_pairs={{0,24},{8,0},{16,8},{24,16},{1,25},{9,1},{17,9},{25,17},{2,26},{10... | collective-permute-start | bytes 3080 | tf_op jit(solution)/shard_map/ppermute | solution.py:228
  30.0 3.6 %collective-permute-start.11 = (f32[2,128]{1,0:T(2,128)S(1)}, f32[2,128]{1,0:T(2,128)S(1)}, u32[]{:S(2)}, u32[]{:S(2)}) collective-permute-start(f32[2,128]{1,0:T(2,128)S(1)} %get-tuple-element.53.rest_0_), channel_id=1, source_target_pairs={{0,16},{8,24},{16,0},{24,8},{1,17},{9,25},{17,1},{25,9},{2,18},{10... | collective-permute-start | bytes 3080 | tf_op jit(solution)/shard_map/ppermute | solution.py:228
  31.5 3.0 %collective-permute-start.10 = (f32[2,128]{1,0:T(2,128)S(1)}, f32[2,128]{1,0:T(2,128)S(1)}, u32[]{:S(2)}, u32[]{:S(2)}) collective-permute-start(f32[2,128]{1,0:T(2,128)S(1)} %get-tuple-element.53.rest_0_), channel_id=1, source_target_pairs={{0,8},{8,16},{16,24},{24,0},{1,9},{9,17},{17,25},{25,1},{2,10},{10... | collective-permute-start | bytes 3080 | tf_op jit(solution)/shard_map/ppermute | solution.py:228
where the time goes:
time: 35.5 us; the launch traced here: 35.4 us
  starting transfers between devices  13 us (37%)
  Pallas kernels  11.1 us (31%)
  waiting for transfers between devices  10.6 us (30%)
  between operations  0.69 us (2%)
    pallas_call x5, Pallas kernels, call(): pl.pallas_call(kernel, out_shape=[jax.ShapeDtypeStruct(shape, jnp.float32...  8.64 us
    ppermute x7, starting transfers between devices, swap(): return lax.ppermute(x, axis, pairs + [(j, i) for i, j in pairs])  7.05 us
    ppermute x7, waiting for transfers between devices, swap(): return lax.ppermute(x, axis, pairs + [(j, i) for i, j in pairs])  4.08 us
    ppermute x2, waiting for transfers between devices, exchange(): return lax.ppermute(x, ('energy', 'atom'), perm)  3.28 us
    ppermute x2, starting transfers between devices, exchange(): return lax.ppermute(x, ('energy', 'atom'), perm)  2.42 us
    ppermute x1, starting transfers between devices, forward(): return lax.ppermute(x, axis, [(i, j) for i, j in ups + downs if i != j])  2.12 us
    ppermute x3, waiting for transfers between devices, addends(): return [x] + [lax.ppermute(x, axis, turn) for turn in turns]  1.62 us
    ppermute x1, waiting for transfers between devices, forward(): return lax.ppermute(x, axis, [(i, j) for i, j in ups + downs if i != j])  1.61 us
  transfers between devices with their start and end apart: 13, of which 8 were waited for; matrix products, arithmetic and copies ran while one was open for 0% of the time, Pallas kernels for 24%

commit v1 on v0

--- a/solution.py
+++ b/solution.py
@@ -21,12 +21,9 @@
     return high, (x - high.astype(jnp.float32)).astype(jnp.bfloat16)
 
 
-def swap(x, axis, first, close=False):
-    size = lax.axis_size(axis)
-    pairs = [(i, i + 1) for i in range(first, size - 1, 2)]
-    if close and first == 1 and size % 2 == 0:
-        pairs.append((0, size - 1))
-    return lax.ppermute(x, axis, pairs + [(j, i) for i, j in pairs])
+def swap(x, axis, first):
+    low = range(first, lax.axis_size(axis) - 1, 2)
+    return lax.ppermute(x, axis, [(i, i + 1) for i in low] + [(i + 1, i) for i in low])
 
 
 def exchange(x, partner, spare):
@@ -42,8 +39,7 @@
     return lax.ppermute(x, ("energy", "atom"), perm)
 
 
-def cross_swap(x):
-    step = 2 if lax.axis_size("atom") % 4 == 0 else 1
+def cross_swap(x, step):
     return exchange(x, lambda e, a: (e + 1 if e % 2 else e - 1, a), lambda e, a: (e, a ^ step))
 
 
@@ -271,7 +267,7 @@
     )(*(pltpu.with_memory_space_constraint(x, pltpu.HBM) for x in sources))
     ahead1 = swap(green1, "atom", 0)
     ahead0 = swap(green0, "atom", 0)
-    by_core, by_cross = swap(green, "energy", 0), swap(green, "energy", 1, close=True)
+    by_core, by_cross = swap(green, "energy", 0), cross_swap(green, 2)
     total0, total1 = call(own_kernel, [spread] * 2, (green0, green1), parts=2)
     ahead0, total0, total1 = lax.optimization_barrier((ahead0, total0, total1))
     across0 = forward(ahead0, "atom")
@@ -286,13 +282,13 @@
     total0, core0, cross0, partial = call(
         far_kernel, [spread, edge, edge, (a_local, orb, orb)], (across0, total0, turned)
     )
-    core0, cross0 = swap(core0, "energy", 0), cross_swap(cross0)
+    core0, cross0 = swap(core0, "energy", 0), cross_swap(cross0, 2)
     total1, core1, cross1, rate = call(
         functools.partial(last_kernel, 1.0 / (4.0 * points)),
         [spread, edge, edge, (a_local, orb)],
         (across1, total1, turned, partial),
     )
-    core1, cross1 = swap(core1, "energy", 0), cross_swap(cross1)
+    core1, cross1 = swap(core1, "energy", 0), cross_swap(cross1, 1)
     cross0, core0, rate = lax.optimization_barrier((cross0, core0, rate))
     rates = addends(rate, "energy")
     return pl.pallas_call(

time: 35.5 us -> 35.5 us (level)
  waiting for transfers between devices: 10.6 us -> 11.4 us
  Pallas kernels: 11.1 us -> 10.5 us
    ppermute x1, waiting for transfers between devices: 1.61 us -> 3.03 us  [forward(): return lax.ppermute(x, axis, [(i, j) for i, j in ups + downs if i != j])]
    ppermute x7 -> x6, starting transfers between devices: 7.05 us -> 6 us  [swap(): lax.ppermute(x, axis, [(i, i + 1) for i in low] + [(i + 1, i) for i in low])]
    ppermute x7 -> x6, waiting for transfers between devices: 4.08 us -> 3.25 us  [swap(): lax.ppermute(x, axis, [(i, i + 1) for i in low] + [(i + 1, i) for i in low])]
    ppermute x2 -> x3, starting transfers between devices: 2.42 us -> 3.24 us  [exchange(): return lax.ppermute(x, ('energy', 'atom'), perm)]
    pallas_call x5, Pallas kernels: 8.64 us -> 8.04 us  [call(): pl.pallas_call(kernel, out_shape=[jax.ShapeDtypeStruct(shape, jnp.float32...]
    ppermute x2 -> x3, waiting for transfers between devices: 3.28 us -> 3.46 us  [exchange(): return lax.ppermute(x, ('energy', 'atom'), perm)]
  transfers between devices with their start and end apart: 13 -> 13, of which waited for: 8 -> 7; matrix products, arithmetic and copies ran while one was open for 0% -> 0% of each run, Pallas kernels for 24% -> 23%
where the time goes in v1:
time: 35.5 us; the launch traced here: 35.4 us
  starting transfers between devices  12.8 us (36%)
  waiting for transfers between devices  11.4 us (32%)
  Pallas kernels  10.5 us (30%)
  between operations  0.69 us (2%)
    pallas_call x5, Pallas kernels, call(): pl.pallas_call(kernel, out_shape=[jax.ShapeDtypeStruct(shape, jnp.float32...  8.04 us
    ppermute x6, starting transfers between devices, swap(): lax.ppermute(x, axis, [(i, i + 1) for i in low] + [(i + 1, i) for i in low])  6 us
    ppermute x3, waiting for transfers between devices, exchange(): return lax.ppermute(x, ('energy', 'atom'), perm)  3.46 us
    ppermute x6, waiting for transfers between devices, swap(): lax.ppermute(x, axis, [(i, i + 1) for i in low] + [(i + 1, i) for i in low])  3.25 us
    ppermute x3, starting transfers between devices, exchange(): return lax.ppermute(x, ('energy', 'atom'), perm)  3.24 us
    ppermute x1, waiting for transfers between devices, forward(): return lax.ppermute(x, axis, [(i, j) for i, j in ups + downs if i != j])  3.03 us
    ppermute x1, starting transfers between devices, forward(): return lax.ppermute(x, axis, [(i, j) for i, j in ups + downs if i != j])  2.12 us
    ppermute x3, waiting for transfers between devices, addends(): return [x] + [lax.ppermute(x, axis, turn) for turn in turns]  1.67 us
  transfers between devices with their start and end apart: 13, of which 7 were waited for; matrix products, arithmetic and copies ran while one was open for 0% of the time, Pallas kernels for 23%

profile of v1, /device:TPU:0, one launch (start us, length us, event | category | flops | bytes accessed | tf_op | source)
XLA Modules:
  0.0 35.4 jit_solution(10786822816623043401)
XLA Ops:
  0.6 1.5 %shard_map.59 = (f32[2,2,128,128]{3,2,1,0:T(8,128)S(1)}, f32[2,2,128,128]{3,2,1,0:T(8,128)S(1)}, f32[2,2,2,128,128]{4,3,2,1,0:T(8,128)S(1)}, f32[2,6,128,128]{3,...) custom-call(f32[2,2,2,128,128]{4,3,2,1,0:T(8,128)} %green.1, f32[2,6,128,128]{3,2,1,0:T(8,128)} %coupling.1, ...), custom_call_target="tpu_custom_call" | custom-call | tf_op jit(solution)/shard_map/pallas_call | solution.py:259
  2.2 3.0 %collective-permute-start = (f32[2,2,128,128]{3,2,1,0:T(8,128)S(1)}, f32[2,2,128,128]{3,2,1,0:T(8,128)S(1)}, u32[]{:S(2)}, u32[]{:S(2)}) collective-permute-start(f32[2,2,128,128]{3,2,1,0:T(8,128)S(1)} %get-tuple-element.31.green0), channel_id=1, source_target_pairs={{0,1},{2,3},{4,5},{6,7},{1,0},{3,2},{5,4},{7,6},{8,9},{10,11},{12,... | collective-permute-start | bytes 786440 | tf_op jit(solution)/shard_map/ppermute | solution.py:26
  5.2 1.6 %collective-permute-start.4 = (f32[2,2,2,128,128]{4,3,2,1,0:T(8,128)S(1)}, f32[2,2,2,128,128]{4,3,2,1,0:T(8,128)S(1)}, u32[]{:S(2)}, u32[]{:S(2)}) collective-permute-start(f32[2,2,2,128,128]{4,3,2,1,0:T(8,128)S(1)} %get-tuple-element.39.green), channel_id=1, source_target_pairs={{0,2},{1,3},{2,0},{3,1},{4,6},{5,7},{6,4},{7,5},{8,16},{9,17},{10,... | collective-permute-start | bytes 1572872 | tf_op jit(solution)/shard_map/ppermute | solution.py:39
  6.8 0.0 collective-permute-start.3
  6.8 0.5 %collective-permute-start.2 = (f32[2,2,128,128]{3,2,1,0:T(8,128)S(1)}, f32[2,2,128,128]{3,2,1,0:T(8,128)S(1)}, u32[]{:S(2)}, u32[]{:S(2)}) collective-permute-start(f32[2,2,128,128]{3,2,1,0:T(8,128)S(1)} %get-tuple-element.42.green1), channel_id=1, source_target_pairs={{0,1},{2,3},{4,5},{6,7},{1,0},{3,2},{5,4},{7,6},{8,9},{10,11},{12,... | collective-permute-start | bytes 786440 | tf_op jit(solution)/shard_map/ppermute | solution.py:26
  7.3 3.2 %shard_map.60 = (f32[6,2,128,128]{3,2,1,0:T(8,128)S(1)}, f32[6,2,128,128]{3,2,1,0:T(8,128)S(1)}) custom-call(s32[2,6]{1,0:T(2,128)S(1)} %get-tuple-element.28.neighbours, f32[2,4,6]{2,1,0:T(4,128)S(1)} %get-tuple-element.29.phonon, f32[2,6,128,128]{3,2,1,0:T(8,128)S(1)} %get-tuple-element.30.coupling, f32[2,2,128,128]{3,2,1,0:T(8,128)S(1)} %get-tuple-element.31.green0, ...), custom_call_target="tpu_custom_call" | custom-call | flops 1000000 | bytes 10000 | tf_op jit(solution)/shard_map/pallas_call | solution.py:245
  10.6 1.8 %collective-permute-done.ahead = f32[2,2,128,128]{3,2,1,0:T(8,128)S(1)} collective-permute-done((f32[2,2,128,128]{3,2,1,0:T(8,128)S(1)}, f32[2,2,128,128]{3,2,1,0:T(8,128)S(1)}, u32[]{:S(2)}, u32[]{:S(2)}) %collective-permute-start) | collective-permute-done | bytes 262176 | tf_op jit(solution)/shard_map/ppermute | solution.py:26
  12.3 2.1 %collective-permute-start.1 = (f32[2,2,128,128]{3,2,1,0:T(8,128)S(1)}, f32[2,2,128,128]{3,2,1,0:T(8,128)S(1)}, u32[]{:S(2)}, u32[]{:S(2)}) collective-permute-start(f32[2,2,128,128]{3,2,1,0:T(8,128)S(1)} %collective-permute-done.ahead), channel_id=1, source_target_pairs={{0,2},{2,4},{4,6},{6,7},{1,0},{3,1},{5,3},{7,5},{8,10},{10,12},{12... | collective-permute-start | bytes 786440 | tf_op jit(solution)/shard_map/ppermute | solution.py:50
  14.4 1.3 %shard_map.61.before = f32[6,2,128,128]{3,2,1,0:T(8,128)S(1)} custom-call(s32[2,6]{1,0:T(2,128)S(1)} %get-tuple-element.28.neighbours, f32[2,4,6]{2,1,0:T(4,128)S(1)} %get-tuple-element.29.phonon, f32[2,6,128,128]{3,2,1,0:T(8,128)S(1)} %get-tuple-element.30.coupling, f32[2,2,128,128]{3,2,1,0:T(8,128)S(1)} %collective-permute-done.ahead, ...), custom_call_target="tpu_custom_call" | custom-call | flops 1000000 | bytes 10000 | tf_op jit(solution)/shard_map/pallas_call | solution.py:245
  15.8 0.7 %collective-permute-start.5 = (f32[2,2,128,128]{3,2,1,0:T(8,128)S(1)}, f32[2,2,128,128]{3,2,1,0:T(8,128)S(1)}, u32[]{:S(2)}, u32[]{:S(2)}) collective-permute-start(f32[2,2,128,128]{3,2,1,0:T(8,128)S(1)} %get-tuple-element.42.green1), channel_id=1, source_target_pairs={{1,2},{3,4},{5,6},{2,1},{4,3},{6,5},{9,10},{11,12},{13,14},{10,9},... | collective-permute-start | bytes 786440 | tf_op jit(solution)/shard_map/ppermute | solution.py:26
  16.5 1.5 %collective-permute-done.2.ahead = f32[2,2,128,128]{3,2,1,0:T(8,128)S(1)} collective-permute-done((f32[2,2,128,128]{3,2,1,0:T(8,128)S(1)}, f32[2,2,128,128]{3,2,1,0:T(8,128)S(1)}, u32[]{:S(2)}, u32[]{:S(2)}) %collective-permute-start.2) | collective-permute-done | bytes 262176 | tf_op jit(solution)/shard_map/ppermute | solution.py:26
  17.9 0.0 collective-permute-done.4.by_cross
  17.9 0.0 collective-permute-done.3.by_core
  17.9 1.7 %shard_map.62 = (f32[6,2,128,128]{3,2,1,0:T(8,128)S(1)}, f32[2,6,2,128,128]{4,3,2,1,0:T(8,128)S(1)}) custom-call(s32[2,6]{1,0:T(2,128)S(1)} %get-tuple-element.28.neighbours, f32[2,4,6]{2,1,0:T(4,128)S(1)} %get-tuple-element.29.phonon, f32[2,6,128,128]{3,2,1,0:T(8,128)S(1)} %get-tuple-element.30.coupling, ...), custom_call_target="tpu_custom_call" | custom-call | flops 1000000 | bytes 10000 | tf_op jit(solution)/shard_map/pallas_call | solution.py:245
  19.7 3.0 %collective-permute-done.1.across = f32[2,2,128,128]{3,2,1,0:T(8,128)S(1)} collective-permute-done((f32[2,2,128,128]{3,2,1,0:T(8,128)S(1)}, f32[2,2,128,128]{3,2,1,0:T(8,128)S(1)}, u32[]{:S(2)}, u32[]{:S(2)}) %collective-permute-start.1) | collective-permute-done | bytes 262176 | tf_op jit(solution)/shard_map/ppermute | solution.py:50
  22.7 0.9 %shard_map.63 = (f32[6,2,128,128]{3,2,1,0:T(8,128)S(1)}, f32[2,2,128,128]{3,2,1,0:T(8,128)S(1)}, f32[2,2,128,128]{3,2,1,0:T(8,128)S(1)}, f32[2,128,128]{2,1,0:T(8,128)S(1)}) custom-call(s32[2,6]{1,0:T(2,128)S(1)} %get-tuple-element.28.neighbours, f32[2,4,6]{2,1,0:T(4,128)S(1)} %get-tuple-element.29.phonon, ...), custom_call_target="tpu_custom_call" | custom-call | flops 1000000 | bytes 10000 | tf_op jit(solution)/shard_map/pallas_call | solution.py:245
  23.6 0.1 collective-permute-start.6
  23.7 1.8 %collective-permute-start.7 = (f32[2,2,128,128]{3,2,1,0:T(8,128)S(1)}, f32[2,2,128,128]{3,2,1,0:T(8,128)S(1)}, u32[]{:S(2)}, u32[]{:S(2)}) collective-permute-start(f32[2,2,128,128]{3,2,1,0:T(8,128)S(1)} %get-tuple-element.47), channel_id=1, source_target_pairs={{0,8},{16,24},{8,0},{24,16},{1,9},{17,25},{9,1},{25,17},{2,10},{18... | collective-permute-start | bytes 786440 | tf_op jit(solution)/shard_map/ppermute | solution.py:26
  25.5 0.0 collective-permute-done.5.across
  25.5 0.9 %shard_map.64 = (f32[6,2,128,128]{3,2,1,0:T(8,128)S(1)}, f32[2,2,128,128]{3,2,1,0:T(8,128)S(1)}, f32[2,2,128,128]{3,2,1,0:T(8,128)S(1)}, f32[2,128]{1,0:T(2,128)S(1)}) custom-call(s32[2,6]{1,0:T(2,128)S(1)} %get-tuple-element.28.neighbours, f32[2,4,6]{2,1,0:T(4,128)S(1)} %get-tuple-element.29.phonon, f32[2,6,128,128]{3,2,1,0:T(8,128)S(1)} %get-tuple-element.30.coupling, ...), custom_call_target="tpu_custom_call" | custom-call | flops 1000000 | bytes 10000 | tf_op jit(solution)/shard_map/pallas_call | solution.py:245
  26.3 1.5 %collective-permute-start.8 = (f32[2,2,128,128]{3,2,1,0:T(8,128)S(1)}, f32[2,2,128,128]{3,2,1,0:T(8,128)S(1)}, u32[]{:S(2)}, u32[]{:S(2)}) collective-permute-start(f32[2,2,128,128]{3,2,1,0:T(8,128)S(1)} %get-tuple-element.51), channel_id=1, source_target_pairs={{0,1},{1,0},{2,3},{3,2},{4,5},{5,4},{6,7},{7,6},{8,16},{9,17},{10,... | collective-permute-start | bytes 786440 | tf_op jit(solution)/shard_map/ppermute | solution.py:39
  27.9 0.0 collective-permute-start.9
  27.9 2.1 %collective-permute-done.6.cross0 = f32[2,2,128,128]{3,2,1,0:T(8,128)S(1)} collective-permute-done((f32[2,2,128,128]{3,2,1,0:T(8,128)S(1)}, f32[2,2,128,128]{3,2,1,0:T(8,128)S(1)}, u32[]{:S(2)}, u32[]{:S(2)}) %collective-permute-start.6) | collective-permute-done | bytes 262176 | tf_op jit(solution)/shard_map/ppermute | solution.py:39
  30.0 0.0 collective-permute-done.7.core0
  30.0 0.0 collective-permute-start.12
  30.0 1.4 %collective-permute-start.11 = (f32[2,128]{1,0:T(2,128)S(1)}, f32[2,128]{1,0:T(2,128)S(1)}, u32[]{:S(2)}, u32[]{:S(2)}) collective-permute-start(f32[2,128]{1,0:T(2,128)S(1)} %get-tuple-element.53.rest_0_), channel_id=1, source_target_pairs={{0,16},{8,24},{16,0},{24,8},{1,17},{9,25},{17,1},{25,9},{2,18},{10... | collective-permute-start | bytes 3080 | tf_op jit(solution)/shard_map/ppermute | solution.py:224
  31.5 0.0 collective-permute-start.10
  31.5 1.3 %collective-permute-done.8.cross1 = f32[2,2,128,128]{3,2,1,0:T(8,128)S(1)} collective-permute-done((f32[2,2,128,128]{3,2,1,0:T(8,128)S(1)}, f32[2,2,128,128]{3,2,1,0:T(8,128)S(1)}, u32[]{:S(2)}, u32[]{:S(2)}) %collective-permute-start.8) | collective-permute-done | bytes 262176 | tf_op jit(solution)/shard_map/ppermute | solution.py:39
  32.8 0.0 collective-permute-done.9.core1
  32.8 0.0 collective-permute-done.12.rest_3_
  32.8 0.8 %collective-permute-done.11.rest_2_ = f32[2,128]{1,0:T(2,128)S(1)} collective-permute-done((f32[2,128]{1,0:T(2,128)S(1)}, f32[2,128]{1,0:T(2,128)S(1)}, u32[]{:S(2)}, u32[]{:S(2)}) %collective-permute-start.11) | collective-permute-done | bytes 1056 | tf_op jit(solution)/shard_map/ppermute | solution.py:224
  33.6 0.9 %collective-permute-done.10.rest_1_ = f32[2,128]{1,0:T(2,128)S(1)} collective-permute-done((f32[2,128]{1,0:T(2,128)S(1)}, f32[2,128]{1,0:T(2,128)S(1)}, u32[]{:S(2)}, u32[]{:S(2)}) %collective-permute-start.10) | collective-permute-done | bytes 1056 | tf_op jit(solution)/shard_map/ppermute | solution.py:224
  34.5 0.9 %shard_map.65 = (f32[2,2,2,128,128]{4,3,2,1,0:T(8,128)}, f32[2,128]{1,0:T(2,128)}) custom-call(f32[6,2,128,128]{3,2,1,0:T(8,128)S(1)} %get-tuple-element.41.total0, f32[6,2,128,128]{3,2,1,0:T(8,128)S(1)} %get-tuple-element.45.total1, f32[2,2,128,128]{3,2,1,0:T(8,128)S(1)} %collective-permute-done.6.cross0, ...), custom_call_target="tpu_custom_call" | custom-call | flops 1000000 | bytes 2000000 | tf_op jit(solution)/shard_map/pallas_call | solution.py:294
Async XLA Ops:
  2.2 10.2 %collective-permute-start = (f32[2,2,128,128]{3,2,1,0:T(8,128)S(1)}, f32[2,2,128,128]{3,2,1,0:T(8,128)S(1)}, u32[]{:S(2)}, u32[]{:S(2)}) collective-permute-start(f32[2,2,128,128]{3,2,1,0:T(8,128)S(1)} %get-tuple-element.31.green0), channel_id=1, source_target_pairs={{0,1},{2,3},{4,5},{6,7},{1,0},{3,2},{5,4},{7,6},{8,9},{10,11},{12,... | collective-permute-start | bytes 786440 | tf_op jit(solution)/shard_map/ppermute | solution.py:26
  5.2 12.8 %collective-permute-start.4 = (f32[2,2,2,128,128]{4,3,2,1,0:T(8,128)S(1)}, f32[2,2,2,128,128]{4,3,2,1,0:T(8,128)S(1)}, u32[]{:S(2)}, u32[]{:S(2)}) collective-permute-start(f32[2,2,2,128,128]{4,3,2,1,0:T(8,128)S(1)} %get-tuple-element.39.green), channel_id=1, source_target_pairs={{0,2},{1,3},{2,0},{3,1},{4,6},{5,7},{6,4},{7,5},{8,16},{9,17},{10,... | collective-permute-start | bytes 1572872 | tf_op jit(solution)/shard_map/ppermute | solution.py:39
  6.8 11.2 %collective-permute-start.3 = (f32[2,2,2,128,128]{4,3,2,1,0:T(8,128)S(1)}, f32[2,2,2,128,128]{4,3,2,1,0:T(8,128)S(1)}, u32[]{:S(2)}, u32[]{:S(2)}) collective-permute-start(f32[2,2,2,128,128]{4,3,2,1,0:T(8,128)S(1)} %get-tuple-element.39.green), channel_id=1, source_target_pairs={{0,8},{16,24},{8,0},{24,16},{1,9},{17,25},{9,1},{25,17},{2,10},{18... | collective-permute-start | bytes 1572872 | tf_op jit(solution)/shard_map/ppermute | solution.py:26
  6.8 11.1 %collective-permute-start.2 = (f32[2,2,128,128]{3,2,1,0:T(8,128)S(1)}, f32[2,2,128,128]{3,2,1,0:T(8,128)S(1)}, u32[]{:S(2)}, u32[]{:S(2)}) collective-permute-start(f32[2,2,128,128]{3,2,1,0:T(8,128)S(1)} %get-tuple-element.42.green1), channel_id=1, source_target_pairs={{0,1},{2,3},{4,5},{6,7},{1,0},{3,2},{5,4},{7,6},{8,9},{10,11},{12,... | collective-permute-start | bytes 786440 | tf_op jit(solution)/shard_map/ppermute | solution.py:26
  12.3 10.4 %collective-permute-start.1 = (f32[2,2,128,128]{3,2,1,0:T(8,128)S(1)}, f32[2,2,128,128]{3,2,1,0:T(8,128)S(1)}, u32[]{:S(2)}, u32[]{:S(2)}) collective-permute-start(f32[2,2,128,128]{3,2,1,0:T(8,128)S(1)} %collective-permute-done.ahead), channel_id=1, source_target_pairs={{0,2},{2,4},{4,6},{6,7},{1,0},{3,1},{5,3},{7,5},{8,10},{10,12},{12... | collective-permute-start | bytes 786440 | tf_op jit(solution)/shard_map/ppermute | solution.py:50
  15.8 9.7 %collective-permute-start.5 = (f32[2,2,128,128]{3,2,1,0:T(8,128)S(1)}, f32[2,2,128,128]{3,2,1,0:T(8,128)S(1)}, u32[]{:S(2)}, u32[]{:S(2)}) collective-permute-start(f32[2,2,128,128]{3,2,1,0:T(8,128)S(1)} %get-tuple-element.42.green1), channel_id=1, source_target_pairs={{1,2},{3,4},{5,6},{2,1},{4,3},{6,5},{9,10},{11,12},{13,14},{10,9},... | collective-permute-start | bytes 786440 | tf_op jit(solution)/shard_map/ppermute | solution.py:26
  23.6 6.4 %collective-permute-start.6 = (f32[2,2,128,128]{3,2,1,0:T(8,128)S(1)}, f32[2,2,128,128]{3,2,1,0:T(8,128)S(1)}, u32[]{:S(2)}, u32[]{:S(2)}) collective-permute-start(f32[2,2,128,128]{3,2,1,0:T(8,128)S(1)} %get-tuple-element.46), channel_id=1, source_target_pairs={{0,2},{1,3},{2,0},{3,1},{4,6},{5,7},{6,4},{7,5},{8,16},{9,17},{10,... | collective-permute-start | bytes 786440 | tf_op jit(solution)/shard_map/ppermute | solution.py:39
  23.7 6.3 %collective-permute-start.7 = (f32[2,2,128,128]{3,2,1,0:T(8,128)S(1)}, f32[2,2,128,128]{3,2,1,0:T(8,128)S(1)}, u32[]{:S(2)}, u32[]{:S(2)}) collective-permute-start(f32[2,2,128,128]{3,2,1,0:T(8,128)S(1)} %get-tuple-element.47), channel_id=1, source_target_pairs={{0,8},{16,24},{8,0},{24,16},{1,9},{17,25},{9,1},{25,17},{2,10},{18... | collective-permute-start | bytes 786440 | tf_op jit(solution)/shard_map/ppermute | solution.py:26
  26.3 6.4 %collective-permute-start.8 = (f32[2,2,128,128]{3,2,1,0:T(8,128)S(1)}, f32[2,2,128,128]{3,2,1,0:T(8,128)S(1)}, u32[]{:S(2)}, u32[]{:S(2)}) collective-permute-start(f32[2,2,128,128]{3,2,1,0:T(8,128)S(1)} %get-tuple-element.51), channel_id=1, source_target_pairs={{0,1},{1,0},{2,3},{3,2},{4,5},{5,4},{6,7},{7,6},{8,16},{9,17},{10,... | collective-permute-start | bytes 786440 | tf_op jit(solution)/shard_map/ppermute | solution.py:39
  27.9 4.9 %collective-permute-start.9 = (f32[2,2,128,128]{3,2,1,0:T(8,128)S(1)}, f32[2,2,128,128]{3,2,1,0:T(8,128)S(1)}, u32[]{:S(2)}, u32[]{:S(2)}) collective-permute-start(f32[2,2,128,128]{3,2,1,0:T(8,128)S(1)} %get-tuple-element.52), channel_id=1, source_target_pairs={{0,8},{16,24},{8,0},{24,16},{1,9},{17,25},{9,1},{25,17},{2,10},{18... | collective-permute-start | bytes 786440 | tf_op jit(solution)/shard_map/ppermute | solution.py:26
  30.0 2.8 %collective-permute-start.12 = (f32[2,128]{1,0:T(2,128)S(1)}, f32[2,128]{1,0:T(2,128)S(1)}, u32[]{:S(2)}, u32[]{:S(2)}) collective-permute-start(f32[2,128]{1,0:T(2,128)S(1)} %get-tuple-element.53.rest_0_), channel_id=1, source_target_pairs={{0,24},{8,0},{16,8},{24,16},{1,25},{9,1},{17,9},{25,17},{2,26},{10... | collective-permute-start | bytes 3080 | tf_op jit(solution)/shard_map/ppermute | solution.py:224
  30.0 3.6 %collective-permute-start.11 = (f32[2,128]{1,0:T(2,128)S(1)}, f32[2,128]{1,0:T(2,128)S(1)}, u32[]{:S(2)}, u32[]{:S(2)}) collective-permute-start(f32[2,128]{1,0:T(2,128)S(1)} %get-tuple-element.53.rest_0_), channel_id=1, source_target_pairs={{0,16},{8,24},{16,0},{24,8},{1,17},{9,25},{17,1},{25,9},{2,18},{10... | collective-permute-start | bytes 3080 | tf_op jit(solution)/shard_map/ppermute | solution.py:224
  31.5 3.0 %collective-permute-start.10 = (f32[2,128]{1,0:T(2,128)S(1)}, f32[2,128]{1,0:T(2,128)S(1)}, u32[]{:S(2)}, u32[]{:S(2)}) collective-permute-start(f32[2,128]{1,0:T(2,128)S(1)} %get-tuple-element.53.rest_0_), channel_id=1, source_target_pairs={{0,8},{8,16},{16,24},{24,0},{1,9},{9,17},{17,25},{25,1},{2,10},{10... | collective-permute-start | bytes 3080 | tf_op jit(solution)/shard_map/ppermute | solution.py:224

commit v2 on v1

--- a/solution.py
+++ b/solution.py
@@ -11,6 +11,7 @@
 REACH = max(SHIFTS)
 OWN, PAIR, FAR = 0, 1, 2
 FEW = 4
+BATCH = 6
 VMEM = pl.BlockSpec(memory_space=pltpu.VMEM)
 SMEM = pl.BlockSpec(memory_space=pltpu.SMEM)
 ANY = pl.BlockSpec(memory_space=pl.ANY)
@@ -39,8 +40,17 @@
     return lax.ppermute(x, ("energy", "atom"), perm)
 
 
-def cross_swap(x, step):
-    return exchange(x, lambda e, a: (e + 1 if e % 2 else e - 1, a), lambda e, a: (e, a ^ step))
+def step_aside(a):
+    return a ^ 2
+
+
+def ends_apart(a):
+    atoms = lax.axis_size("atom")
+    return ((a - 2) ^ 2) + 2 if atoms % 4 == 0 and 2 <= a < atoms - 2 else a ^ 1
+
+
+def cross_swap(x, other):
+    return exchange(x, lambda e, a: (e + 1 if e % 2 else e - 1, a), lambda e, a: (e, other(a)))
 
 
 def forward(x, axis):
@@ -144,7 +154,7 @@
 def pair_kernel(neighbours, phonon, coupling, ahead, before, total, blocks, picked):
     total[...] = before[...]
     put_blocks(blocks, 0, ahead)
-    add_pairs(PAIR, neighbours, phonon, coupling, blocks, (total,), picked, 4)
+    add_pairs(PAIR, neighbours, phonon, coupling, blocks, (total,), picked, BATCH)
 
 
 def turn_kernel(
@@ -202,7 +212,7 @@
 def add_far(neighbours, phonon, coupling, across, before, total, blocks, picked):
     total[...] = before[...]
     put_blocks(blocks, 0, across)
-    add_pairs(FAR, neighbours, phonon, coupling, blocks, (total,), picked, 4)
+    add_pairs(FAR, neighbours, phonon, coupling, blocks, (total,), picked, BATCH)
 
 
 def last_kernel(
@@ -267,7 +277,7 @@
     )(*(pltpu.with_memory_space_constraint(x, pltpu.HBM) for x in sources))
     ahead1 = swap(green1, "atom", 0)
     ahead0 = swap(green0, "atom", 0)
-    by_core, by_cross = swap(green, "energy", 0), cross_swap(green, 2)
+    by_core, by_cross = swap(green, "energy", 0), cross_swap(green, step_aside)
     total0, total1 = call(own_kernel, [spread] * 2, (green0, green1), parts=2)
     ahead0, total0, total1 = lax.optimization_barrier((ahead0, total0, total1))
     across0 = forward(ahead0, "atom")
@@ -282,13 +292,13 @@
     total0, core0, cross0, partial = call(
         far_kernel, [spread, edge, edge, (a_local, orb, orb)], (across0, total0, turned)
     )
-    core0, cross0 = swap(core0, "energy", 0), cross_swap(cross0, 2)
+    core0, cross0 = swap(core0, "energy", 0), cross_swap(cross0, ends_apart)
     total1, core1, cross1, rate = call(
         functools.partial(last_kernel, 1.0 / (4.0 * points)),
         [spread, edge, edge, (a_local, orb)],
         (across1, total1, turned, partial),
     )
-    core1, cross1 = swap(core1, "energy", 0), cross_swap(cross1, 1)
+    core1, cross1 = swap(core1, "energy", 0), swap(cross1, "energy", 1)
     cross0, core0, rate = lax.optimization_barrier((cross0, core0, rate))
     rates = addends(rate, "energy")
     return pl.pallas_call(

time: 35.5 us -> 36.2 us (1.020)
  the two profiles are of different devices: /device:TPU:0 before, /device:TPU:16 now
where the time goes in v2:
time: 36.2 us; the launch traced here: 35.8 us
  starting transfers between devices  15.9 us (44%)
  Pallas kernels  11.4 us (31%)
  waiting for transfers between devices  7.78 us (21%)
  between operations  0.74 us (2%)
    ppermute x7, starting transfers between devices, swap(): lax.ppermute(x, axis, [(i, i + 1) for i in low] + [(i + 1, i) for i in low])  10.4 us
    pallas_call x5, Pallas kernels, call(): pl.pallas_call(kernel, out_shape=[jax.ShapeDtypeStruct(shape, jnp.float32...  9 us
    ppermute x7, waiting for transfers between devices, swap(): lax.ppermute(x, axis, [(i, i + 1) for i in low] + [(i + 1, i) for i in low])  4.8 us
    ppermute x3, waiting for transfers between devices, addends(): return [x] + [lax.ppermute(x, axis, turn) for turn in turns]  2.97 us
    ppermute x2, starting transfers between devices, exchange(): return lax.ppermute(x, ('energy', 'atom'), perm)  2.15 us
    ppermute x3, starting transfers between devices, addends(): return [x] + [lax.ppermute(x, axis, turn) for turn in turns]  1.71 us
    ppermute x1, starting transfers between devices, forward(): return lax.ppermute(x, axis, [(i, j) for i, j in ups + downs if i != j])  1.58 us
    pallas_call x1, Pallas kernels, per_device(): pl.pallas_call(fetch_kernel, out_shape=[jax.ShapeDtypeStruct(green.shape[...  1.51 us
  transfers between devices with their start and end apart: 13, of which 4 were waited for; matrix products, arithmetic and copies ran while one was open for 0% of the time, Pallas kernels for 25%

profile of v2, /device:TPU:16, one launch (start us, length us, event | category | flops | bytes accessed | tf_op | source)
XLA Modules:
  0.0 35.8 jit_solution(15607450982356988116)
XLA Ops:
  0.6 1.5 %shard_map.59 = (f32[2,2,128,128]{3,2,1,0:T(8,128)S(1)}, f32[2,2,128,128]{3,2,1,0:T(8,128)S(1)}, f32[2,2,2,128,128]{4,3,2,1,0:T(8,128)S(1)}, f32[2,6,128,128]{3,...) custom-call(f32[2,2,2,128,128]{4,3,2,1,0:T(8,128)} %green.1, f32[2,6,128,128]{3,2,1,0:T(8,128)} %coupling.1, ...), custom_call_target="tpu_custom_call" | custom-call | tf_op jit(solution)/shard_map/pallas_call | solution.py:269
  2.2 1.6 %collective-permute-start = (f32[2,2,128,128]{3,2,1,0:T(8,128)S(1)}, f32[2,2,128,128]{3,2,1,0:T(8,128)S(1)}, u32[]{:S(2)}, u32[]{:S(2)}) collective-permute-start(f32[2,2,128,128]{3,2,1,0:T(8,128)S(1)} %get-tuple-element.31.green0), channel_id=1, source_target_pairs={{0,1},{2,3},{4,5},{6,7},{1,0},{3,2},{5,4},{7,6},{8,9},{10,11},{12,... | collective-permute-start | bytes 786440 | tf_op jit(solution)/shard_map/ppermute | solution.py:27
  3.7 1.6 %collective-permute-start.4 = (f32[2,2,2,128,128]{4,3,2,1,0:T(8,128)S(1)}, f32[2,2,2,128,128]{4,3,2,1,0:T(8,128)S(1)}, u32[]{:S(2)}, u32[]{:S(2)}) collective-permute-start(f32[2,2,2,128,128]{4,3,2,1,0:T(8,128)S(1)} %get-tuple-element.39.green), channel_id=1, source_target_pairs={{0,2},{1,3},{2,0},{3,1},{4,6},{5,7},{6,4},{7,5},{8,16},{9,17},{10,... | collective-permute-start | bytes 1572872 | tf_op jit(solution)/shard_map/ppermute | solution.py:40
  5.3 0.0 collective-permute-start.3
  5.3 0.5 %collective-permute-start.2 = (f32[2,2,128,128]{3,2,1,0:T(8,128)S(1)}, f32[2,2,128,128]{3,2,1,0:T(8,128)S(1)}, u32[]{:S(2)}, u32[]{:S(2)}) collective-permute-start(f32[2,2,128,128]{3,2,1,0:T(8,128)S(1)} %get-tuple-element.42.green1), channel_id=1, source_target_pairs={{0,1},{2,3},{4,5},{6,7},{1,0},{3,2},{5,4},{7,6},{8,9},{10,11},{12,... | collective-permute-start | bytes 786440 | tf_op jit(solution)/shard_map/ppermute | solution.py:27
  5.9 2.6 %shard_map.60 = (f32[6,2,128,128]{3,2,1,0:T(8,128)S(1)}, f32[6,2,128,128]{3,2,1,0:T(8,128)S(1)}) custom-call(s32[2,6]{1,0:T(2,128)S(1)} %get-tuple-element.28.neighbours, f32[2,4,6]{2,1,0:T(4,128)S(1)} %get-tuple-element.29.phonon, f32[2,6,128,128]{3,2,1,0:T(8,128)S(1)} %get-tuple-element.30.coupling, f32[2,2,128,128]{3,2,1,0:T(8,128)S(1)} %get-tuple-element.31.green0, ...), custom_call_target="tpu_custom_call" | custom-call | flops 1000000 | bytes 10000 | tf_op jit(solution)/shard_map/pallas_call | solution.py:255
  8.5 2.9 %collective-permute-done.ahead = f32[2,2,128,128]{3,2,1,0:T(8,128)S(1)} collective-permute-done((f32[2,2,128,128]{3,2,1,0:T(8,128)S(1)}, f32[2,2,128,128]{3,2,1,0:T(8,128)S(1)}, u32[]{:S(2)}, u32[]{:S(2)}) %collective-permute-start) | collective-permute-done | bytes 262176 | tf_op jit(solution)/shard_map/ppermute | solution.py:27
  11.4 1.6 %collective-permute-start.1 = (f32[2,2,128,128]{3,2,1,0:T(8,128)S(1)}, f32[2,2,128,128]{3,2,1,0:T(8,128)S(1)}, u32[]{:S(2)}, u32[]{:S(2)}) collective-permute-start(f32[2,2,128,128]{3,2,1,0:T(8,128)S(1)} %collective-permute-done.ahead), channel_id=1, source_target_pairs={{0,2},{2,4},{4,6},{6,7},{1,0},{3,1},{5,3},{7,5},{8,10},{10,12},{12... | collective-permute-start | bytes 786440 | tf_op jit(solution)/shard_map/ppermute | solution.py:60
  13.0 1.4 %shard_map.61.before = f32[6,2,128,128]{3,2,1,0:T(8,128)S(1)} custom-call(s32[2,6]{1,0:T(2,128)S(1)} %get-tuple-element.28.neighbours, f32[2,4,6]{2,1,0:T(4,128)S(1)} %get-tuple-element.29.phonon, f32[2,6,128,128]{3,2,1,0:T(8,128)S(1)} %get-tuple-element.30.coupling, f32[2,2,128,128]{3,2,1,0:T(8,128)S(1)} %collective-permute-done.ahead, ...), custom_call_target="tpu_custom_call" | custom-call | flops 1000000 | bytes 10000 | tf_op jit(solution)/shard_map/pallas_call | solution.py:255
  14.4 2.2 %collective-permute-start.5 = (f32[2,2,128,128]{3,2,1,0:T(8,128)S(1)}, f32[2,2,128,128]{3,2,1,0:T(8,128)S(1)}, u32[]{:S(2)}, u32[]{:S(2)}) collective-permute-start(f32[2,2,128,128]{3,2,1,0:T(8,128)S(1)} %get-tuple-element.42.green1), channel_id=1, source_target_pairs={{1,2},{3,4},{5,6},{2,1},{4,3},{6,5},{9,10},{11,12},{13,14},{10,9},... | collective-permute-start | bytes 786440 | tf_op jit(solution)/shard_map/ppermute | solution.py:27
  16.6 0.0 collective-permute-done.2.ahead
  16.6 0.0 collective-permute-done.4.by_cross
  16.6 0.0 collective-permute-done.3.by_core
  16.6 1.8 %shard_map.62 = (f32[6,2,128,128]{3,2,1,0:T(8,128)S(1)}, f32[2,6,2,128,128]{4,3,2,1,0:T(8,128)S(1)}) custom-call(s32[2,6]{1,0:T(2,128)S(1)} %get-tuple-element.28.neighbours, f32[2,4,6]{2,1,0:T(4,128)S(1)} %get-tuple-element.29.phonon, f32[2,6,128,128]{3,2,1,0:T(8,128)S(1)} %get-tuple-element.30.coupling, ...), custom_call_target="tpu_custom_call" | custom-call | flops 1000000 | bytes 10000 | tf_op jit(solution)/shard_map/pallas_call | solution.py:255
  18.5 0.0 collective-permute-done.1.across
  18.5 1.6 %shard_map.63 = (f32[6,2,128,128]{3,2,1,0:T(8,128)S(1)}, f32[2,2,128,128]{3,2,1,0:T(8,128)S(1)}, f32[2,2,128,128]{3,2,1,0:T(8,128)S(1)}, f32[2,128,128]{2,1,0:T(8,128)S(1)}) custom-call(s32[2,6]{1,0:T(2,128)S(1)} %get-tuple-element.28.neighbours, f32[2,4,6]{2,1,0:T(4,128)S(1)} %get-tuple-element.29.phonon, ...), custom_call_target="tpu_custom_call" | custom-call | flops 1000000 | bytes 10000 | tf_op jit(solution)/shard_map/pallas_call | solution.py:255
  20.0 0.6 %collective-permute-start.6 = (f32[2,2,128,128]{3,2,1,0:T(8,128)S(1)}, f32[2,2,128,128]{3,2,1,0:T(8,128)S(1)}, u32[]{:S(2)}, u32[]{:S(2)}) collective-permute-start(f32[2,2,128,128]{3,2,1,0:T(8,128)S(1)} %get-tuple-element.46), channel_id=1, source_target_pairs={{0,1},{1,0},{2,4},{3,5},{4,2},{5,3},{6,7},{7,6},{8,16},{9,17},{10,... | collective-permute-start | bytes 786440 | tf_op jit(solution)/shard_map/ppermute | solution.py:40
  20.6 1.1 %collective-permute-start.7 = (f32[2,2,128,128]{3,2,1,0:T(8,128)S(1)}, f32[2,2,128,128]{3,2,1,0:T(8,128)S(1)}, u32[]{:S(2)}, u32[]{:S(2)}) collective-permute-start(f32[2,2,128,128]{3,2,1,0:T(8,128)S(1)} %get-tuple-element.47), channel_id=1, source_target_pairs={{0,8},{16,24},{8,0},{24,16},{1,9},{17,25},{9,1},{25,17},{2,10},{18... | collective-permute-start | bytes 786440 | tf_op jit(solution)/shard_map/ppermute | solution.py:27
  21.7 1.9 %collective-permute-done.5.across = f32[2,2,128,128]{3,2,1,0:T(8,128)S(1)} collective-permute-done((f32[2,2,128,128]{3,2,1,0:T(8,128)S(1)}, f32[2,2,128,128]{3,2,1,0:T(8,128)S(1)}, u32[]{:S(2)}, u32[]{:S(2)}) %collective-permute-start.5) | collective-permute-done | bytes 262176 | tf_op jit(solution)/shard_map/ppermute | solution.py:27
  23.6 1.6 %shard_map.64 = (f32[6,2,128,128]{3,2,1,0:T(8,128)S(1)}, f32[2,2,128,128]{3,2,1,0:T(8,128)S(1)}, f32[2,2,128,128]{3,2,1,0:T(8,128)S(1)}, f32[2,128]{1,0:T(2,128)S(1)}) custom-call(s32[2,6]{1,0:T(2,128)S(1)} %get-tuple-element.28.neighbours, f32[2,4,6]{2,1,0:T(4,128)S(1)} %get-tuple-element.29.phonon, f32[2,6,128,128]{3,2,1,0:T(8,128)S(1)} %get-tuple-element.30.coupling, ...), custom_call_target="tpu_custom_call" | custom-call | flops 1000000 | bytes 10000 | tf_op jit(solution)/shard_map/pallas_call | solution.py:255
  25.2 0.7 %collective-permute-start.8 = (f32[2,2,128,128]{3,2,1,0:T(8,128)S(1)}, f32[2,2,128,128]{3,2,1,0:T(8,128)S(1)}, u32[]{:S(2)}, u32[]{:S(2)}) collective-permute-start(f32[2,2,128,128]{3,2,1,0:T(8,128)S(1)} %get-tuple-element.51), channel_id=1, source_target_pairs={{8,16},{16,8},{9,17},{17,9},{10,18},{18,10},{11,19},{19,11},{12,20... | collective-permute-start | bytes 786440 | tf_op jit(solution)/shard_map/ppermute | solution.py:27
  25.8 4.3 %collective-permute-start.9 = (f32[2,2,128,128]{3,2,1,0:T(8,128)S(1)}, f32[2,2,128,128]{3,2,1,0:T(8,128)S(1)}, u32[]{:S(2)}, u32[]{:S(2)}) collective-permute-start(f32[2,2,128,128]{3,2,1,0:T(8,128)S(1)} %get-tuple-element.52), channel_id=1, source_target_pairs={{0,8},{16,24},{8,0},{24,16},{1,9},{17,25},{9,1},{25,17},{2,10},{18... | collective-permute-start | bytes 786440 | tf_op jit(solution)/shard_map/ppermute | solution.py:27
  30.2 0.0 collective-permute-done.6.cross0
  30.2 0.0 collective-permute-done.7.core0
  30.2 0.0 collective-permute-start.12
  30.2 1.7 %collective-permute-start.11 = (f32[2,128]{1,0:T(2,128)S(1)}, f32[2,128]{1,0:T(2,128)S(1)}, u32[]{:S(2)}, u32[]{:S(2)}) collective-permute-start(f32[2,128]{1,0:T(2,128)S(1)} %get-tuple-element.53.rest_0_), channel_id=1, source_target_pairs={{0,16},{8,24},{16,0},{24,8},{1,17},{9,25},{17,1},{25,9},{2,18},{10... | collective-permute-start | bytes 3080 | tf_op jit(solution)/shard_map/ppermute | solution.py:234
  31.9 0.0 collective-permute-start.10
  31.9 0.0 collective-permute-done.8.cross1
  31.9 0.0 collective-permute-done.9.core1
  31.9 0.0 collective-permute-done.12.rest_3_
  31.9 2.4 %collective-permute-done.11.rest_2_ = f32[2,128]{1,0:T(2,128)S(1)} collective-permute-done((f32[2,128]{1,0:T(2,128)S(1)}, f32[2,128]{1,0:T(2,128)S(1)}, u32[]{:S(2)}, u32[]{:S(2)}) %collective-permute-start.11) | collective-permute-done | bytes 1056 | tf_op jit(solution)/shard_map/ppermute | solution.py:234
  34.4 0.5 %collective-permute-done.10.rest_1_ = f32[2,128]{1,0:T(2,128)S(1)} collective-permute-done((f32[2,128]{1,0:T(2,128)S(1)}, f32[2,128]{1,0:T(2,128)S(1)}, u32[]{:S(2)}, u32[]{:S(2)}) %collective-permute-start.10) | collective-permute-done | bytes 1056 | tf_op jit(solution)/shard_map/ppermute | solution.py:234
  34.9 0.9 %shard_map.65 = (f32[2,2,2,128,128]{4,3,2,1,0:T(8,128)}, f32[2,128]{1,0:T(2,128)}) custom-call(f32[6,2,128,128]{3,2,1,0:T(8,128)S(1)} %get-tuple-element.41.total0, f32[6,2,128,128]{3,2,1,0:T(8,128)S(1)} %get-tuple-element.45.total1, f32[2,2,128,128]{3,2,1,0:T(8,128)S(1)} %collective-permute-done.6.cross0, ...), custom_call_target="tpu_custom_call" | custom-call | flops 1000000 | bytes 2000000 | tf_op jit(solution)/shard_map/pallas_call | solution.py:304
Async XLA Ops:
  2.2 9.3 %collective-permute-start = (f32[2,2,128,128]{3,2,1,0:T(8,128)S(1)}, f32[2,2,128,128]{3,2,1,0:T(8,128)S(1)}, u32[]{:S(2)}, u32[]{:S(2)}) collective-permute-start(f32[2,2,128,128]{3,2,1,0:T(8,128)S(1)} %get-tuple-element.31.green0), channel_id=1, source_target_pairs={{0,1},{2,3},{4,5},{6,7},{1,0},{3,2},{5,4},{7,6},{8,9},{10,11},{12,... | collective-permute-start | bytes 786440 | tf_op jit(solution)/shard_map/ppermute | solution.py:27
  3.7 12.9 %collective-permute-start.4 = (f32[2,2,2,128,128]{4,3,2,1,0:T(8,128)S(1)}, f32[2,2,2,128,128]{4,3,2,1,0:T(8,128)S(1)}, u32[]{:S(2)}, u32[]{:S(2)}) collective-permute-start(f32[2,2,2,128,128]{4,3,2,1,0:T(8,128)S(1)} %get-tuple-element.39.green), channel_id=1, source_target_pairs={{0,2},{1,3},{2,0},{3,1},{4,6},{5,7},{6,4},{7,5},{8,16},{9,17},{10,... | collective-permute-start | bytes 1572872 | tf_op jit(solution)/shard_map/ppermute | solution.py:40
  5.3 11.3 %collective-permute-start.3 = (f32[2,2,2,128,128]{4,3,2,1,0:T(8,128)S(1)}, f32[2,2,2,128,128]{4,3,2,1,0:T(8,128)S(1)}, u32[]{:S(2)}, u32[]{:S(2)}) collective-permute-start(f32[2,2,2,128,128]{4,3,2,1,0:T(8,128)S(1)} %get-tuple-element.39.green), channel_id=1, source_target_pairs={{0,8},{16,24},{8,0},{24,16},{1,9},{17,25},{9,1},{25,17},{2,10},{18... | collective-permute-start | bytes 1572872 | tf_op jit(solution)/shard_map/ppermute | solution.py:27
  5.3 11.3 %collective-permute-start.2 = (f32[2,2,128,128]{3,2,1,0:T(8,128)S(1)}, f32[2,2,128,128]{3,2,1,0:T(8,128)S(1)}, u32[]{:S(2)}, u32[]{:S(2)}) collective-permute-start(f32[2,2,128,128]{3,2,1,0:T(8,128)S(1)} %get-tuple-element.42.green1), channel_id=1, source_target_pairs={{0,1},{2,3},{4,5},{6,7},{1,0},{3,2},{5,4},{7,6},{8,9},{10,11},{12,... | collective-permute-start | bytes 786440 | tf_op jit(solution)/shard_map/ppermute | solution.py:27
  11.4 7.0 %collective-permute-start.1 = (f32[2,2,128,128]{3,2,1,0:T(8,128)S(1)}, f32[2,2,128,128]{3,2,1,0:T(8,128)S(1)}, u32[]{:S(2)}, u32[]{:S(2)}) collective-permute-start(f32[2,2,128,128]{3,2,1,0:T(8,128)S(1)} %collective-permute-done.ahead), channel_id=1, source_target_pairs={{0,2},{2,4},{4,6},{6,7},{1,0},{3,1},{5,3},{7,5},{8,10},{10,12},{12... | collective-permute-start | bytes 786440 | tf_op jit(solution)/shard_map/ppermute | solution.py:60
  14.4 9.2 %collective-permute-start.5 = (f32[2,2,128,128]{3,2,1,0:T(8,128)S(1)}, f32[2,2,128,128]{3,2,1,0:T(8,128)S(1)}, u32[]{:S(2)}, u32[]{:S(2)}) collective-permute-start(f32[2,2,128,128]{3,2,1,0:T(8,128)S(1)} %get-tuple-element.42.green1), channel_id=1, source_target_pairs={{1,2},{3,4},{5,6},{2,1},{4,3},{6,5},{9,10},{11,12},{13,14},{10,9},... | collective-permute-start | bytes 786440 | tf_op jit(solution)/shard_map/ppermute | solution.py:27
  20.0 10.2 %collective-permute-start.6 = (f32[2,2,128,128]{3,2,1,0:T(8,128)S(1)}, f32[2,2,128,128]{3,2,1,0:T(8,128)S(1)}, u32[]{:S(2)}, u32[]{:S(2)}) collective-permute-start(f32[2,2,128,128]{3,2,1,0:T(8,128)S(1)} %get-tuple-element.46), channel_id=1, source_target_pairs={{0,1},{1,0},{2,4},{3,5},{4,2},{5,3},{6,7},{7,6},{8,16},{9,17},{10,... | collective-permute-start | bytes 786440 | tf_op jit(solution)/shard_map/ppermute | solution.py:40
  20.6 9.6 %collective-permute-start.7 = (f32[2,2,128,128]{3,2,1,0:T(8,128)S(1)}, f32[2,2,128,128]{3,2,1,0:T(8,128)S(1)}, u32[]{:S(2)}, u32[]{:S(2)}) collective-permute-start(f32[2,2,128,128]{3,2,1,0:T(8,128)S(1)} %get-tuple-element.47), channel_id=1, source_target_pairs={{0,8},{16,24},{8,0},{24,16},{1,9},{17,25},{9,1},{25,17},{2,10},{18... | collective-permute-start | bytes 786440 | tf_op jit(solution)/shard_map/ppermute | solution.py:27
  25.2 6.8 %collective-permute-start.8 = (f32[2,2,128,128]{3,2,1,0:T(8,128)S(1)}, f32[2,2,128,128]{3,2,1,0:T(8,128)S(1)}, u32[]{:S(2)}, u32[]{:S(2)}) collective-permute-start(f32[2,2,128,128]{3,2,1,0:T(8,128)S(1)} %get-tuple-element.51), channel_id=1, source_target_pairs={{8,16},{16,8},{9,17},{17,9},{10,18},{18,10},{11,19},{19,11},{12,20... | collective-permute-start | bytes 786440 | tf_op jit(solution)/shard_map/ppermute | solution.py:27
  25.8 6.1 %collective-permute-start.9 = (f32[2,2,128,128]{3,2,1,0:T(8,128)S(1)}, f32[2,2,128,128]{3,2,1,0:T(8,128)S(1)}, u32[]{:S(2)}, u32[]{:S(2)}) collective-permute-start(f32[2,2,128,128]{3,2,1,0:T(8,128)S(1)} %get-tuple-element.52), channel_id=1, source_target_pairs={{0,8},{16,24},{8,0},{24,16},{1,9},{17,25},{9,1},{25,17},{2,10},{18... | collective-permute-start | bytes 786440 | tf_op jit(solution)/shard_map/ppermute | solution.py:27
  30.2 1.7 %collective-permute-start.12 = (f32[2,128]{1,0:T(2,128)S(1)}, f32[2,128]{1,0:T(2,128)S(1)}, u32[]{:S(2)}, u32[]{:S(2)}) collective-permute-start(f32[2,128]{1,0:T(2,128)S(1)} %get-tuple-element.53.rest_0_), channel_id=1, source_target_pairs={{0,24},{8,0},{16,8},{24,16},{1,25},{9,1},{17,9},{25,17},{2,26},{10... | collective-permute-start | bytes 3080 | tf_op jit(solution)/shard_map/ppermute | solution.py:234
  30.2 4.2 %collective-permute-start.11 = (f32[2,128]{1,0:T(2,128)S(1)}, f32[2,128]{1,0:T(2,128)S(1)}, u32[]{:S(2)}, u32[]{:S(2)}) collective-permute-start(f32[2,128]{1,0:T(2,128)S(1)} %get-tuple-element.53.rest_0_), channel_id=1, source_target_pairs={{0,16},{8,24},{16,0},{24,8},{1,17},{9,25},{17,1},{25,9},{2,18},{10... | collective-permute-start | bytes 3080 | tf_op jit(solution)/shard_map/ppermute | solution.py:234
  31.9 3.0 %collective-permute-start.10 = (f32[2,128]{1,0:T(2,128)S(1)}, f32[2,128]{1,0:T(2,128)S(1)}, u32[]{:S(2)}, u32[]{:S(2)}) collective-permute-start(f32[2,128]{1,0:T(2,128)S(1)} %get-tuple-element.53.rest_0_), channel_id=1, source_target_pairs={{0,8},{8,16},{16,24},{24,0},{1,9},{9,17},{17,25},{25,1},{2,10},{10... | collective-permute-start | bytes 3080 | tf_op jit(solution)/shard_map/ppermute | solution.py:234

commit v3 on v1

--- a/solution.py
+++ b/solution.py
@@ -11,6 +11,7 @@
 REACH = max(SHIFTS)
 OWN, PAIR, FAR = 0, 1, 2
 FEW = 4
+BATCH = 6
 VMEM = pl.BlockSpec(memory_space=pltpu.VMEM)
 SMEM = pl.BlockSpec(memory_space=pltpu.SMEM)
 ANY = pl.BlockSpec(memory_space=pl.ANY)
@@ -121,9 +122,7 @@
     lax.fori_loop(0, (found + size - 1) // size, batch, None)
 
 
-def fetch_kernel(green, coupling, phonon, neighbours, *rest):
-    *results, sems = rest
-    sources = [green.at[0], green.at[1], green, coupling, phonon, neighbours]
+def copy_all(sources, results, sems):
     copies = [
         pltpu.make_async_copy(source, result, sems.at[i])
         for i, (source, result) in enumerate(zip(sources, results))
@@ -134,6 +133,14 @@
         copy.wait()
 
 
+def part_kernel(green, part, sems):
+    copy_all([green.at[0]], [part], sems)
+
+
+def fetch_kernel(green, coupling, phonon, neighbours, *rest):
+    copy_all([green.at[1], green, coupling, phonon, neighbours], rest[:-1], rest[-1])
+
+
 def own_kernel(neighbours, phonon, coupling, green0, green1, total0, total1, blocks, picked):
     for c, (green, total) in enumerate(((green0, total0), (green1, total1))):
         put_blocks(blocks, c, green)
@@ -144,7 +151,7 @@
 def pair_kernel(neighbours, phonon, coupling, ahead, before, total, blocks, picked):
     total[...] = before[...]
     put_blocks(blocks, 0, ahead)
-    add_pairs(PAIR, neighbours, phonon, coupling, blocks, (total,), picked, 4)
+    add_pairs(PAIR, neighbours, phonon, coupling, blocks, (total,), picked, BATCH)
 
 
 def turn_kernel(
@@ -202,7 +209,7 @@
 def add_far(neighbours, phonon, coupling, across, before, total, blocks, picked):
     total[...] = before[...]
     put_blocks(blocks, 0, across)
-    add_pairs(FAR, neighbours, phonon, coupling, blocks, (total,), picked, 4)
+    add_pairs(FAR, neighbours, phonon, coupling, blocks, (total,), picked, BATCH)
 
 
 def last_kernel(
@@ -255,16 +262,21 @@
             cost_estimate=pl.CostEstimate(flops=10**6, bytes_accessed=10**4, transcendentals=0),
         )(neighbours, phonon, coupling, *operands)
 
+    def fetch(kernel, out, sources):
+        return pl.pallas_call(
+            kernel,
+            out_shape=[jax.ShapeDtypeStruct(x.shape, x.dtype) for x in out],
+            in_specs=[ANY] * len(sources),
+            out_specs=[VMEM] * len(out),
+            scratch_shapes=[pltpu.SemaphoreType.DMA((len(out),))],
+            compiler_params=pltpu.CompilerParams(vmem_limit_bytes=24 * 2**20),
+        )(*(pltpu.with_memory_space_constraint(x, pltpu.HBM) for x in sources))
+
     sources = (green, coupling, jnp.swapaxes(phonon, 1, 2), neighbours)
-    green0, green1, green, coupling, phonon, neighbours = pl.pallas_call(
-        fetch_kernel,
-        out_shape=[jax.ShapeDtypeStruct(green.shape[1:], green.dtype)] * 2
-        + [jax.ShapeDtypeStruct(x.shape, x.dtype) for x in sources],
-        in_specs=[ANY] * 4,
-        out_specs=[VMEM] * 6,
-        scratch_shapes=[pltpu.SemaphoreType.DMA((6,))],
-        compiler_params=pltpu.CompilerParams(vmem_limit_bytes=24 * 2**20),
-    )(*(pltpu.with_memory_space_constraint(x, pltpu.HBM) for x in sources))
+    part = jax.ShapeDtypeStruct(green.shape[1:], green.dtype)
+    (green0,) = fetch(part_kernel, [part], [green])
+    green0, *sources = lax.optimization_barrier((green0, *sources))
+    green1, green, coupling, phonon, neighbours = fetch(fetch_kernel, [part, *sources], sources)
     ahead1 = swap(green1, "atom", 0)
     ahead0 = swap(green0, "atom", 0)
     by_core, by_cross = swap(green, "energy", 0), cross_swap(green, 2)

time: 35.5 us -> 35 us (0.986)
  waiting for transfers between devices: 11.4 us -> 8.41 us
  Pallas kernels: 10.5 us -> 12.7 us
    ppermute x3, starting transfers between devices: 3.24 us -> 5.74 us  [exchange(): return lax.ppermute(x, ('energy', 'atom'), perm)]
    ppermute x6, waiting for transfers between devices: 3.25 us -> 1.26 us  [swap(): lax.ppermute(x, axis, [(i, i + 1) for i in low] + [(i + 1, i) for i in low])]
    pallas_call x5, Pallas kernels: 8.04 us -> 9.42 us  [call(): pl.pallas_call(kernel, out_shape=[jax.ShapeDtypeStruct(shape, jnp.float32...]
    ppermute x1, starting transfers between devices: 2.12 us -> 0.76 us  [forward(): return lax.ppermute(x, axis, [(i, j) for i, j in ups + downs if i != j])]
    ppermute x6, starting transfers between devices: 6 us -> 5.04 us  [swap(): lax.ppermute(x, axis, [(i, i + 1) for i in low] + [(i + 1, i) for i in low])]
    ppermute x3, waiting for transfers between devices: 1.67 us -> 0.78 us  [addends(): return [x] + [lax.ppermute(x, axis, turn) for turn in turns]]
    pallas_call x1 -> x2, Pallas kernels: 1.51 us -> 2.38 us  [fetch(): pl.pallas_call(kernel, out_shape=[jax.ShapeDtypeStruct(x.shape, x.dtype)...]
    ppermute x3, waiting for transfers between devices: 3.46 us -> 2.86 us  [exchange(): return lax.ppermute(x, ('energy', 'atom'), perm)]
  transfers between devices with their start and end apart: 13 -> 13, of which waited for: 7 -> 5; matrix products, arithmetic and copies ran while one was open for 0% -> 0% of each run, Pallas kernels for 23% -> 31%
where the time goes in v3:
time: 35 us; the launch traced here: 34.8 us
  starting transfers between devices  13 us (37%)
  Pallas kernels  12.7 us (36%)
  waiting for transfers between devices  8.41 us (24%)
  between operations  0.71 us (2%)
    pallas_call x5, Pallas kernels, call(): pl.pallas_call(kernel, out_shape=[jax.ShapeDtypeStruct(shape, jnp.float32...  9.42 us
    ppermute x3, starting transfers between devices, exchange(): return lax.ppermute(x, ('energy', 'atom'), perm)  5.74 us
    ppermute x6, starting transfers between devices, swap(): lax.ppermute(x, axis, [(i, i + 1) for i in low] + [(i + 1, i) for i in low])  5.04 us
    ppermute x1, waiting for transfers between devices, forward(): return lax.ppermute(x, axis, [(i, j) for i, j in ups + downs if i != j])  3.5 us
    ppermute x3, waiting for transfers between devices, exchange(): return lax.ppermute(x, ('energy', 'atom'), perm)  2.86 us
    pallas_call x2, Pallas kernels, fetch(): pl.pallas_call(kernel, out_shape=[jax.ShapeDtypeStruct(x.shape, x.dtype)...  2.38 us
    ppermute x3, starting transfers between devices, addends(): return [x] + [lax.ppermute(x, axis, turn) for turn in turns]  1.48 us
    ppermute x6, waiting for transfers between devices, swap(): lax.ppermute(x, axis, [(i, i + 1) for i in low] + [(i + 1, i) for i in low])  1.26 us
  transfers between devices with their start and end apart: 13, of which 5 were waited for; matrix products, arithmetic and copies ran while one was open for 0% of the time, Pallas kernels for 31%

profile of v3, /device:TPU:0, one launch (start us, length us, event | category | flops | bytes accessed | tf_op | source)
XLA Modules:
  0.0 34.8 jit_solution(7081615870042135478)
XLA Ops:
  0.6 1.0 %shard_map.59.green0 = f32[2,2,128,128]{3,2,1,0:T(8,128)S(1)} custom-call(f32[2,2,2,128,128]{4,3,2,1,0:T(8,128)} %green.2), custom_call_target="tpu_custom_call" | custom-call | tf_op jit(solution)/shard_map/pallas_call | solution.py:266
  1.6 3.0 %collective-permute-start = (f32[2,2,128,128]{3,2,1,0:T(8,128)S(1)}, f32[2,2,128,128]{3,2,1,0:T(8,128)S(1)}, u32[]{:S(2)}, u32[]{:S(2)}) collective-permute-start(f32[2,2,128,128]{3,2,1,0:T(8,128)S(1)} %shard_map.59.green0), channel_id=1, source_target_pairs={{0,1},{2,3},{4,5},{6,7},{1,0},{3,2},{5,4},{7,6},{8,9},{10,11},{12,... | collective-permute-start | bytes 786440 | tf_op jit(solution)/shard_map/ppermute | solution.py:27
  4.6 1.4 %shard_map.60 = (f32[2,2,128,128]{3,2,1,0:T(8,128)S(1)}, f32[2,2,2,128,128]{4,3,2,1,0:T(8,128)S(1)}, f32[2,6,128,128]{3,2,1,0:T(8,128)S(1)}, f32[2,4,6]{2,1,0:T(4,128)S(1)}, s32[2,6]{1,0:T(2,128)S(1)}) custom-call(f32[2,2,2,128,128]{4,3,2,1,0:T(8,128)} %green.2, f32[2,6,128,128]{3,2,1,0:T(8,128)} %coupling, f32[2,4,6]{2,1,0:T(4,128)} %bitcast.1, s32[2,6]{1,0:T(2,128)} %neighbours), custom_call_target="tpu_custom_call" | custom-call | tf_op jit(solution)/shard_map/pallas_call | solution.py:266
  6.1 1.6 %collective-permute-start.4 = (f32[2,2,2,128,128]{4,3,2,1,0:T(8,128)S(1)}, f32[2,2,2,128,128]{4,3,2,1,0:T(8,128)S(1)}, u32[]{:S(2)}, u32[]{:S(2)}) collective-permute-start(f32[2,2,2,128,128]{4,3,2,1,0:T(8,128)S(1)} %get-tuple-element.47.green), channel_id=1, source_target_pairs={{0,2},{1,3},{2,0},{3,1},{4,6},{5,7},{6,4},{7,5},{8,16},{9,17},{10,... | collective-permute-start | bytes 1572872 | tf_op jit(solution)/shard_map/ppermute | solution.py:40
  7.7 0.0 collective-permute-start.3
  7.7 0.5 %collective-permute-start.2 = (f32[2,2,128,128]{3,2,1,0:T(8,128)S(1)}, f32[2,2,128,128]{3,2,1,0:T(8,128)S(1)}, u32[]{:S(2)}, u32[]{:S(2)}) collective-permute-start(f32[2,2,128,128]{3,2,1,0:T(8,128)S(1)} %get-tuple-element.50.green1), channel_id=1, source_target_pairs={{0,1},{2,3},{4,5},{6,7},{1,0},{3,2},{5,4},{7,6},{8,9},{10,11},{12,... | collective-permute-start | bytes 786440 | tf_op jit(solution)/shard_map/ppermute | solution.py:27
  8.2 4.5 %shard_map.61 = (f32[6,2,128,128]{3,2,1,0:T(8,128)S(1)}, f32[6,2,128,128]{3,2,1,0:T(8,128)S(1)}) custom-call(s32[2,6]{1,0:T(2,128)S(1)} %get-tuple-element.36.neighbours, f32[2,4,6]{2,1,0:T(4,128)S(1)} %get-tuple-element.37.phonon, f32[2,6,128,128]{3,2,1,0:T(8,128)S(1)} %get-tuple-element.38.coupling, f32[2,2,128,128]{3,2,1,0:T(8,128)S(1)} %shard_map.59.green0, ...), custom_call_target="tpu_custom_call" | custom-call | flops 1000000 | bytes 10000 | tf_op jit(solution)/shard_map/pallas_call | solution.py:252
  12.7 0.0 collective-permute-done.ahead
  12.7 0.8 %collective-permute-start.1 = (f32[2,2,128,128]{3,2,1,0:T(8,128)S(1)}, f32[2,2,128,128]{3,2,1,0:T(8,128)S(1)}, u32[]{:S(2)}, u32[]{:S(2)}) collective-permute-start(f32[2,2,128,128]{3,2,1,0:T(8,128)S(1)} %collective-permute-done.ahead), channel_id=1, source_target_pairs={{0,2},{2,4},{4,6},{6,7},{1,0},{3,1},{5,3},{7,5},{8,10},{10,12},{12... | collective-permute-start | bytes 786440 | tf_op jit(solution)/shard_map/ppermute | solution.py:51
  13.5 1.4 %shard_map.62.before = f32[6,2,128,128]{3,2,1,0:T(8,128)S(1)} custom-call(s32[2,6]{1,0:T(2,128)S(1)} %get-tuple-element.36.neighbours, f32[2,4,6]{2,1,0:T(4,128)S(1)} %get-tuple-element.37.phonon, f32[2,6,128,128]{3,2,1,0:T(8,128)S(1)} %get-tuple-element.38.coupling, f32[2,2,128,128]{3,2,1,0:T(8,128)S(1)} %collective-permute-done.ahead, ...), custom_call_target="tpu_custom_call" | custom-call | flops 1000000 | bytes 10000 | tf_op jit(solution)/shard_map/pallas_call | solution.py:252
  14.9 0.7 %collective-permute-start.5 = (f32[2,2,128,128]{3,2,1,0:T(8,128)S(1)}, f32[2,2,128,128]{3,2,1,0:T(8,128)S(1)}, u32[]{:S(2)}, u32[]{:S(2)}) collective-permute-start(f32[2,2,128,128]{3,2,1,0:T(8,128)S(1)} %get-tuple-element.50.green1), channel_id=1, source_target_pairs={{1,2},{3,4},{5,6},{2,1},{4,3},{6,5},{9,10},{11,12},{13,14},{10,9},... | collective-permute-start | bytes 786440 | tf_op jit(solution)/shard_map/ppermute | solution.py:27
  15.6 1.2 %collective-permute-done.2.ahead = f32[2,2,128,128]{3,2,1,0:T(8,128)S(1)} collective-permute-done((f32[2,2,128,128]{3,2,1,0:T(8,128)S(1)}, f32[2,2,128,128]{3,2,1,0:T(8,128)S(1)}, u32[]{:S(2)}, u32[]{:S(2)}) %collective-permute-start.2) | collective-permute-done | bytes 262176 | tf_op jit(solution)/shard_map/ppermute | solution.py:27
  16.8 0.0 collective-permute-done.4.by_cross
  16.8 0.0 collective-permute-done.3.by_core
  16.8 1.8 %shard_map.63 = (f32[6,2,128,128]{3,2,1,0:T(8,128)S(1)}, f32[2,6,2,128,128]{4,3,2,1,0:T(8,128)S(1)}) custom-call(s32[2,6]{1,0:T(2,128)S(1)} %get-tuple-element.36.neighbours, f32[2,4,6]{2,1,0:T(4,128)S(1)} %get-tuple-element.37.phonon, f32[2,6,128,128]{3,2,1,0:T(8,128)S(1)} %get-tuple-element.38.coupling, ...), custom_call_target="tpu_custom_call" | custom-call | flops 1000000 | bytes 10000 | tf_op jit(solution)/shard_map/pallas_call | solution.py:252
  18.7 3.5 %collective-permute-done.1.across = f32[2,2,128,128]{3,2,1,0:T(8,128)S(1)} collective-permute-done((f32[2,2,128,128]{3,2,1,0:T(8,128)S(1)}, f32[2,2,128,128]{3,2,1,0:T(8,128)S(1)}, u32[]{:S(2)}, u32[]{:S(2)}) %collective-permute-start.1) | collective-permute-done | bytes 262176 | tf_op jit(solution)/shard_map/ppermute | solution.py:51
  22.2 0.9 %shard_map.64 = (f32[6,2,128,128]{3,2,1,0:T(8,128)S(1)}, f32[2,2,128,128]{3,2,1,0:T(8,128)S(1)}, f32[2,2,128,128]{3,2,1,0:T(8,128)S(1)}, f32[2,128,128]{2,1,0:T(8,128)S(1)}) custom-call(s32[2,6]{1,0:T(2,128)S(1)} %get-tuple-element.36.neighbours, f32[2,4,6]{2,1,0:T(4,128)S(1)} %get-tuple-element.37.phonon, ...), custom_call_target="tpu_custom_call" | custom-call | flops 1000000 | bytes 10000 | tf_op jit(solution)/shard_map/pallas_call | solution.py:252
  23.0 1.1 %collective-permute-start.6 = (f32[2,2,128,128]{3,2,1,0:T(8,128)S(1)}, f32[2,2,128,128]{3,2,1,0:T(8,128)S(1)}, u32[]{:S(2)}, u32[]{:S(2)}) collective-permute-start(f32[2,2,128,128]{3,2,1,0:T(8,128)S(1)} %get-tuple-element.54), channel_id=1, source_target_pairs={{0,2},{1,3},{2,0},{3,1},{4,6},{5,7},{6,4},{7,5},{8,16},{9,17},{10,... | collective-permute-start | bytes 786440 | tf_op jit(solution)/shard_map/ppermute | solution.py:40
  24.1 0.8 %collective-permute-start.7 = (f32[2,2,128,128]{3,2,1,0:T(8,128)S(1)}, f32[2,2,128,128]{3,2,1,0:T(8,128)S(1)}, u32[]{:S(2)}, u32[]{:S(2)}) collective-permute-start(f32[2,2,128,128]{3,2,1,0:T(8,128)S(1)} %get-tuple-element.55), channel_id=1, source_target_pairs={{0,8},{16,24},{8,0},{24,16},{1,9},{17,25},{9,1},{25,17},{2,10},{18... | collective-permute-start | bytes 786440 | tf_op jit(solution)/shard_map/ppermute | solution.py:27
  24.9 0.0 collective-permute-done.5.across
  24.9 0.9 %shard_map.65 = (f32[6,2,128,128]{3,2,1,0:T(8,128)S(1)}, f32[2,2,128,128]{3,2,1,0:T(8,128)S(1)}, f32[2,2,128,128]{3,2,1,0:T(8,128)S(1)}, f32[2,128]{1,0:T(2,128)S(1)}) custom-call(s32[2,6]{1,0:T(2,128)S(1)} %get-tuple-element.36.neighbours, f32[2,4,6]{2,1,0:T(4,128)S(1)} %get-tuple-element.37.phonon, f32[2,6,128,128]{3,2,1,0:T(8,128)S(1)} %get-tuple-element.38.coupling, ...), custom_call_target="tpu_custom_call" | custom-call | flops 1000000 | bytes 10000 | tf_op jit(solution)/shard_map/pallas_call | solution.py:252
  25.8 3.0 %collective-permute-start.8 = (f32[2,2,128,128]{3,2,1,0:T(8,128)S(1)}, f32[2,2,128,128]{3,2,1,0:T(8,128)S(1)}, u32[]{:S(2)}, u32[]{:S(2)}) collective-permute-start(f32[2,2,128,128]{3,2,1,0:T(8,128)S(1)} %get-tuple-element.59), channel_id=1, source_target_pairs={{0,1},{1,0},{2,3},{3,2},{4,5},{5,4},{6,7},{7,6},{8,16},{9,17},{10,... | collective-permute-start | bytes 786440 | tf_op jit(solution)/shard_map/ppermute | solution.py:40
  28.8 0.0 collective-permute-start.9
  28.8 0.7 %collective-permute-done.6.cross0 = f32[2,2,128,128]{3,2,1,0:T(8,128)S(1)} collective-permute-done((f32[2,2,128,128]{3,2,1,0:T(8,128)S(1)}, f32[2,2,128,128]{3,2,1,0:T(8,128)S(1)}, u32[]{:S(2)}, u32[]{:S(2)}) %collective-permute-start.6) | collective-permute-done | bytes 262176 | tf_op jit(solution)/shard_map/ppermute | solution.py:40
  29.5 0.0 collective-permute-done.7.core0
  29.5 0.0 collective-permute-start.12
  29.5 1.5 %collective-permute-start.11 = (f32[2,128]{1,0:T(2,128)S(1)}, f32[2,128]{1,0:T(2,128)S(1)}, u32[]{:S(2)}, u32[]{:S(2)}) collective-permute-start(f32[2,128]{1,0:T(2,128)S(1)} %get-tuple-element.61.rest_0_), channel_id=1, source_target_pairs={{0,16},{8,24},{16,0},{24,8},{1,17},{9,25},{17,1},{25,9},{2,18},{10... | collective-permute-start | bytes 3080 | tf_op jit(solution)/shard_map/ppermute | solution.py:231
  30.9 0.0 collective-permute-start.10
  30.9 2.2 %collective-permute-done.8.cross1 = f32[2,2,128,128]{3,2,1,0:T(8,128)S(1)} collective-permute-done((f32[2,2,128,128]{3,2,1,0:T(8,128)S(1)}, f32[2,2,128,128]{3,2,1,0:T(8,128)S(1)}, u32[]{:S(2)}, u32[]{:S(2)}) %collective-permute-start.8) | collective-permute-done | bytes 262176 | tf_op jit(solution)/shard_map/ppermute | solution.py:40
  33.1 0.0 collective-permute-done.9.core1
  33.2 0.0 collective-permute-done.12.rest_3_
  33.2 0.0 collective-permute-done.11.rest_2_
  33.2 0.8 %collective-permute-done.10.rest_1_ = f32[2,128]{1,0:T(2,128)S(1)} collective-permute-done((f32[2,128]{1,0:T(2,128)S(1)}, f32[2,128]{1,0:T(2,128)S(1)}, u32[]{:S(2)}, u32[]{:S(2)}) %collective-permute-start.10) | collective-permute-done | bytes 1056 | tf_op jit(solution)/shard_map/ppermute | solution.py:231
  33.9 0.9 %shard_map.66 = (f32[2,2,2,128,128]{4,3,2,1,0:T(8,128)}, f32[2,128]{1,0:T(2,128)}) custom-call(f32[6,2,128,128]{3,2,1,0:T(8,128)S(1)} %get-tuple-element.49.total0, f32[6,2,128,128]{3,2,1,0:T(8,128)S(1)} %get-tuple-element.53.total1, f32[2,2,128,128]{3,2,1,0:T(8,128)S(1)} %collective-permute-done.6.cross0, ...), custom_call_target="tpu_custom_call" | custom-call | flops 1000000 | bytes 2000000 | tf_op jit(solution)/shard_map/pallas_call | solution.py:306
Async XLA Ops:
  1.6 11.1 %collective-permute-start = (f32[2,2,128,128]{3,2,1,0:T(8,128)S(1)}, f32[2,2,128,128]{3,2,1,0:T(8,128)S(1)}, u32[]{:S(2)}, u32[]{:S(2)}) collective-permute-start(f32[2,2,128,128]{3,2,1,0:T(8,128)S(1)} %shard_map.59.green0), channel_id=1, source_target_pairs={{0,1},{2,3},{4,5},{6,7},{1,0},{3,2},{5,4},{7,6},{8,9},{10,11},{12,... | collective-permute-start | bytes 786440 | tf_op jit(solution)/shard_map/ppermute | solution.py:27
  6.1 10.8 %collective-permute-start.4 = (f32[2,2,2,128,128]{4,3,2,1,0:T(8,128)S(1)}, f32[2,2,2,128,128]{4,3,2,1,0:T(8,128)S(1)}, u32[]{:S(2)}, u32[]{:S(2)}) collective-permute-start(f32[2,2,2,128,128]{4,3,2,1,0:T(8,128)S(1)} %get-tuple-element.47.green), channel_id=1, source_target_pairs={{0,2},{1,3},{2,0},{3,1},{4,6},{5,7},{6,4},{7,5},{8,16},{9,17},{10,... | collective-permute-start | bytes 1572872 | tf_op jit(solution)/shard_map/ppermute | solution.py:40
  7.7 9.1 %collective-permute-start.3 = (f32[2,2,2,128,128]{4,3,2,1,0:T(8,128)S(1)}, f32[2,2,2,128,128]{4,3,2,1,0:T(8,128)S(1)}, u32[]{:S(2)}, u32[]{:S(2)}) collective-permute-start(f32[2,2,2,128,128]{4,3,2,1,0:T(8,128)S(1)} %get-tuple-element.47.green), channel_id=1, source_target_pairs={{0,8},{16,24},{8,0},{24,16},{1,9},{17,25},{9,1},{25,17},{2,10},{18... | collective-permute-start | bytes 1572872 | tf_op jit(solution)/shard_map/ppermute | solution.py:27
  7.7 9.1 %collective-permute-start.2 = (f32[2,2,128,128]{3,2,1,0:T(8,128)S(1)}, f32[2,2,128,128]{3,2,1,0:T(8,128)S(1)}, u32[]{:S(2)}, u32[]{:S(2)}) collective-permute-start(f32[2,2,128,128]{3,2,1,0:T(8,128)S(1)} %get-tuple-element.50.green1), channel_id=1, source_target_pairs={{0,1},{2,3},{4,5},{6,7},{1,0},{3,2},{5,4},{7,6},{8,9},{10,11},{12,... | collective-permute-start | bytes 786440 | tf_op jit(solution)/shard_map/ppermute | solution.py:27
  12.7 9.4 %collective-permute-start.1 = (f32[2,2,128,128]{3,2,1,0:T(8,128)S(1)}, f32[2,2,128,128]{3,2,1,0:T(8,128)S(1)}, u32[]{:S(2)}, u32[]{:S(2)}) collective-permute-start(f32[2,2,128,128]{3,2,1,0:T(8,128)S(1)} %collective-permute-done.ahead), channel_id=1, source_target_pairs={{0,2},{2,4},{4,6},{6,7},{1,0},{3,1},{5,3},{7,5},{8,10},{10,12},{12... | collective-permute-start | bytes 786440 | tf_op jit(solution)/shard_map/ppermute | solution.py:51
  14.9 10.0 %collective-permute-start.5 = (f32[2,2,128,128]{3,2,1,0:T(8,128)S(1)}, f32[2,2,128,128]{3,2,1,0:T(8,128)S(1)}, u32[]{:S(2)}, u32[]{:S(2)}) collective-permute-start(f32[2,2,128,128]{3,2,1,0:T(8,128)S(1)} %get-tuple-element.50.green1), channel_id=1, source_target_pairs={{1,2},{3,4},{5,6},{2,1},{4,3},{6,5},{9,10},{11,12},{13,14},{10,9},... | collective-permute-start | bytes 786440 | tf_op jit(solution)/shard_map/ppermute | solution.py:27
  23.0 6.4 %collective-permute-start.6 = (f32[2,2,128,128]{3,2,1,0:T(8,128)S(1)}, f32[2,2,128,128]{3,2,1,0:T(8,128)S(1)}, u32[]{:S(2)}, u32[]{:S(2)}) collective-permute-start(f32[2,2,128,128]{3,2,1,0:T(8,128)S(1)} %get-tuple-element.54), channel_id=1, source_target_pairs={{0,2},{1,3},{2,0},{3,1},{4,6},{5,7},{6,4},{7,5},{8,16},{9,17},{10,... | collective-permute-start | bytes 786440 | tf_op jit(solution)/shard_map/ppermute | solution.py:40
  24.1 5.3 %collective-permute-start.7 = (f32[2,2,128,128]{3,2,1,0:T(8,128)S(1)}, f32[2,2,128,128]{3,2,1,0:T(8,128)S(1)}, u32[]{:S(2)}, u32[]{:S(2)}) collective-permute-start(f32[2,2,128,128]{3,2,1,0:T(8,128)S(1)} %get-tuple-element.55), channel_id=1, source_target_pairs={{0,8},{16,24},{8,0},{24,16},{1,9},{17,25},{9,1},{25,17},{2,10},{18... | collective-permute-start | bytes 786440 | tf_op jit(solution)/shard_map/ppermute | solution.py:27
  25.8 7.4 %collective-permute-start.8 = (f32[2,2,128,128]{3,2,1,0:T(8,128)S(1)}, f32[2,2,128,128]{3,2,1,0:T(8,128)S(1)}, u32[]{:S(2)}, u32[]{:S(2)}) collective-permute-start(f32[2,2,128,128]{3,2,1,0:T(8,128)S(1)} %get-tuple-element.59), channel_id=1, source_target_pairs={{0,1},{1,0},{2,3},{3,2},{4,5},{5,4},{6,7},{7,6},{8,16},{9,17},{10,... | collective-permute-start | bytes 786440 | tf_op jit(solution)/shard_map/ppermute | solution.py:40
  28.8 4.4 %collective-permute-start.9 = (f32[2,2,128,128]{3,2,1,0:T(8,128)S(1)}, f32[2,2,128,128]{3,2,1,0:T(8,128)S(1)}, u32[]{:S(2)}, u32[]{:S(2)}) collective-permute-start(f32[2,2,128,128]{3,2,1,0:T(8,128)S(1)} %get-tuple-element.60), channel_id=1, source_target_pairs={{0,8},{16,24},{8,0},{24,16},{1,9},{17,25},{9,1},{25,17},{2,10},{18... | collective-permute-start | bytes 786440 | tf_op jit(solution)/shard_map/ppermute | solution.py:27
  29.5 3.7 %collective-permute-start.12 = (f32[2,128]{1,0:T(2,128)S(1)}, f32[2,128]{1,0:T(2,128)S(1)}, u32[]{:S(2)}, u32[]{:S(2)}) collective-permute-start(f32[2,128]{1,0:T(2,128)S(1)} %get-tuple-element.61.rest_0_), channel_id=1, source_target_pairs={{0,24},{8,0},{16,8},{24,16},{1,25},{9,1},{17,9},{25,17},{2,26},{10... | collective-permute-start | bytes 3080 | tf_op jit(solution)/shard_map/ppermute | solution.py:231
  29.5 3.7 %collective-permute-start.11 = (f32[2,128]{1,0:T(2,128)S(1)}, f32[2,128]{1,0:T(2,128)S(1)}, u32[]{:S(2)}, u32[]{:S(2)}) collective-permute-start(f32[2,128]{1,0:T(2,128)S(1)} %get-tuple-element.61.rest_0_), channel_id=1, source_target_pairs={{0,16},{8,24},{16,0},{24,8},{1,17},{9,25},{17,1},{25,9},{2,18},{10... | collective-permute-start | bytes 3080 | tf_op jit(solution)/shard_map/ppermute | solution.py:231
  30.9 3.0 %collective-permute-start.10 = (f32[2,128]{1,0:T(2,128)S(1)}, f32[2,128]{1,0:T(2,128)S(1)}, u32[]{:S(2)}, u32[]{:S(2)}) collective-permute-start(f32[2,128]{1,0:T(2,128)S(1)} %get-tuple-element.61.rest_0_), channel_id=1, source_target_pairs={{0,8},{8,16},{16,24},{24,0},{1,9},{9,17},{17,25},{25,1},{2,10},{10... | collective-permute-start | bytes 3080 | tf_op jit(solution)/shard_map/ppermute | solution.py:231

commit v4 on v3

--- a/solution.py
+++ b/solution.py
@@ -300,9 +300,11 @@
         [spread, edge, edge, (a_local, orb)],
         (across1, total1, turned, partial),
     )
-    core1, cross1 = swap(core1, "energy", 0), cross_swap(cross1, 1)
-    cross0, core0, rate = lax.optimization_barrier((cross0, core0, rate))
+    cross1 = cross_swap(cross1, 1)
+    core0, rate = lax.optimization_barrier((core0, rate))
     rates = addends(rate, "energy")
+    cross0, core1, rates = lax.optimization_barrier((cross0, core1, rates))
+    core1 = swap(core1, "energy", 0)
     return pl.pallas_call(
         functools.partial(end_kernel, energies),
         out_shape=[

time: 35 us -> 36 us (1.029)
  the two profiles are of different devices: /device:TPU:0 before, /device:TPU:21 now
where the time goes in v4:
time: 36 us; the launch traced here: 35.4 us
  starting transfers between devices  17.8 us (49%)
  Pallas kernels  12.3 us (34%)
  waiting for transfers between devices  4.61 us (13%)
  between operations  0.75 us (2%)
    ppermute x6, starting transfers between devices, swap(): lax.ppermute(x, axis, [(i, i + 1) for i in low] + [(i + 1, i) for i in low])  10.4 us
    pallas_call x5, Pallas kernels, call(): pl.pallas_call(kernel, out_shape=[jax.ShapeDtypeStruct(shape, jnp.float32...  8.98 us
    ppermute x3, starting transfers between devices, addends(): return [x] + [lax.ppermute(x, axis, turn) for turn in turns]  4.5 us
    ppermute x3, waiting for transfers between devices, exchange(): return lax.ppermute(x, ('energy', 'atom'), perm)  3.86 us
    ppermute x3, starting transfers between devices, exchange(): return lax.ppermute(x, ('energy', 'atom'), perm)  2.86 us
    pallas_call x2, Pallas kernels, fetch(): pl.pallas_call(kernel, out_shape=[jax.ShapeDtypeStruct(x.shape, x.dtype)...  2.38 us
    pallas_call x1, Pallas kernels, per_device(): pl.pallas_call(functools.partial(end_kernel, energies), out_shape=[jax.Sh...  0.91 us
  transfers between devices with their start and end apart: 13, of which 2 were waited for; matrix products, arithmetic and copies ran while one was open for 0% of the time, Pallas kernels for 29%

profile of v4, /device:TPU:21, one launch (start us, length us, event | category | flops | bytes accessed | tf_op | source)
XLA Modules:
  0.0 35.4 jit_solution(2629008642276327417)
XLA Ops:
  0.6 1.0 %shard_map.59.green0 = f32[2,2,128,128]{3,2,1,0:T(8,128)S(1)} custom-call(f32[2,2,2,128,128]{4,3,2,1,0:T(8,128)} %green.2), custom_call_target="tpu_custom_call" | custom-call | tf_op jit(solution)/shard_map/pallas_call | solution.py:266
  1.6 0.3 collective-permute-start
  1.9 1.4 %shard_map.60 = (f32[2,2,128,128]{3,2,1,0:T(8,128)S(1)}, f32[2,2,2,128,128]{4,3,2,1,0:T(8,128)S(1)}, f32[2,6,128,128]{3,2,1,0:T(8,128)S(1)}, f32[2,4,6]{2,1,0:T(4,128)S(1)}, s32[2,6]{1,0:T(2,128)S(1)}) custom-call(f32[2,2,2,128,128]{4,3,2,1,0:T(8,128)} %green.2, f32[2,6,128,128]{3,2,1,0:T(8,128)} %coupling, f32[2,4,6]{2,1,0:T(4,128)} %bitcast.1, s32[2,6]{1,0:T(2,128)} %neighbours), custom_call_target="tpu_custom_call" | custom-call | tf_op jit(solution)/shard_map/pallas_call | solution.py:266
  3.3 2.1 %collective-permute-start.4 = (f32[2,2,2,128,128]{4,3,2,1,0:T(8,128)S(1)}, f32[2,2,2,128,128]{4,3,2,1,0:T(8,128)S(1)}, u32[]{:S(2)}, u32[]{:S(2)}) collective-permute-start(f32[2,2,2,128,128]{4,3,2,1,0:T(8,128)S(1)} %get-tuple-element.52.green), channel_id=1, source_target_pairs={{0,2},{1,3},{2,0},{3,1},{4,6},{5,7},{6,4},{7,5},{8,16},{9,17},{10,... | collective-permute-start | bytes 1572872 | tf_op jit(solution)/shard_map/ppermute | solution.py:40
  5.4 0.5 %collective-permute-start.3 = (f32[2,2,2,128,128]{4,3,2,1,0:T(8,128)S(1)}, f32[2,2,2,128,128]{4,3,2,1,0:T(8,128)S(1)}, u32[]{:S(2)}, u32[]{:S(2)}) collective-permute-start(f32[2,2,2,128,128]{4,3,2,1,0:T(8,128)S(1)} %get-tuple-element.52.green), channel_id=1, source_target_pairs={{0,8},{16,24},{8,0},{24,16},{1,9},{17,25},{9,1},{25,17},{2,10},{18... | collective-permute-start | bytes 1572872 | tf_op jit(solution)/shard_map/ppermute | solution.py:27
  5.9 1.2 %collective-permute-start.2 = (f32[2,2,128,128]{3,2,1,0:T(8,128)S(1)}, f32[2,2,128,128]{3,2,1,0:T(8,128)S(1)}, u32[]{:S(2)}, u32[]{:S(2)}) collective-permute-start(f32[2,2,128,128]{3,2,1,0:T(8,128)S(1)} %get-tuple-element.55.green1), channel_id=1, source_target_pairs={{0,1},{2,3},{4,5},{6,7},{1,0},{3,2},{5,4},{7,6},{8,9},{10,11},{12,... | collective-permute-start | bytes 786440 | tf_op jit(solution)/shard_map/ppermute | solution.py:27
  7.2 2.6 %shard_map.61 = (f32[6,2,128,128]{3,2,1,0:T(8,128)S(1)}, f32[6,2,128,128]{3,2,1,0:T(8,128)S(1)}) custom-call(s32[2,6]{1,0:T(2,128)S(1)} %get-tuple-element.41.neighbours, f32[2,4,6]{2,1,0:T(4,128)S(1)} %get-tuple-element.42.phonon, f32[2,6,128,128]{3,2,1,0:T(8,128)S(1)} %get-tuple-element.43.coupling, f32[2,2,128,128]{3,2,1,0:T(8,128)S(1)} %shard_map.59.green0, ...), custom_call_target="tpu_custom_call" | custom-call | flops 1000000 | bytes 10000 | tf_op jit(solution)/shard_map/pallas_call | solution.py:252
  9.8 0.0 collective-permute-done.ahead
  9.8 0.1 collective-permute-start.1
  9.9 1.4 %shard_map.62.before = f32[6,2,128,128]{3,2,1,0:T(8,128)S(1)} custom-call(s32[2,6]{1,0:T(2,128)S(1)} %get-tuple-element.41.neighbours, f32[2,4,6]{2,1,0:T(4,128)S(1)} %get-tuple-element.42.phonon, f32[2,6,128,128]{3,2,1,0:T(8,128)S(1)} %get-tuple-element.43.coupling, f32[2,2,128,128]{3,2,1,0:T(8,128)S(1)} %collective-permute-done.ahead, ...), custom_call_target="tpu_custom_call" | custom-call | flops 1000000 | bytes 10000 | tf_op jit(solution)/shard_map/pallas_call | solution.py:252
  11.3 5.8 %collective-permute-start.5 = (f32[2,2,128,128]{3,2,1,0:T(8,128)S(1)}, f32[2,2,128,128]{3,2,1,0:T(8,128)S(1)}, u32[]{:S(2)}, u32[]{:S(2)}) collective-permute-start(f32[2,2,128,128]{3,2,1,0:T(8,128)S(1)} %get-tuple-element.55.green1), channel_id=1, source_target_pairs={{1,2},{3,4},{5,6},{2,1},{4,3},{6,5},{9,10},{11,12},{13,14},{10,9},... | collective-permute-start | bytes 786440 | tf_op jit(solution)/shard_map/ppermute | solution.py:27
  17.0 0.0 collective-permute-done.2.ahead
  17.0 0.0 collective-permute-done.4.by_cross
  17.1 0.0 collective-permute-done.3.by_core
  17.1 1.8 %shard_map.63 = (f32[6,2,128,128]{3,2,1,0:T(8,128)S(1)}, f32[2,6,2,128,128]{4,3,2,1,0:T(8,128)S(1)}) custom-call(s32[2,6]{1,0:T(2,128)S(1)} %get-tuple-element.41.neighbours, f32[2,4,6]{2,1,0:T(4,128)S(1)} %get-tuple-element.42.phonon, f32[2,6,128,128]{3,2,1,0:T(8,128)S(1)} %get-tuple-element.43.coupling, ...), custom_call_target="tpu_custom_call" | custom-call | flops 1000000 | bytes 10000 | tf_op jit(solution)/shard_map/pallas_call | solution.py:252
  18.9 0.0 collective-permute-done.1.across
  18.9 1.6 %shard_map.64 = (f32[6,2,128,128]{3,2,1,0:T(8,128)S(1)}, f32[2,2,128,128]{3,2,1,0:T(8,128)S(1)}, f32[2,2,128,128]{3,2,1,0:T(8,128)S(1)}, f32[2,128,128]{2,1,0:T(8,128)S(1)}) custom-call(s32[2,6]{1,0:T(2,128)S(1)} %get-tuple-element.41.neighbours, f32[2,4,6]{2,1,0:T(4,128)S(1)} %get-tuple-element.42.phonon, ...), custom_call_target="tpu_custom_call" | custom-call | flops 1000000 | bytes 10000 | tf_op jit(solution)/shard_map/pallas_call | solution.py:252
  20.5 1.4 %collective-permute-start.7 = (f32[2,2,128,128]{3,2,1,0:T(8,128)S(1)}, f32[2,2,128,128]{3,2,1,0:T(8,128)S(1)}, u32[]{:S(2)}, u32[]{:S(2)}) collective-permute-start(f32[2,2,128,128]{3,2,1,0:T(8,128)S(1)} %get-tuple-element.61), channel_id=1, source_target_pairs={{0,8},{16,24},{8,0},{24,16},{1,9},{17,25},{9,1},{25,17},{2,10},{18... | collective-permute-start | bytes 786440 | tf_op jit(solution)/shard_map/ppermute | solution.py:27
  21.9 0.7 %collective-permute-start.6 = (f32[2,2,128,128]{3,2,1,0:T(8,128)S(1)}, f32[2,2,128,128]{3,2,1,0:T(8,128)S(1)}, u32[]{:S(2)}, u32[]{:S(2)}) collective-permute-start(f32[2,2,128,128]{3,2,1,0:T(8,128)S(1)} %get-tuple-element.59), channel_id=1, source_target_pairs={{0,2},{1,3},{2,0},{3,1},{4,6},{5,7},{6,4},{7,5},{8,16},{9,17},{10,... | collective-permute-start | bytes 786440 | tf_op jit(solution)/shard_map/ppermute | solution.py:40
  22.6 0.0 collective-permute-done.5.across
  22.6 1.6 %shard_map.65 = (f32[6,2,128,128]{3,2,1,0:T(8,128)S(1)}, f32[2,2,128,128]{3,2,1,0:T(8,128)S(1)}, f32[2,2,128,128]{3,2,1,0:T(8,128)S(1)}, f32[2,128]{1,0:T(2,128)S(1)}) custom-call(s32[2,6]{1,0:T(2,128)S(1)} %get-tuple-element.41.neighbours, f32[2,4,6]{2,1,0:T(4,128)S(1)} %get-tuple-element.42.phonon, f32[2,6,128,128]{3,2,1,0:T(8,128)S(1)} %get-tuple-element.43.coupling, ...), custom_call_target="tpu_custom_call" | custom-call | flops 1000000 | bytes 10000 | tf_op jit(solution)/shard_map/pallas_call | solution.py:252
  24.2 0.0 collective-permute-done.7.core0
  24.2 1.7 %collective-permute-start.10 = (f32[2,128]{1,0:T(2,128)S(1)}, f32[2,128]{1,0:T(2,128)S(1)}, u32[]{:S(2)}, u32[]{:S(2)}) collective-permute-start(f32[2,128]{1,0:T(2,128)S(1)} %get-tuple-element.68.rest_0_), channel_id=1, source_target_pairs={{0,24},{8,0},{16,8},{24,16},{1,25},{9,1},{17,9},{25,17},{2,26},{10... | collective-permute-start | bytes 3080 | tf_op jit(solution)/shard_map/ppermute | solution.py:231
  25.9 0.8 %collective-permute-start.9 = (f32[2,128]{1,0:T(2,128)S(1)}, f32[2,128]{1,0:T(2,128)S(1)}, u32[]{:S(2)}, u32[]{:S(2)}) collective-permute-start(f32[2,128]{1,0:T(2,128)S(1)} %get-tuple-element.68.rest_0_), channel_id=1, source_target_pairs={{0,16},{8,24},{16,0},{24,8},{1,17},{9,25},{17,1},{25,9},{2,18},{10... | collective-permute-start | bytes 3080 | tf_op jit(solution)/shard_map/ppermute | solution.py:231
  26.8 1.9 %collective-permute-start.8 = (f32[2,128]{1,0:T(2,128)S(1)}, f32[2,128]{1,0:T(2,128)S(1)}, u32[]{:S(2)}, u32[]{:S(2)}) collective-permute-start(f32[2,128]{1,0:T(2,128)S(1)} %get-tuple-element.68.rest_0_), channel_id=1, source_target_pairs={{0,8},{8,16},{16,24},{24,0},{1,9},{9,17},{17,25},{25,1},{2,10},{10... | collective-permute-start | bytes 3080 | tf_op jit(solution)/shard_map/ppermute | solution.py:231
  28.7 0.0 collective-permute-start.11
  28.8 0.0 collective-permute-done.6.cross0
  28.8 0.0 collective-permute-done.10.rest_3_
  28.8 0.0 collective-permute-done.9.rest_2_
  28.8 0.7 %collective-permute-done.8.rest_1_ = f32[2,128]{1,0:T(2,128)S(1)} collective-permute-done((f32[2,128]{1,0:T(2,128)S(1)}, f32[2,128]{1,0:T(2,128)S(1)}, u32[]{:S(2)}, u32[]{:S(2)}) %collective-permute-start.8) | collective-permute-done | bytes 1056 | tf_op jit(solution)/shard_map/ppermute | solution.py:231
  29.4 1.2 %collective-permute-start.12 = (f32[2,2,128,128]{3,2,1,0:T(8,128)S(1)}, f32[2,2,128,128]{3,2,1,0:T(8,128)S(1)}, u32[]{:S(2)}, u32[]{:S(2)}) collective-permute-start(f32[2,2,128,128]{3,2,1,0:T(8,128)S(1)} %get-tuple-element.67), channel_id=1, source_target_pairs={{0,8},{16,24},{8,0},{24,16},{1,9},{17,25},{9,1},{25,17},{2,10},{18... | collective-permute-start | bytes 786440 | tf_op jit(solution)/shard_map/ppermute | solution.py:27
  30.7 3.9 %collective-permute-done.11.cross1 = f32[2,2,128,128]{3,2,1,0:T(8,128)S(1)} collective-permute-done((f32[2,2,128,128]{3,2,1,0:T(8,128)S(1)}, f32[2,2,128,128]{3,2,1,0:T(8,128)S(1)}, u32[]{:S(2)}, u32[]{:S(2)}) %collective-permute-start.11) | collective-permute-done | bytes 262176 | tf_op jit(solution)/shard_map/ppermute | solution.py:40
  34.5 0.0 collective-permute-done.12.core1
  34.5 0.9 %shard_map.66 = (f32[2,2,2,128,128]{4,3,2,1,0:T(8,128)}, f32[2,128]{1,0:T(2,128)}) custom-call(f32[6,2,128,128]{3,2,1,0:T(8,128)S(1)} %get-tuple-element.54.total0, f32[6,2,128,128]{3,2,1,0:T(8,128)S(1)} %get-tuple-element.58.total1, f32[2,2,128,128]{3,2,1,0:T(8,128)S(1)} %collective-permute-done.6.cross0, ...), custom_call_target="tpu_custom_call" | custom-call | flops 1000000 | bytes 2000000 | tf_op jit(solution)/shard_map/pallas_call | solution.py:308
Async XLA Ops:
  1.6 8.2 %collective-permute-start = (f32[2,2,128,128]{3,2,1,0:T(8,128)S(1)}, f32[2,2,128,128]{3,2,1,0:T(8,128)S(1)}, u32[]{:S(2)}, u32[]{:S(2)}) collective-permute-start(f32[2,2,128,128]{3,2,1,0:T(8,128)S(1)} %shard_map.59.green0), channel_id=1, source_target_pairs={{0,1},{2,3},{4,5},{6,7},{1,0},{3,2},{5,4},{7,6},{8,9},{10,11},{12,... | collective-permute-start | bytes 786440 | tf_op jit(solution)/shard_map/ppermute | solution.py:27
  3.3 13.7 %collective-permute-start.4 = (f32[2,2,2,128,128]{4,3,2,1,0:T(8,128)S(1)}, f32[2,2,2,128,128]{4,3,2,1,0:T(8,128)S(1)}, u32[]{:S(2)}, u32[]{:S(2)}) collective-permute-start(f32[2,2,2,128,128]{4,3,2,1,0:T(8,128)S(1)} %get-tuple-element.52.green), channel_id=1, source_target_pairs={{0,2},{1,3},{2,0},{3,1},{4,6},{5,7},{6,4},{7,5},{8,16},{9,17},{10,... | collective-permute-start | bytes 1572872 | tf_op jit(solution)/shard_map/ppermute | solution.py:40
  5.4 11.6 %collective-permute-start.3 = (f32[2,2,2,128,128]{4,3,2,1,0:T(8,128)S(1)}, f32[2,2,2,128,128]{4,3,2,1,0:T(8,128)S(1)}, u32[]{:S(2)}, u32[]{:S(2)}) collective-permute-start(f32[2,2,2,128,128]{4,3,2,1,0:T(8,128)S(1)} %get-tuple-element.52.green), channel_id=1, source_target_pairs={{0,8},{16,24},{8,0},{24,16},{1,9},{17,25},{9,1},{25,17},{2,10},{18... | collective-permute-start | bytes 1572872 | tf_op jit(solution)/shard_map/ppermute | solution.py:27
  5.9 11.1 %collective-permute-start.2 = (f32[2,2,128,128]{3,2,1,0:T(8,128)S(1)}, f32[2,2,128,128]{3,2,1,0:T(8,128)S(1)}, u32[]{:S(2)}, u32[]{:S(2)}) collective-permute-start(f32[2,2,128,128]{3,2,1,0:T(8,128)S(1)} %get-tuple-element.55.green1), channel_id=1, source_target_pairs={{0,1},{2,3},{4,5},{6,7},{1,0},{3,2},{5,4},{7,6},{8,9},{10,11},{12,... | collective-permute-start | bytes 786440 | tf_op jit(solution)/shard_map/ppermute | solution.py:27
  9.8 9.1 %collective-permute-start.1 = (f32[2,2,128,128]{3,2,1,0:T(8,128)S(1)}, f32[2,2,128,128]{3,2,1,0:T(8,128)S(1)}, u32[]{:S(2)}, u32[]{:S(2)}) collective-permute-start(f32[2,2,128,128]{3,2,1,0:T(8,128)S(1)} %collective-permute-done.ahead), channel_id=1, source_target_pairs={{0,2},{2,4},{4,6},{6,7},{1,0},{3,1},{5,3},{7,5},{8,10},{10,12},{12... | collective-permute-start | bytes 786440 | tf_op jit(solution)/shard_map/ppermute | solution.py:51
  11.3 11.3 %collective-permute-start.5 = (f32[2,2,128,128]{3,2,1,0:T(8,128)S(1)}, f32[2,2,128,128]{3,2,1,0:T(8,128)S(1)}, u32[]{:S(2)}, u32[]{:S(2)}) collective-permute-start(f32[2,2,128,128]{3,2,1,0:T(8,128)S(1)} %get-tuple-element.55.green1), channel_id=1, source_target_pairs={{1,2},{3,4},{5,6},{2,1},{4,3},{6,5},{9,10},{11,12},{13,14},{10,9},... | collective-permute-start | bytes 786440 | tf_op jit(solution)/shard_map/ppermute | solution.py:27
  20.5 3.7 %collective-permute-start.7 = (f32[2,2,128,128]{3,2,1,0:T(8,128)S(1)}, f32[2,2,128,128]{3,2,1,0:T(8,128)S(1)}, u32[]{:S(2)}, u32[]{:S(2)}) collective-permute-start(f32[2,2,128,128]{3,2,1,0:T(8,128)S(1)} %get-tuple-element.61), channel_id=1, source_target_pairs={{0,8},{16,24},{8,0},{24,16},{1,9},{17,25},{9,1},{25,17},{2,10},{18... | collective-permute-start | bytes 786440 | tf_op jit(solution)/shard_map/ppermute | solution.py:27
  21.9 6.9 %collective-permute-start.6 = (f32[2,2,128,128]{3,2,1,0:T(8,128)S(1)}, f32[2,2,128,128]{3,2,1,0:T(8,128)S(1)}, u32[]{:S(2)}, u32[]{:S(2)}) collective-permute-start(f32[2,2,128,128]{3,2,1,0:T(8,128)S(1)} %get-tuple-element.59), channel_id=1, source_target_pairs={{0,2},{1,3},{2,0},{3,1},{4,6},{5,7},{6,4},{7,5},{8,16},{9,17},{10,... | collective-permute-start | bytes 786440 | tf_op jit(solution)/shard_map/ppermute | solution.py:40
  24.2 4.5 %collective-permute-start.10 = (f32[2,128]{1,0:T(2,128)S(1)}, f32[2,128]{1,0:T(2,128)S(1)}, u32[]{:S(2)}, u32[]{:S(2)}) collective-permute-start(f32[2,128]{1,0:T(2,128)S(1)} %get-tuple-element.68.rest_0_), channel_id=1, source_target_pairs={{0,24},{8,0},{16,8},{24,16},{1,25},{9,1},{17,9},{25,17},{2,26},{10... | collective-permute-start | bytes 3080 | tf_op jit(solution)/shard_map/ppermute | solution.py:231
  25.9 2.8 %collective-permute-start.9 = (f32[2,128]{1,0:T(2,128)S(1)}, f32[2,128]{1,0:T(2,128)S(1)}, u32[]{:S(2)}, u32[]{:S(2)}) collective-permute-start(f32[2,128]{1,0:T(2,128)S(1)} %get-tuple-element.68.rest_0_), channel_id=1, source_target_pairs={{0,16},{8,24},{16,0},{24,8},{1,17},{9,25},{17,1},{25,9},{2,18},{10... | collective-permute-start | bytes 3080 | tf_op jit(solution)/shard_map/ppermute | solution.py:231
  26.8 2.7 %collective-permute-start.8 = (f32[2,128]{1,0:T(2,128)S(1)}, f32[2,128]{1,0:T(2,128)S(1)}, u32[]{:S(2)}, u32[]{:S(2)}) collective-permute-start(f32[2,128]{1,0:T(2,128)S(1)} %get-tuple-element.68.rest_0_), channel_id=1, source_target_pairs={{0,8},{8,16},{16,24},{24,0},{1,9},{9,17},{17,25},{25,1},{2,10},{10... | collective-permute-start | bytes 3080 | tf_op jit(solution)/shard_map/ppermute | solution.py:231
  28.7 5.8 %collective-permute-start.11 = (f32[2,2,128,128]{3,2,1,0:T(8,128)S(1)}, f32[2,2,128,128]{3,2,1,0:T(8,128)S(1)}, u32[]{:S(2)}, u32[]{:S(2)}) collective-permute-start(f32[2,2,128,128]{3,2,1,0:T(8,128)S(1)} %get-tuple-element.66), channel_id=1, source_target_pairs={{0,1},{1,0},{2,3},{3,2},{4,5},{5,4},{6,7},{7,6},{8,16},{9,17},{10,... | collective-permute-start | bytes 786440 | tf_op jit(solution)/shard_map/ppermute | solution.py:40
  29.4 5.1 %collective-permute-start.12 = (f32[2,2,128,128]{3,2,1,0:T(8,128)S(1)}, f32[2,2,128,128]{3,2,1,0:T(8,128)S(1)}, u32[]{:S(2)}, u32[]{:S(2)}) collective-permute-start(f32[2,2,128,128]{3,2,1,0:T(8,128)S(1)} %get-tuple-element.67), channel_id=1, source_target_pairs={{0,8},{16,24},{8,0},{24,16},{1,9},{17,25},{9,1},{25,17},{2,10},{18... | collective-permute-start | bytes 786440 | tf_op jit(solution)/shard_map/ppermute | solution.py:27

commit v5 on v3

--- a/solution.py
+++ b/solution.py
@@ -154,10 +154,7 @@
     add_pairs(PAIR, neighbours, phonon, coupling, blocks, (total,), picked, BATCH)
 
 
-def turn_kernel(
-    size, neighbours, phonon, coupling, ahead, before, green, by_core, by_cross,
-    total, turned, blocks, picked,
-):
+def turn_kernel(size, total0, green, by_core, by_cross, turned, partial):
     e_local, a_local = green.shape[1], green.shape[2]
     core, cross = partner_energies(turned.shape[1])
     has_core, has_cross = has_partners(size)
@@ -168,7 +165,8 @@
             for e in range(REACH):
                 turned[c, core + e, a] = by_core[c, e, a].T * has_core
                 turned[c, cross + e, a] = by_cross[c, e, a].T * has_cross
-    pair_kernel(neighbours, phonon, coupling, ahead, before, total, blocks, picked)
+    for a in range(a_local):
+        partial[a] = rate_sums(total0, turned, 0, a)
 
 
 def partner_energies(spread):
@@ -197,13 +195,9 @@
     return sums
 
 
-def far_kernel(
-    neighbours, phonon, coupling, across, before, turned, total, core, cross, partial, blocks, picked
-):
+def far_kernel(neighbours, phonon, coupling, across, before, total, core, cross, blocks, picked):
     add_far(neighbours, phonon, coupling, across, before, total, blocks, picked)
     finish(total, core, cross)
-    for a in range(partial.shape[0]):
-        partial[a] = rate_sums(total, turned, 0, a)
 
 
 def add_far(neighbours, phonon, coupling, across, before, total, blocks, picked):
@@ -286,15 +280,21 @@
     (total0,) = call(pair_kernel, [spread], (ahead0, total0))
     green1, total0 = lax.optimization_barrier((green1, total0))
     across1 = swap(green1, "atom", 1)
-    total1, turned = call(
+    (total1,) = call(pair_kernel, [spread], (ahead1, total1))
+    total0, total1 = lax.optimization_barrier((total0, total1))
+    total0, core0, cross0 = call(far_kernel, [spread, edge, edge], (across0, total0))
+    core0, cross0 = swap(core0, "energy", 0), cross_swap(cross0, 2)
+    turned, partial = pl.pallas_call(
         functools.partial(turn_kernel, energies),
-        [spread, (2,) + spread],
-        (ahead1, total1, green, by_core, by_cross),
-    )
-    total0, core0, cross0, partial = call(
-        far_kernel, [spread, edge, edge, (a_local, orb, orb)], (across0, total0, turned)
-    )
-    core0, cross0 = swap(core0, "energy", 0), cross_swap(cross0, 2)
+        out_shape=[
+            jax.ShapeDtypeStruct((2,) + spread, jnp.float32),
+            jax.ShapeDtypeStruct((a_local, orb, orb), jnp.float32),
+        ],
+        in_specs=[VMEM] * 4,
+        out_specs=[VMEM] * 2,
+        compiler_params=pltpu.CompilerParams(vmem_limit_bytes=24 * 2**20),
+        cost_estimate=pl.CostEstimate(flops=10**6, bytes_accessed=10**4, transcendentals=0),
+    )(total0, green, by_core, by_cross)
     total1, core1, cross1, rate = call(
         functools.partial(last_kernel, 1.0 / (4.0 * points)),
         [spread, edge, edge, (a_local, orb)],

time: 35 us -> 34.9 us (level)
  waiting for transfers between devices: 8.41 us -> 8.95 us
  Pallas kernels: 12.7 us -> 12.3 us
    ppermute x3, starting transfers between devices: 5.74 us -> 4.67 us  [exchange(): return lax.ppermute(x, ('energy', 'atom'), perm)]
    pallas_call x5, Pallas kernels: 9.42 us -> 8.38 us  [call(): pl.pallas_call(kernel, out_shape=[jax.ShapeDtypeStruct(shape, jnp.float32...]
    ppermute x1, starting transfers between devices: 0.76 us -> 1.65 us  [forward(): return lax.ppermute(x, axis, [(i, j) for i, j in ups + downs if i != j])]
    pallas_call x0 -> x1, Pallas kernels: none -> 0.58 us  [per_device(): pl.pallas_call(functools.partial(turn_kernel, energies), out_shape=[jax.S...]
    ppermute x1, waiting for transfers between devices: 3.5 us -> 3.9 us  [forward(): return lax.ppermute(x, axis, [(i, j) for i, j in ups + downs if i != j])]
  transfers between devices with their start and end apart: 13 -> 13, of which waited for: 5 -> 6; matrix products, arithmetic and copies ran while one was open for 0% -> 0% of each run, Pallas kernels for 31% -> 30%
where the time goes in v5:
time: 34.9 us; the launch traced here: 34.7 us
  starting transfers between devices  12.8 us (37%)
  Pallas kernels  12.3 us (35%)
  waiting for transfers between devices  8.95 us (26%)
  between operations  0.72 us (2%)
    pallas_call x5, Pallas kernels, call(): pl.pallas_call(kernel, out_shape=[jax.ShapeDtypeStruct(shape, jnp.float32...  8.38 us
    ppermute x6, starting transfers between devices, swap(): lax.ppermute(x, axis, [(i, i + 1) for i in low] + [(i + 1, i) for i in low])  5.03 us
    ppermute x3, starting transfers between devices, exchange(): return lax.ppermute(x, ('energy', 'atom'), perm)  4.67 us
    ppermute x1, waiting for transfers between devices, forward(): return lax.ppermute(x, axis, [(i, j) for i, j in ups + downs if i != j])  3.9 us
    ppermute x3, waiting for transfers between devices, exchange(): return lax.ppermute(x, ('energy', 'atom'), perm)  3.07 us
    pallas_call x2, Pallas kernels, fetch(): pl.pallas_call(kernel, out_shape=[jax.ShapeDtypeStruct(x.shape, x.dtype)...  2.38 us
    ppermute x1, starting transfers between devices, forward(): return lax.ppermute(x, axis, [(i, j) for i, j in ups + downs if i != j])  1.65 us
    ppermute x3, starting transfers between devices, addends(): return [x] + [lax.ppermute(x, axis, turn) for turn in turns]  1.44 us
  transfers between devices with their start and end apart: 13, of which 6 were waited for; matrix products, arithmetic and copies ran while one was open for 0% of the time, Pallas kernels for 30%

profile of v5, /device:TPU:0, one launch (start us, length us, event | category | flops | bytes accessed | tf_op | source)
XLA Modules:
  0.0 34.7 jit_solution(2720493861483151377)
XLA Ops:
  0.6 1.0 %shard_map.59.green0 = f32[2,2,128,128]{3,2,1,0:T(8,128)S(1)} custom-call(f32[2,2,2,128,128]{4,3,2,1,0:T(8,128)} %green.2), custom_call_target="tpu_custom_call" | custom-call | tf_op jit(solution)/shard_map/pallas_call | solution.py:260
  1.6 3.0 %collective-permute-start = (f32[2,2,128,128]{3,2,1,0:T(8,128)S(1)}, f32[2,2,128,128]{3,2,1,0:T(8,128)S(1)}, u32[]{:S(2)}, u32[]{:S(2)}) collective-permute-start(f32[2,2,128,128]{3,2,1,0:T(8,128)S(1)} %shard_map.59.green0), channel_id=1, source_target_pairs={{0,1},{2,3},{4,5},{6,7},{1,0},{3,2},{5,4},{7,6},{8,9},{10,11},{12,... | collective-permute-start | bytes 786440 | tf_op jit(solution)/shard_map/ppermute | solution.py:27
  4.6 1.4 %shard_map.60 = (f32[2,2,128,128]{3,2,1,0:T(8,128)S(1)}, f32[2,2,2,128,128]{4,3,2,1,0:T(8,128)S(1)}, f32[2,6,128,128]{3,2,1,0:T(8,128)S(1)}, f32[2,4,6]{2,1,0:T(4,128)S(1)}, s32[2,6]{1,0:T(2,128)S(1)}) custom-call(f32[2,2,2,128,128]{4,3,2,1,0:T(8,128)} %green.2, f32[2,6,128,128]{3,2,1,0:T(8,128)} %coupling, f32[2,4,6]{2,1,0:T(4,128)} %bitcast.1, s32[2,6]{1,0:T(2,128)} %neighbours), custom_call_target="tpu_custom_call" | custom-call | tf_op jit(solution)/shard_map/pallas_call | solution.py:260
  6.1 1.6 %collective-permute-start.5 = (f32[2,2,2,128,128]{4,3,2,1,0:T(8,128)S(1)}, f32[2,2,2,128,128]{4,3,2,1,0:T(8,128)S(1)}, u32[]{:S(2)}, u32[]{:S(2)}) collective-permute-start(f32[2,2,2,128,128]{4,3,2,1,0:T(8,128)S(1)} %get-tuple-element.52.green), channel_id=1, source_target_pairs={{0,2},{1,3},{2,0},{3,1},{4,6},{5,7},{6,4},{7,5},{8,16},{9,17},{10,... | collective-permute-start | bytes 1572872 | tf_op jit(solution)/shard_map/ppermute | solution.py:40
  7.7 0.0 collective-permute-start.4
  7.7 0.5 %collective-permute-start.2 = (f32[2,2,128,128]{3,2,1,0:T(8,128)S(1)}, f32[2,2,128,128]{3,2,1,0:T(8,128)S(1)}, u32[]{:S(2)}, u32[]{:S(2)}) collective-permute-start(f32[2,2,128,128]{3,2,1,0:T(8,128)S(1)} %get-tuple-element.50.green1), channel_id=1, source_target_pairs={{0,1},{2,3},{4,5},{6,7},{1,0},{3,2},{5,4},{7,6},{8,9},{10,11},{12,... | collective-permute-start | bytes 786440 | tf_op jit(solution)/shard_map/ppermute | solution.py:27
  8.2 3.9 %shard_map.61 = (f32[6,2,128,128]{3,2,1,0:T(8,128)S(1)}, f32[6,2,128,128]{3,2,1,0:T(8,128)S(1)}) custom-call(s32[2,6]{1,0:T(2,128)S(1)} %get-tuple-element.37.neighbours, f32[2,4,6]{2,1,0:T(4,128)S(1)} %get-tuple-element.38.phonon, f32[2,6,128,128]{3,2,1,0:T(8,128)S(1)} %get-tuple-element.39.coupling, f32[2,2,128,128]{3,2,1,0:T(8,128)S(1)} %shard_map.59.green0, ...), custom_call_target="tpu_custom_call" | custom-call | flops 1000000 | bytes 10000 | tf_op jit(solution)/shard_map/pallas_call | solution.py:246
  12.2 0.0 collective-permute-done.ahead
  12.2 1.6 %collective-permute-start.1 = (f32[2,2,128,128]{3,2,1,0:T(8,128)S(1)}, f32[2,2,128,128]{3,2,1,0:T(8,128)S(1)}, u32[]{:S(2)}, u32[]{:S(2)}) collective-permute-start(f32[2,2,128,128]{3,2,1,0:T(8,128)S(1)} %collective-permute-done.ahead), channel_id=1, source_target_pairs={{0,2},{2,4},{4,6},{6,7},{1,0},{3,1},{5,3},{7,5},{8,10},{10,12},{12... | collective-permute-start | bytes 786440 | tf_op jit(solution)/shard_map/ppermute | solution.py:51
  13.8 1.4 %shard_map.62.before = f32[6,2,128,128]{3,2,1,0:T(8,128)S(1)} custom-call(s32[2,6]{1,0:T(2,128)S(1)} %get-tuple-element.37.neighbours, f32[2,4,6]{2,1,0:T(4,128)S(1)} %get-tuple-element.38.phonon, f32[2,6,128,128]{3,2,1,0:T(8,128)S(1)} %get-tuple-element.39.coupling, f32[2,2,128,128]{3,2,1,0:T(8,128)S(1)} %collective-permute-done.ahead, ...), custom_call_target="tpu_custom_call" | custom-call | flops 1000000 | bytes 10000 | tf_op jit(solution)/shard_map/pallas_call | solution.py:246
  15.2 0.7 %collective-permute-start.3 = (f32[2,2,128,128]{3,2,1,0:T(8,128)S(1)}, f32[2,2,128,128]{3,2,1,0:T(8,128)S(1)}, u32[]{:S(2)}, u32[]{:S(2)}) collective-permute-start(f32[2,2,128,128]{3,2,1,0:T(8,128)S(1)} %get-tuple-element.50.green1), channel_id=1, source_target_pairs={{1,2},{3,4},{5,6},{2,1},{4,3},{6,5},{9,10},{11,12},{13,14},{10,9},... | collective-permute-start | bytes 786440 | tf_op jit(solution)/shard_map/ppermute | solution.py:27
  15.9 0.9 %collective-permute-done.2.ahead = f32[2,2,128,128]{3,2,1,0:T(8,128)S(1)} collective-permute-done((f32[2,2,128,128]{3,2,1,0:T(8,128)S(1)}, f32[2,2,128,128]{3,2,1,0:T(8,128)S(1)}, u32[]{:S(2)}, u32[]{:S(2)}) %collective-permute-start.2) | collective-permute-done | bytes 262176 | tf_op jit(solution)/shard_map/ppermute | solution.py:27
  16.8 1.4 %shard_map.63.before = f32[6,2,128,128]{3,2,1,0:T(8,128)S(1)} custom-call(s32[2,6]{1,0:T(2,128)S(1)} %get-tuple-element.37.neighbours, f32[2,4,6]{2,1,0:T(4,128)S(1)} %get-tuple-element.38.phonon, f32[2,6,128,128]{3,2,1,0:T(8,128)S(1)} %get-tuple-element.39.coupling, f32[2,2,128,128]{3,2,1,0:T(8,128)S(1)} %collective-permute-done.2.ahead, ...), custom_call_target="tpu_custom_call" | custom-call | flops 1000000 | bytes 10000 | tf_op jit(solution)/shard_map/pallas_call | solution.py:246
  18.3 3.9 %collective-permute-done.1.across = f32[2,2,128,128]{3,2,1,0:T(8,128)S(1)} collective-permute-done((f32[2,2,128,128]{3,2,1,0:T(8,128)S(1)}, f32[2,2,128,128]{3,2,1,0:T(8,128)S(1)}, u32[]{:S(2)}, u32[]{:S(2)}) %collective-permute-start.1) | collective-permute-done | bytes 262176 | tf_op jit(solution)/shard_map/ppermute | solution.py:51
  22.2 0.7 %shard_map.64 = (f32[6,2,128,128]{3,2,1,0:T(8,128)S(1)}, f32[2,2,128,128]{3,2,1,0:T(8,128)S(1)}, f32[2,2,128,128]{3,2,1,0:T(8,128)S(1)}) custom-call(s32[2,6]{1,0:T(2,128)S(1)} %get-tuple-element.37.neighbours, f32[2,4,6]{2,1,0:T(4,128)S(1)} %get-tuple-element.38.phonon, f32[2,6,128,128]{3,2,1,0:T(8,128)S(1)} %get-tuple-element.39.coupling, ...), custom_call_target="tpu_custom_call" | custom-call | flops 1000000 | bytes 10000 | tf_op jit(solution)/shard_map/pallas_call | solution.py:246
  22.9 1.1 %collective-permute-start.6 = (f32[2,2,128,128]{3,2,1,0:T(8,128)S(1)}, f32[2,2,128,128]{3,2,1,0:T(8,128)S(1)}, u32[]{:S(2)}, u32[]{:S(2)}) collective-permute-start(f32[2,2,128,128]{3,2,1,0:T(8,128)S(1)} %get-tuple-element.56), channel_id=1, source_target_pairs={{0,2},{1,3},{2,0},{3,1},{4,6},{5,7},{6,4},{7,5},{8,16},{9,17},{10,... | collective-permute-start | bytes 786440 | tf_op jit(solution)/shard_map/ppermute | solution.py:40
  24.0 0.8 %collective-permute-start.7 = (f32[2,2,128,128]{3,2,1,0:T(8,128)S(1)}, f32[2,2,128,128]{3,2,1,0:T(8,128)S(1)}, u32[]{:S(2)}, u32[]{:S(2)}) collective-permute-start(f32[2,2,128,128]{3,2,1,0:T(8,128)S(1)} %get-tuple-element.57), channel_id=1, source_target_pairs={{0,8},{16,24},{8,0},{24,16},{1,9},{17,25},{9,1},{25,17},{2,10},{18... | collective-permute-start | bytes 786440 | tf_op jit(solution)/shard_map/ppermute | solution.py:27
  24.8 0.0 collective-permute-done.5.by_cross
  24.8 0.0 collective-permute-done.4.by_core
  24.8 0.6 %shard_map.65 = (f32[2,6,2,128,128]{4,3,2,1,0:T(8,128)S(1)}, f32[2,128,128]{2,1,0:T(8,128)S(1)}) custom-call(f32[6,2,128,128]{3,2,1,0:T(8,128)S(1)} %get-tuple-element.49.total0, f32[2,2,2,128,128]{4,3,2,1,0:T(8,128)S(1)} %get-tuple-element.52.green, f32[2,2,2,128,128]{4,3,2,1,0:T(8,128)S(1)} %collective-permute-done.4.by_core, ...), custom_call_target="tpu_custom_call" | custom-call | flops 1000000 | bytes 10000 | tf_op jit(solution)/shard_map/pallas_call | solution.py:287
  25.4 0.0 collective-permute-done.3.across
  25.4 0.9 %shard_map.66 = (f32[6,2,128,128]{3,2,1,0:T(8,128)S(1)}, f32[2,2,128,128]{3,2,1,0:T(8,128)S(1)}, f32[2,2,128,128]{3,2,1,0:T(8,128)S(1)}, f32[2,128]{1,0:T(2,128)S(1)}) custom-call(s32[2,6]{1,0:T(2,128)S(1)} %get-tuple-element.37.neighbours, f32[2,4,6]{2,1,0:T(4,128)S(1)} %get-tuple-element.38.phonon, f32[2,6,128,128]{3,2,1,0:T(8,128)S(1)} %get-tuple-element.39.coupling, ...), custom_call_target="tpu_custom_call" | custom-call | flops 1000000 | bytes 10000 | tf_op jit(solution)/shard_map/pallas_call | solution.py:246
  26.3 1.9 %collective-permute-start.8 = (f32[2,2,128,128]{3,2,1,0:T(8,128)S(1)}, f32[2,2,128,128]{3,2,1,0:T(8,128)S(1)}, u32[]{:S(2)}, u32[]{:S(2)}) collective-permute-start(f32[2,2,128,128]{3,2,1,0:T(8,128)S(1)} %get-tuple-element.61), channel_id=1, source_target_pairs={{0,1},{1,0},{2,3},{3,2},{4,5},{5,4},{6,7},{7,6},{8,16},{9,17},{10,... | collective-permute-start | bytes 786440 | tf_op jit(solution)/shard_map/ppermute | solution.py:40
  28.2 0.0 collective-permute-start.9
  28.2 1.1 %collective-permute-done.6.cross0 = f32[2,2,128,128]{3,2,1,0:T(8,128)S(1)} collective-permute-done((f32[2,2,128,128]{3,2,1,0:T(8,128)S(1)}, f32[2,2,128,128]{3,2,1,0:T(8,128)S(1)}, u32[]{:S(2)}, u32[]{:S(2)}) %collective-permute-start.6) | collective-permute-done | bytes 262176 | tf_op jit(solution)/shard_map/ppermute | solution.py:40
  29.4 0.0 collective-permute-done.7.core0
  29.4 0.0 collective-permute-start.12
  29.4 1.4 %collective-permute-start.11 = (f32[2,128]{1,0:T(2,128)S(1)}, f32[2,128]{1,0:T(2,128)S(1)}, u32[]{:S(2)}, u32[]{:S(2)}) collective-permute-start(f32[2,128]{1,0:T(2,128)S(1)} %get-tuple-element.63.rest_0_), channel_id=1, source_target_pairs={{0,16},{8,24},{16,0},{24,8},{1,17},{9,25},{17,1},{25,9},{2,18},{10... | collective-permute-start | bytes 3080 | tf_op jit(solution)/shard_map/ppermute | solution.py:225
  30.8 0.0 collective-permute-start.10
  30.8 2.0 %collective-permute-done.8.cross1 = f32[2,2,128,128]{3,2,1,0:T(8,128)S(1)} collective-permute-done((f32[2,2,128,128]{3,2,1,0:T(8,128)S(1)}, f32[2,2,128,128]{3,2,1,0:T(8,128)S(1)}, u32[]{:S(2)}, u32[]{:S(2)}) %collective-permute-start.8) | collective-permute-done | bytes 262176 | tf_op jit(solution)/shard_map/ppermute | solution.py:40
  32.8 0.0 collective-permute-done.9.core1
  32.8 0.0 collective-permute-done.12.rest_3_
  32.8 0.2 collective-permute-done.11.rest_2_
  32.9 0.9 %collective-permute-done.10.rest_1_ = f32[2,128]{1,0:T(2,128)S(1)} collective-permute-done((f32[2,128]{1,0:T(2,128)S(1)}, f32[2,128]{1,0:T(2,128)S(1)}, u32[]{:S(2)}, u32[]{:S(2)}) %collective-permute-start.10) | collective-permute-done | bytes 1056 | tf_op jit(solution)/shard_map/ppermute | solution.py:225
  33.8 0.9 %shard_map.67 = (f32[2,2,2,128,128]{4,3,2,1,0:T(8,128)}, f32[2,128]{1,0:T(2,128)}) custom-call(f32[6,2,128,128]{3,2,1,0:T(8,128)S(1)} %get-tuple-element.49.total0, f32[6,2,128,128]{3,2,1,0:T(8,128)S(1)} %get-tuple-element.55.total1, f32[2,2,128,128]{3,2,1,0:T(8,128)S(1)} %collective-permute-done.6.cross0, ...), custom_call_target="tpu_custom_call" | custom-call | flops 1000000 | bytes 2000000 | tf_op jit(solution)/shard_map/pallas_call | solution.py:306
Async XLA Ops:
  1.6 10.6 %collective-permute-start = (f32[2,2,128,128]{3,2,1,0:T(8,128)S(1)}, f32[2,2,128,128]{3,2,1,0:T(8,128)S(1)}, u32[]{:S(2)}, u32[]{:S(2)}) collective-permute-start(f32[2,2,128,128]{3,2,1,0:T(8,128)S(1)} %shard_map.59.green0), channel_id=1, source_target_pairs={{0,1},{2,3},{4,5},{6,7},{1,0},{3,2},{5,4},{7,6},{8,9},{10,11},{12,... | collective-permute-start | bytes 786440 | tf_op jit(solution)/shard_map/ppermute | solution.py:27
  6.1 18.8 %collective-permute-start.5 = (f32[2,2,2,128,128]{4,3,2,1,0:T(8,128)S(1)}, f32[2,2,2,128,128]{4,3,2,1,0:T(8,128)S(1)}, u32[]{:S(2)}, u32[]{:S(2)}) collective-permute-start(f32[2,2,2,128,128]{4,3,2,1,0:T(8,128)S(1)} %get-tuple-element.52.green), channel_id=1, source_target_pairs={{0,2},{1,3},{2,0},{3,1},{4,6},{5,7},{6,4},{7,5},{8,16},{9,17},{10,... | collective-permute-start | bytes 1572872 | tf_op jit(solution)/shard_map/ppermute | solution.py:40
  7.7 17.1 %collective-permute-start.4 = (f32[2,2,2,128,128]{4,3,2,1,0:T(8,128)S(1)}, f32[2,2,2,128,128]{4,3,2,1,0:T(8,128)S(1)}, u32[]{:S(2)}, u32[]{:S(2)}) collective-permute-start(f32[2,2,2,128,128]{4,3,2,1,0:T(8,128)S(1)} %get-tuple-element.52.green), channel_id=1, source_target_pairs={{0,8},{16,24},{8,0},{24,16},{1,9},{17,25},{9,1},{25,17},{2,10},{18... | collective-permute-start | bytes 1572872 | tf_op jit(solution)/shard_map/ppermute | solution.py:27
  7.7 9.1 %collective-permute-start.2 = (f32[2,2,128,128]{3,2,1,0:T(8,128)S(1)}, f32[2,2,128,128]{3,2,1,0:T(8,128)S(1)}, u32[]{:S(2)}, u32[]{:S(2)}) collective-permute-start(f32[2,2,128,128]{3,2,1,0:T(8,128)S(1)} %get-tuple-element.50.green1), channel_id=1, source_target_pairs={{0,1},{2,3},{4,5},{6,7},{1,0},{3,2},{5,4},{7,6},{8,9},{10,11},{12,... | collective-permute-start | bytes 786440 | tf_op jit(solution)/shard_map/ppermute | solution.py:27
  12.2 10.0 %collective-permute-start.1 = (f32[2,2,128,128]{3,2,1,0:T(8,128)S(1)}, f32[2,2,128,128]{3,2,1,0:T(8,128)S(1)}, u32[]{:S(2)}, u32[]{:S(2)}) collective-permute-start(f32[2,2,128,128]{3,2,1,0:T(8,128)S(1)} %collective-permute-done.ahead), channel_id=1, source_target_pairs={{0,2},{2,4},{4,6},{6,7},{1,0},{3,1},{5,3},{7,5},{8,10},{10,12},{12... | collective-permute-start | bytes 786440 | tf_op jit(solution)/shard_map/ppermute | solution.py:51
  15.2 10.2 %collective-permute-start.3 = (f32[2,2,128,128]{3,2,1,0:T(8,128)S(1)}, f32[2,2,128,128]{3,2,1,0:T(8,128)S(1)}, u32[]{:S(2)}, u32[]{:S(2)}) collective-permute-start(f32[2,2,128,128]{3,2,1,0:T(8,128)S(1)} %get-tuple-element.50.green1), channel_id=1, source_target_pairs={{1,2},{3,4},{5,6},{2,1},{4,3},{6,5},{9,10},{11,12},{13,14},{10,9},... | collective-permute-start | bytes 786440 | tf_op jit(solution)/shard_map/ppermute | solution.py:27
  22.9 6.4 %collective-permute-start.6 = (f32[2,2,128,128]{3,2,1,0:T(8,128)S(1)}, f32[2,2,128,128]{3,2,1,0:T(8,128)S(1)}, u32[]{:S(2)}, u32[]{:S(2)}) collective-permute-start(f32[2,2,128,128]{3,2,1,0:T(8,128)S(1)} %get-tuple-element.56), channel_id=1, source_target_pairs={{0,2},{1,3},{2,0},{3,1},{4,6},{5,7},{6,4},{7,5},{8,16},{9,17},{10,... | collective-permute-start | bytes 786440 | tf_op jit(solution)/shard_map/ppermute | solution.py:40
  24.0 5.3 %collective-permute-start.7 = (f32[2,2,128,128]{3,2,1,0:T(8,128)S(1)}, f32[2,2,128,128]{3,2,1,0:T(8,128)S(1)}, u32[]{:S(2)}, u32[]{:S(2)}) collective-permute-start(f32[2,2,128,128]{3,2,1,0:T(8,128)S(1)} %get-tuple-element.57), channel_id=1, source_target_pairs={{0,8},{16,24},{8,0},{24,16},{1,9},{17,25},{9,1},{25,17},{2,10},{18... | collective-permute-start | bytes 786440 | tf_op jit(solution)/shard_map/ppermute | solution.py:27
  26.3 6.4 %collective-permute-start.8 = (f32[2,2,128,128]{3,2,1,0:T(8,128)S(1)}, f32[2,2,128,128]{3,2,1,0:T(8,128)S(1)}, u32[]{:S(2)}, u32[]{:S(2)}) collective-permute-start(f32[2,2,128,128]{3,2,1,0:T(8,128)S(1)} %get-tuple-element.61), channel_id=1, source_target_pairs={{0,1},{1,0},{2,3},{3,2},{4,5},{5,4},{6,7},{7,6},{8,16},{9,17},{10,... | collective-permute-start | bytes 786440 | tf_op jit(solution)/shard_map/ppermute | solution.py:40
  28.2 4.5 %collective-permute-start.9 = (f32[2,2,128,128]{3,2,1,0:T(8,128)S(1)}, f32[2,2,128,128]{3,2,1,0:T(8,128)S(1)}, u32[]{:S(2)}, u32[]{:S(2)}) collective-permute-start(f32[2,2,128,128]{3,2,1,0:T(8,128)S(1)} %get-tuple-element.62), channel_id=1, source_target_pairs={{0,8},{16,24},{8,0},{24,16},{1,9},{17,25},{9,1},{25,17},{2,10},{18... | collective-permute-start | bytes 786440 | tf_op jit(solution)/shard_map/ppermute | solution.py:27
  29.4 3.4 %collective-permute-start.12 = (f32[2,128]{1,0:T(2,128)S(1)}, f32[2,128]{1,0:T(2,128)S(1)}, u32[]{:S(2)}, u32[]{:S(2)}) collective-permute-start(f32[2,128]{1,0:T(2,128)S(1)} %get-tuple-element.63.rest_0_), channel_id=1, source_target_pairs={{0,24},{8,0},{16,8},{24,16},{1,25},{9,1},{17,9},{25,17},{2,26},{10... | collective-permute-start | bytes 3080 | tf_op jit(solution)/shard_map/ppermute | solution.py:225
  29.4 3.6 %collective-permute-start.11 = (f32[2,128]{1,0:T(2,128)S(1)}, f32[2,128]{1,0:T(2,128)S(1)}, u32[]{:S(2)}, u32[]{:S(2)}) collective-permute-start(f32[2,128]{1,0:T(2,128)S(1)} %get-tuple-element.63.rest_0_), channel_id=1, source_target_pairs={{0,16},{8,24},{16,0},{24,8},{1,17},{9,25},{17,1},{25,9},{2,18},{10... | collective-permute-start | bytes 3080 | tf_op jit(solution)/shard_map/ppermute | solution.py:225
  30.8 3.0 %collective-permute-start.10 = (f32[2,128]{1,0:T(2,128)S(1)}, f32[2,128]{1,0:T(2,128)S(1)}, u32[]{:S(2)}, u32[]{:S(2)}) collective-permute-start(f32[2,128]{1,0:T(2,128)S(1)} %get-tuple-element.63.rest_0_), channel_id=1, source_target_pairs={{0,8},{8,16},{16,24},{24,0},{1,9},{9,17},{17,25},{25,1},{2,10},{10... | collective-permute-start | bytes 3080 | tf_op jit(solution)/shard_map/ppermute | solution.py:225

commit v6 on v5

--- a/solution.py
+++ b/solution.py
@@ -221,7 +221,10 @@
     size = lax.axis_size(axis)
     if size > FEW:
         return [lax.psum(x, axis)]
-    turns = [[(i, (i + k) % size) for i in range(size)] for k in range(1, size)]
+    if size & (size - 1):
+        turns = [[(i, (i + k) % size) for i in range(size)] for k in range(1, size)]
+    else:
+        turns = [[(i, i ^ k) for i in range(size)] for k in range(1, size)]
     return [x] + [lax.ppermute(x, axis, turn) for turn in turns]
 
 

time: 34.9 us -> 34.1 us (0.977)
  Pallas kernels: 12.3 us -> 11.6 us
    ppermute x3, waiting for transfers between devices: 1.03 us -> 0.21 us  [addends(): return [x] + [lax.ppermute(x, axis, turn) for turn in turns]]
    ppermute x6, starting transfers between devices: 5.03 us -> 4.31 us  [swap(): lax.ppermute(x, axis, [(i, i + 1) for i in low] + [(i + 1, i) for i in low])]
    pallas_call x5, Pallas kernels: 8.38 us -> 7.74 us  [call(): pl.pallas_call(kernel, out_shape=[jax.ShapeDtypeStruct(shape, jnp.float32...]
    ppermute x3, starting transfers between devices: 1.44 us -> 1.86 us  [addends(): return [x] + [lax.ppermute(x, axis, turn) for turn in turns]]
  transfers between devices with their start and end apart: 13 -> 13, of which waited for: 6 -> 5; matrix products, arithmetic and copies ran while one was open for 0% -> 0% of each run, Pallas kernels for 30% -> 29%
where the time goes in v6:
time: 34.1 us; the launch traced here: 33.9 us
  starting transfers between devices  12.9 us (38%)
  Pallas kernels  11.6 us (34%)
  waiting for transfers between devices  8.66 us (25%)
  between operations  0.72 us (2%)
    pallas_call x5, Pallas kernels, call(): pl.pallas_call(kernel, out_shape=[jax.ShapeDtypeStruct(shape, jnp.float32...  7.74 us
    ppermute x3, starting transfers between devices, exchange(): return lax.ppermute(x, ('energy', 'atom'), perm)  4.76 us
    ppermute x6, starting transfers between devices, swap(): lax.ppermute(x, axis, [(i, i + 1) for i in low] + [(i + 1, i) for i in low])  4.31 us
    ppermute x1, waiting for transfers between devices, forward(): return lax.ppermute(x, axis, [(i, j) for i, j in ups + downs if i != j])  3.9 us
    ppermute x3, waiting for transfers between devices, exchange(): return lax.ppermute(x, ('energy', 'atom'), perm)  3.29 us
    pallas_call x2, Pallas kernels, fetch(): pl.pallas_call(kernel, out_shape=[jax.ShapeDtypeStruct(x.shape, x.dtype)...  2.38 us
    ppermute x1, starting transfers between devices, forward(): return lax.ppermute(x, axis, [(i, j) for i, j in ups + downs if i != j])  1.96 us
    ppermute x3, starting transfers between devices, addends(): return [x] + [lax.ppermute(x, axis, turn) for turn in turns]  1.86 us
  transfers between devices with their start and end apart: 13, of which 5 were waited for; matrix products, arithmetic and copies ran while one was open for 0% of the time, Pallas kernels for 29%

profile of v6, /device:TPU:0, one launch (start us, length us, event | category | flops | bytes accessed | tf_op | source)
XLA Modules:
  0.0 33.9 jit_solution(8548600804667164676)
XLA Ops:
  0.6 1.0 %shard_map.59.green0 = f32[2,2,128,128]{3,2,1,0:T(8,128)S(1)} custom-call(f32[2,2,2,128,128]{4,3,2,1,0:T(8,128)} %green.2), custom_call_target="tpu_custom_call" | custom-call | tf_op jit(solution)/shard_map/pallas_call | solution.py:263
  1.6 3.0 %collective-permute-start = (f32[2,2,128,128]{3,2,1,0:T(8,128)S(1)}, f32[2,2,128,128]{3,2,1,0:T(8,128)S(1)}, u32[]{:S(2)}, u32[]{:S(2)}) collective-permute-start(f32[2,2,128,128]{3,2,1,0:T(8,128)S(1)} %shard_map.59.green0), channel_id=1, source_target_pairs={{0,1},{2,3},{4,5},{6,7},{1,0},{3,2},{5,4},{7,6},{8,9},{10,11},{12,... | collective-permute-start | bytes 786440 | tf_op jit(solution)/shard_map/ppermute | solution.py:27
  4.6 1.4 %shard_map.60 = (f32[2,2,128,128]{3,2,1,0:T(8,128)S(1)}, f32[2,2,2,128,128]{4,3,2,1,0:T(8,128)S(1)}, f32[2,6,128,128]{3,2,1,0:T(8,128)S(1)}, f32[2,4,6]{2,1,0:T(4,128)S(1)}, s32[2,6]{1,0:T(2,128)S(1)}) custom-call(f32[2,2,2,128,128]{4,3,2,1,0:T(8,128)} %green.2, f32[2,6,128,128]{3,2,1,0:T(8,128)} %coupling, f32[2,4,6]{2,1,0:T(4,128)} %bitcast.1, s32[2,6]{1,0:T(2,128)} %neighbours), custom_call_target="tpu_custom_call" | custom-call | tf_op jit(solution)/shard_map/pallas_call | solution.py:263
  6.1 1.6 %collective-permute-start.5 = (f32[2,2,2,128,128]{4,3,2,1,0:T(8,128)S(1)}, f32[2,2,2,128,128]{4,3,2,1,0:T(8,128)S(1)}, u32[]{:S(2)}, u32[]{:S(2)}) collective-permute-start(f32[2,2,2,128,128]{4,3,2,1,0:T(8,128)S(1)} %get-tuple-element.52.green), channel_id=1, source_target_pairs={{0,2},{1,3},{2,0},{3,1},{4,6},{5,7},{6,4},{7,5},{8,16},{9,17},{10,... | collective-permute-start | bytes 1572872 | tf_op jit(solution)/shard_map/ppermute | solution.py:40
  7.7 0.0 collective-permute-start.4
  7.7 0.5 %collective-permute-start.2 = (f32[2,2,128,128]{3,2,1,0:T(8,128)S(1)}, f32[2,2,128,128]{3,2,1,0:T(8,128)S(1)}, u32[]{:S(2)}, u32[]{:S(2)}) collective-permute-start(f32[2,2,128,128]{3,2,1,0:T(8,128)S(1)} %get-tuple-element.50.green1), channel_id=1, source_target_pairs={{0,1},{2,3},{4,5},{6,7},{1,0},{3,2},{5,4},{7,6},{8,9},{10,11},{12,... | collective-permute-start | bytes 786440 | tf_op jit(solution)/shard_map/ppermute | solution.py:27
  8.2 3.3 %shard_map.61 = (f32[6,2,128,128]{3,2,1,0:T(8,128)S(1)}, f32[6,2,128,128]{3,2,1,0:T(8,128)S(1)}) custom-call(s32[2,6]{1,0:T(2,128)S(1)} %get-tuple-element.37.neighbours, f32[2,4,6]{2,1,0:T(4,128)S(1)} %get-tuple-element.38.phonon, f32[2,6,128,128]{3,2,1,0:T(8,128)S(1)} %get-tuple-element.39.coupling, f32[2,2,128,128]{3,2,1,0:T(8,128)S(1)} %shard_map.59.green0, ...), custom_call_target="tpu_custom_call" | custom-call | flops 1000000 | bytes 10000 | tf_op jit(solution)/shard_map/pallas_call | solution.py:249
  11.5 0.0 collective-permute-done.ahead
  11.5 2.0 %collective-permute-start.1 = (f32[2,2,128,128]{3,2,1,0:T(8,128)S(1)}, f32[2,2,128,128]{3,2,1,0:T(8,128)S(1)}, u32[]{:S(2)}, u32[]{:S(2)}) collective-permute-start(f32[2,2,128,128]{3,2,1,0:T(8,128)S(1)} %collective-permute-done.ahead), channel_id=1, source_target_pairs={{0,2},{2,4},{4,6},{6,7},{1,0},{3,1},{5,3},{7,5},{8,10},{10,12},{12... | collective-permute-start | bytes 786440 | tf_op jit(solution)/shard_map/ppermute | solution.py:51
  13.5 1.4 %shard_map.62.before = f32[6,2,128,128]{3,2,1,0:T(8,128)S(1)} custom-call(s32[2,6]{1,0:T(2,128)S(1)} %get-tuple-element.37.neighbours, f32[2,4,6]{2,1,0:T(4,128)S(1)} %get-tuple-element.38.phonon, f32[2,6,128,128]{3,2,1,0:T(8,128)S(1)} %get-tuple-element.39.coupling, f32[2,2,128,128]{3,2,1,0:T(8,128)S(1)} %collective-permute-done.ahead, ...), custom_call_target="tpu_custom_call" | custom-call | flops 1000000 | bytes 10000 | tf_op jit(solution)/shard_map/pallas_call | solution.py:249
  14.9 0.7 %collective-permute-start.3 = (f32[2,2,128,128]{3,2,1,0:T(8,128)S(1)}, f32[2,2,128,128]{3,2,1,0:T(8,128)S(1)}, u32[]{:S(2)}, u32[]{:S(2)}) collective-permute-start(f32[2,2,128,128]{3,2,1,0:T(8,128)S(1)} %get-tuple-element.50.green1), channel_id=1, source_target_pairs={{1,2},{3,4},{5,6},{2,1},{4,3},{6,5},{9,10},{11,12},{13,14},{10,9},... | collective-permute-start | bytes 786440 | tf_op jit(solution)/shard_map/ppermute | solution.py:27
  15.6 1.3 %collective-permute-done.2.ahead = f32[2,2,128,128]{3,2,1,0:T(8,128)S(1)} collective-permute-done((f32[2,2,128,128]{3,2,1,0:T(8,128)S(1)}, f32[2,2,128,128]{3,2,1,0:T(8,128)S(1)}, u32[]{:S(2)}, u32[]{:S(2)}) %collective-permute-start.2) | collective-permute-done | bytes 262176 | tf_op jit(solution)/shard_map/ppermute | solution.py:27
  16.8 1.4 %shard_map.63.before = f32[6,2,128,128]{3,2,1,0:T(8,128)S(1)} custom-call(s32[2,6]{1,0:T(2,128)S(1)} %get-tuple-element.37.neighbours, f32[2,4,6]{2,1,0:T(4,128)S(1)} %get-tuple-element.38.phonon, f32[2,6,128,128]{3,2,1,0:T(8,128)S(1)} %get-tuple-element.39.coupling, f32[2,2,128,128]{3,2,1,0:T(8,128)S(1)} %collective-permute-done.2.ahead, ...), custom_call_target="tpu_custom_call" | custom-call | flops 1000000 | bytes 10000 | tf_op jit(solution)/shard_map/pallas_call | solution.py:249
  18.3 3.9 %collective-permute-done.1.across = f32[2,2,128,128]{3,2,1,0:T(8,128)S(1)} collective-permute-done((f32[2,2,128,128]{3,2,1,0:T(8,128)S(1)}, f32[2,2,128,128]{3,2,1,0:T(8,128)S(1)}, u32[]{:S(2)}, u32[]{:S(2)}) %collective-permute-start.1) | collective-permute-done | bytes 262176 | tf_op jit(solution)/shard_map/ppermute | solution.py:51
  22.2 0.7 %shard_map.64 = (f32[6,2,128,128]{3,2,1,0:T(8,128)S(1)}, f32[2,2,128,128]{3,2,1,0:T(8,128)S(1)}, f32[2,2,128,128]{3,2,1,0:T(8,128)S(1)}) custom-call(s32[2,6]{1,0:T(2,128)S(1)} %get-tuple-element.37.neighbours, f32[2,4,6]{2,1,0:T(4,128)S(1)} %get-tuple-element.38.phonon, f32[2,6,128,128]{3,2,1,0:T(8,128)S(1)} %get-tuple-element.39.coupling, ...), custom_call_target="tpu_custom_call" | custom-call | flops 1000000 | bytes 10000 | tf_op jit(solution)/shard_map/pallas_call | solution.py:249
  22.9 1.8 %collective-permute-start.6 = (f32[2,2,128,128]{3,2,1,0:T(8,128)S(1)}, f32[2,2,128,128]{3,2,1,0:T(8,128)S(1)}, u32[]{:S(2)}, u32[]{:S(2)}) collective-permute-start(f32[2,2,128,128]{3,2,1,0:T(8,128)S(1)} %get-tuple-element.56), channel_id=1, source_target_pairs={{0,2},{1,3},{2,0},{3,1},{4,6},{5,7},{6,4},{7,5},{8,16},{9,17},{10,... | collective-permute-start | bytes 786440 | tf_op jit(solution)/shard_map/ppermute | solution.py:40
  24.8 0.1 collective-permute-start.7
  24.8 0.0 collective-permute-done.5.by_cross
  24.8 0.0 collective-permute-done.4.by_core
  24.8 0.6 %shard_map.65 = (f32[2,6,2,128,128]{4,3,2,1,0:T(8,128)S(1)}, f32[2,128,128]{2,1,0:T(8,128)S(1)}) custom-call(f32[6,2,128,128]{3,2,1,0:T(8,128)S(1)} %get-tuple-element.49.total0, f32[2,2,2,128,128]{4,3,2,1,0:T(8,128)S(1)} %get-tuple-element.52.green, f32[2,2,2,128,128]{4,3,2,1,0:T(8,128)S(1)} %collective-permute-done.4.by_core, ...), custom_call_target="tpu_custom_call" | custom-call | flops 1000000 | bytes 10000 | tf_op jit(solution)/shard_map/pallas_call | solution.py:290
  25.4 0.0 collective-permute-done.3.across
  25.4 0.9 %shard_map.66 = (f32[6,2,128,128]{3,2,1,0:T(8,128)S(1)}, f32[2,2,128,128]{3,2,1,0:T(8,128)S(1)}, f32[2,2,128,128]{3,2,1,0:T(8,128)S(1)}, f32[2,128]{1,0:T(2,128)S(1)}) custom-call(s32[2,6]{1,0:T(2,128)S(1)} %get-tuple-element.37.neighbours, f32[2,4,6]{2,1,0:T(4,128)S(1)} %get-tuple-element.38.phonon, f32[2,6,128,128]{3,2,1,0:T(8,128)S(1)} %get-tuple-element.39.coupling, ...), custom_call_target="tpu_custom_call" | custom-call | flops 1000000 | bytes 10000 | tf_op jit(solution)/shard_map/pallas_call | solution.py:249
  26.3 1.3 %collective-permute-start.8 = (f32[2,2,128,128]{3,2,1,0:T(8,128)S(1)}, f32[2,2,128,128]{3,2,1,0:T(8,128)S(1)}, u32[]{:S(2)}, u32[]{:S(2)}) collective-permute-start(f32[2,2,128,128]{3,2,1,0:T(8,128)S(1)} %get-tuple-element.61), channel_id=1, source_target_pairs={{0,1},{1,0},{2,3},{3,2},{4,5},{5,4},{6,7},{7,6},{8,16},{9,17},{10,... | collective-permute-start | bytes 786440 | tf_op jit(solution)/shard_map/ppermute | solution.py:40
  27.6 0.0 collective-permute-start.9
  27.6 1.8 %collective-permute-done.6.cross0 = f32[2,2,128,128]{3,2,1,0:T(8,128)S(1)} collective-permute-done((f32[2,2,128,128]{3,2,1,0:T(8,128)S(1)}, f32[2,2,128,128]{3,2,1,0:T(8,128)S(1)}, u32[]{:S(2)}, u32[]{:S(2)}) %collective-permute-start.6) | collective-permute-done | bytes 262176 | tf_op jit(solution)/shard_map/ppermute | solution.py:40
  29.4 0.0 collective-permute-done.7.core0
  29.4 0.0 collective-permute-start.12
  29.4 1.4 %collective-permute-start.11 = (f32[2,128]{1,0:T(2,128)S(1)}, f32[2,128]{1,0:T(2,128)S(1)}, u32[]{:S(2)}, u32[]{:S(2)}) collective-permute-start(f32[2,128]{1,0:T(2,128)S(1)} %get-tuple-element.63.rest_0_), channel_id=1, source_target_pairs={{0,16},{8,24},{16,0},{24,8},{1,17},{9,25},{17,1},{25,9},{2,18},{10... | collective-permute-start | bytes 3080 | tf_op jit(solution)/shard_map/ppermute | solution.py:228
  30.8 0.4 %collective-permute-start.10 = (f32[2,128]{1,0:T(2,128)S(1)}, f32[2,128]{1,0:T(2,128)S(1)}, u32[]{:S(2)}, u32[]{:S(2)}) collective-permute-start(f32[2,128]{1,0:T(2,128)S(1)} %get-tuple-element.63.rest_0_), channel_id=1, source_target_pairs={{0,8},{8,0},{16,24},{24,16},{1,9},{9,1},{17,25},{25,17},{2,10},{10... | collective-permute-start | bytes 3080 | tf_op jit(solution)/shard_map/ppermute | solution.py:228
  31.2 1.5 %collective-permute-done.8.cross1 = f32[2,2,128,128]{3,2,1,0:T(8,128)S(1)} collective-permute-done((f32[2,2,128,128]{3,2,1,0:T(8,128)S(1)}, f32[2,2,128,128]{3,2,1,0:T(8,128)S(1)}, u32[]{:S(2)}, u32[]{:S(2)}) %collective-permute-start.8) | collective-permute-done | bytes 262176 | tf_op jit(solution)/shard_map/ppermute | solution.py:40
  32.8 0.0 collective-permute-done.9.core1
  32.8 0.0 collective-permute-done.12.rest_3_
  32.8 0.2 collective-permute-done.11.rest_2_
  33.0 0.0 collective-permute-done.10.rest_1_
  33.0 0.9 %shard_map.67 = (f32[2,2,2,128,128]{4,3,2,1,0:T(8,128)}, f32[2,128]{1,0:T(2,128)}) custom-call(f32[6,2,128,128]{3,2,1,0:T(8,128)S(1)} %get-tuple-element.49.total0, f32[6,2,128,128]{3,2,1,0:T(8,128)S(1)} %get-tuple-element.55.total1, f32[2,2,128,128]{3,2,1,0:T(8,128)S(1)} %collective-permute-done.6.cross0, ...), custom_call_target="tpu_custom_call" | custom-call | flops 1000000 | bytes 2000000 | tf_op jit(solution)/shard_map/pallas_call | solution.py:309
Async XLA Ops:
  1.6 9.9 %collective-permute-start = (f32[2,2,128,128]{3,2,1,0:T(8,128)S(1)}, f32[2,2,128,128]{3,2,1,0:T(8,128)S(1)}, u32[]{:S(2)}, u32[]{:S(2)}) collective-permute-start(f32[2,2,128,128]{3,2,1,0:T(8,128)S(1)} %shard_map.59.green0), channel_id=1, source_target_pairs={{0,1},{2,3},{4,5},{6,7},{1,0},{3,2},{5,4},{7,6},{8,9},{10,11},{12,... | collective-permute-start | bytes 786440 | tf_op jit(solution)/shard_map/ppermute | solution.py:27
  6.1 18.8 %collective-permute-start.5 = (f32[2,2,2,128,128]{4,3,2,1,0:T(8,128)S(1)}, f32[2,2,2,128,128]{4,3,2,1,0:T(8,128)S(1)}, u32[]{:S(2)}, u32[]{:S(2)}) collective-permute-start(f32[2,2,2,128,128]{4,3,2,1,0:T(8,128)S(1)} %get-tuple-element.52.green), channel_id=1, source_target_pairs={{0,2},{1,3},{2,0},{3,1},{4,6},{5,7},{6,4},{7,5},{8,16},{9,17},{10,... | collective-permute-start | bytes 1572872 | tf_op jit(solution)/shard_map/ppermute | solution.py:40
  7.7 17.1 %collective-permute-start.4 = (f32[2,2,2,128,128]{4,3,2,1,0:T(8,128)S(1)}, f32[2,2,2,128,128]{4,3,2,1,0:T(8,128)S(1)}, u32[]{:S(2)}, u32[]{:S(2)}) collective-permute-start(f32[2,2,2,128,128]{4,3,2,1,0:T(8,128)S(1)} %get-tuple-element.52.green), channel_id=1, source_target_pairs={{0,8},{16,24},{8,0},{24,16},{1,9},{17,25},{9,1},{25,17},{2,10},{18... | collective-permute-start | bytes 1572872 | tf_op jit(solution)/shard_map/ppermute | solution.py:27
  7.7 9.1 %collective-permute-start.2 = (f32[2,2,128,128]{3,2,1,0:T(8,128)S(1)}, f32[2,2,128,128]{3,2,1,0:T(8,128)S(1)}, u32[]{:S(2)}, u32[]{:S(2)}) collective-permute-start(f32[2,2,128,128]{3,2,1,0:T(8,128)S(1)} %get-tuple-element.50.green1), channel_id=1, source_target_pairs={{0,1},{2,3},{4,5},{6,7},{1,0},{3,2},{5,4},{7,6},{8,9},{10,11},{12,... | collective-permute-start | bytes 786440 | tf_op jit(solution)/shard_map/ppermute | solution.py:27
  11.5 10.6 %collective-permute-start.1 = (f32[2,2,128,128]{3,2,1,0:T(8,128)S(1)}, f32[2,2,128,128]{3,2,1,0:T(8,128)S(1)}, u32[]{:S(2)}, u32[]{:S(2)}) collective-permute-start(f32[2,2,128,128]{3,2,1,0:T(8,128)S(1)} %collective-permute-done.ahead), channel_id=1, source_target_pairs={{0,2},{2,4},{4,6},{6,7},{1,0},{3,1},{5,3},{7,5},{8,10},{10,12},{12... | collective-permute-start | bytes 786440 | tf_op jit(solution)/shard_map/ppermute | solution.py:51
  14.9 10.5 %collective-permute-start.3 = (f32[2,2,128,128]{3,2,1,0:T(8,128)S(1)}, f32[2,2,128,128]{3,2,1,0:T(8,128)S(1)}, u32[]{:S(2)}, u32[]{:S(2)}) collective-permute-start(f32[2,2,128,128]{3,2,1,0:T(8,128)S(1)} %get-tuple-element.50.green1), channel_id=1, source_target_pairs={{1,2},{3,4},{5,6},{2,1},{4,3},{6,5},{9,10},{11,12},{13,14},{10,9},... | collective-permute-start | bytes 786440 | tf_op jit(solution)/shard_map/ppermute | solution.py:27
  22.9 6.4 %collective-permute-start.6 = (f32[2,2,128,128]{3,2,1,0:T(8,128)S(1)}, f32[2,2,128,128]{3,2,1,0:T(8,128)S(1)}, u32[]{:S(2)}, u32[]{:S(2)}) collective-permute-start(f32[2,2,128,128]{3,2,1,0:T(8,128)S(1)} %get-tuple-element.56), channel_id=1, source_target_pairs={{0,2},{1,3},{2,0},{3,1},{4,6},{5,7},{6,4},{7,5},{8,16},{9,17},{10,... | collective-permute-start | bytes 786440 | tf_op jit(solution)/shard_map/ppermute | solution.py:40
  24.8 4.6 %collective-permute-start.7 = (f32[2,2,128,128]{3,2,1,0:T(8,128)S(1)}, f32[2,2,128,128]{3,2,1,0:T(8,128)S(1)}, u32[]{:S(2)}, u32[]{:S(2)}) collective-permute-start(f32[2,2,128,128]{3,2,1,0:T(8,128)S(1)} %get-tuple-element.57), channel_id=1, source_target_pairs={{0,8},{16,24},{8,0},{24,16},{1,9},{17,25},{9,1},{25,17},{2,10},{18... | collective-permute-start | bytes 786440 | tf_op jit(solution)/shard_map/ppermute | solution.py:27
  26.3 6.4 %collective-permute-start.8 = (f32[2,2,128,128]{3,2,1,0:T(8,128)S(1)}, f32[2,2,128,128]{3,2,1,0:T(8,128)S(1)}, u32[]{:S(2)}, u32[]{:S(2)}) collective-permute-start(f32[2,2,128,128]{3,2,1,0:T(8,128)S(1)} %get-tuple-element.61), channel_id=1, source_target_pairs={{0,1},{1,0},{2,3},{3,2},{4,5},{5,4},{6,7},{7,6},{8,16},{9,17},{10,... | collective-permute-start | bytes 786440 | tf_op jit(solution)/shard_map/ppermute | solution.py:40
  27.6 5.2 %collective-permute-start.9 = (f32[2,2,128,128]{3,2,1,0:T(8,128)S(1)}, f32[2,2,128,128]{3,2,1,0:T(8,128)S(1)}, u32[]{:S(2)}, u32[]{:S(2)}) collective-permute-start(f32[2,2,128,128]{3,2,1,0:T(8,128)S(1)} %get-tuple-element.62), channel_id=1, source_target_pairs={{0,8},{16,24},{8,0},{24,16},{1,9},{17,25},{9,1},{25,17},{2,10},{18... | collective-permute-start | bytes 786440 | tf_op jit(solution)/shard_map/ppermute | solution.py:27
  29.4 3.4 %collective-permute-start.12 = (f32[2,128]{1,0:T(2,128)S(1)}, f32[2,128]{1,0:T(2,128)S(1)}, u32[]{:S(2)}, u32[]{:S(2)}) collective-permute-start(f32[2,128]{1,0:T(2,128)S(1)} %get-tuple-element.63.rest_0_), channel_id=1, source_target_pairs={{0,24},{8,16},{16,8},{24,0},{1,25},{9,17},{17,9},{25,1},{2,26},{10... | collective-permute-start | bytes 3080 | tf_op jit(solution)/shard_map/ppermute | solution.py:228
  29.4 3.6 %collective-permute-start.11 = (f32[2,128]{1,0:T(2,128)S(1)}, f32[2,128]{1,0:T(2,128)S(1)}, u32[]{:S(2)}, u32[]{:S(2)}) collective-permute-start(f32[2,128]{1,0:T(2,128)S(1)} %get-tuple-element.63.rest_0_), channel_id=1, source_target_pairs={{0,16},{8,24},{16,0},{24,8},{1,17},{9,25},{17,1},{25,9},{2,18},{10... | collective-permute-start | bytes 3080 | tf_op jit(solution)/shard_map/ppermute | solution.py:228
  30.8 2.2 %collective-permute-start.10 = (f32[2,128]{1,0:T(2,128)S(1)}, f32[2,128]{1,0:T(2,128)S(1)}, u32[]{:S(2)}, u32[]{:S(2)}) collective-permute-start(f32[2,128]{1,0:T(2,128)S(1)} %get-tuple-element.63.rest_0_), channel_id=1, source_target_pairs={{0,8},{8,0},{16,24},{24,16},{1,9},{9,1},{17,25},{25,17},{2,10},{10... | collective-permute-start | bytes 3080 | tf_op jit(solution)/shard_map/ppermute | solution.py:228

commit v7 on v6

--- a/solution.py
+++ b/solution.py
@@ -40,8 +40,15 @@
     return lax.ppermute(x, ("energy", "atom"), perm)
 
 
-def cross_swap(x, step):
-    return exchange(x, lambda e, a: (e + 1 if e % 2 else e - 1, a), lambda e, a: (e, a ^ step))
+def cross_swap(x, low_step, high_step):
+    half = lax.axis_size("atom") // 2
+    if half % 4:
+        low_step = high_step = 1
+
+    def spare(e, a):
+        return e, a ^ (low_step if a < half else high_step)
+
+    return exchange(x, lambda e, a: (e + 1 if e % 2 else e - 1, a), spare)
 
 
 def forward(x, axis):
@@ -276,7 +283,7 @@
     green1, green, coupling, phonon, neighbours = fetch(fetch_kernel, [part, *sources], sources)
     ahead1 = swap(green1, "atom", 0)
     ahead0 = swap(green0, "atom", 0)
-    by_core, by_cross = swap(green, "energy", 0), cross_swap(green, 2)
+    by_core, by_cross = swap(green, "energy", 0), cross_swap(green, 2, 2)
     total0, total1 = call(own_kernel, [spread] * 2, (green0, green1), parts=2)
     ahead0, total0, total1 = lax.optimization_barrier((ahead0, total0, total1))
     across0 = forward(ahead0, "atom")
@@ -286,7 +293,7 @@
     (total1,) = call(pair_kernel, [spread], (ahead1, total1))
     total0, total1 = lax.optimization_barrier((total0, total1))
     total0, core0, cross0 = call(far_kernel, [spread, edge, edge], (across0, total0))
-    core0, cross0 = swap(core0, "energy", 0), cross_swap(cross0, 2)
+    core0, cross0 = swap(core0, "energy", 0), cross_swap(cross0, 2, 2)
     turned, partial = pl.pallas_call(
         functools.partial(turn_kernel, energies),
         out_shape=[
@@ -303,7 +310,7 @@
         [spread, edge, edge, (a_local, orb)],
         (across1, total1, turned, partial),
     )
-    core1, cross1 = swap(core1, "energy", 0), cross_swap(cross1, 1)
+    core1, cross1 = swap(core1, "energy", 0), cross_swap(cross1, 2, 1)
     cross0, core0, rate = lax.optimization_barrier((cross0, core0, rate))
     rates = addends(rate, "energy")
     return pl.pallas_call(

time: 34.1 us -> 34.1 us (level)
    ppermute x3, starting transfers between devices: 4.76 us -> 3.92 us  [exchange(): return lax.ppermute(x, ('energy', 'atom'), perm)]
    ppermute x6, starting transfers between devices: 4.31 us -> 5.03 us  [swap(): lax.ppermute(x, axis, [(i, i + 1) for i in low] + [(i + 1, i) for i in low])]
where the time goes in v7:
time: 34.1 us; the launch traced here: 33.9 us
  starting transfers between devices  12.8 us (38%)
  Pallas kernels  11.6 us (34%)
  waiting for transfers between devices  8.77 us (26%)
  between operations  0.72 us (2%)
    pallas_call x5, Pallas kernels, call(): pl.pallas_call(kernel, out_shape=[jax.ShapeDtypeStruct(shape, jnp.float32...  7.74 us
    ppermute x6, starting transfers between devices, swap(): lax.ppermute(x, axis, [(i, i + 1) for i in low] + [(i + 1, i) for i in low])  5.03 us
    ppermute x3, starting transfers between devices, exchange(): return lax.ppermute(x, ('energy', 'atom'), perm)  3.92 us
    ppermute x1, waiting for transfers between devices, forward(): return lax.ppermute(x, axis, [(i, j) for i, j in ups + downs if i != j])  3.9 us
    ppermute x3, waiting for transfers between devices, exchange(): return lax.ppermute(x, ('energy', 'atom'), perm)  3.4 us
    pallas_call x2, Pallas kernels, fetch(): pl.pallas_call(kernel, out_shape=[jax.ShapeDtypeStruct(x.shape, x.dtype)...  2.38 us
    ppermute x1, starting transfers between devices, forward(): return lax.ppermute(x, axis, [(i, j) for i, j in ups + downs if i != j])  1.96 us
    ppermute x3, starting transfers between devices, addends(): return [x] + [lax.ppermute(x, axis, turn) for turn in turns]  1.86 us
  transfers between devices with their start and end apart: 13, of which 5 were waited for; matrix products, arithmetic and copies ran while one was open for 0% of the time, Pallas kernels for 29%

profile of v7, /device:TPU:0, one launch (start us, length us, event | category | flops | bytes accessed | tf_op | source)
XLA Modules:
  0.0 33.9 jit_solution(13363958639234037635)
XLA Ops:
  0.6 1.0 %shard_map.59.green0 = f32[2,2,128,128]{3,2,1,0:T(8,128)S(1)} custom-call(f32[2,2,2,128,128]{4,3,2,1,0:T(8,128)} %green.2), custom_call_target="tpu_custom_call" | custom-call | tf_op jit(solution)/shard_map/pallas_call | solution.py:270
  1.6 3.0 %collective-permute-start = (f32[2,2,128,128]{3,2,1,0:T(8,128)S(1)}, f32[2,2,128,128]{3,2,1,0:T(8,128)S(1)}, u32[]{:S(2)}, u32[]{:S(2)}) collective-permute-start(f32[2,2,128,128]{3,2,1,0:T(8,128)S(1)} %shard_map.59.green0), channel_id=1, source_target_pairs={{0,1},{2,3},{4,5},{6,7},{1,0},{3,2},{5,4},{7,6},{8,9},{10,11},{12,... | collective-permute-start | bytes 786440 | tf_op jit(solution)/shard_map/ppermute | solution.py:27
  4.6 1.4 %shard_map.60 = (f32[2,2,128,128]{3,2,1,0:T(8,128)S(1)}, f32[2,2,2,128,128]{4,3,2,1,0:T(8,128)S(1)}, f32[2,6,128,128]{3,2,1,0:T(8,128)S(1)}, f32[2,4,6]{2,1,0:T(4,128)S(1)}, s32[2,6]{1,0:T(2,128)S(1)}) custom-call(f32[2,2,2,128,128]{4,3,2,1,0:T(8,128)} %green.2, f32[2,6,128,128]{3,2,1,0:T(8,128)} %coupling, f32[2,4,6]{2,1,0:T(4,128)} %bitcast.1, s32[2,6]{1,0:T(2,128)} %neighbours), custom_call_target="tpu_custom_call" | custom-call | tf_op jit(solution)/shard_map/pallas_call | solution.py:270
  6.1 1.6 %collective-permute-start.5 = (f32[2,2,2,128,128]{4,3,2,1,0:T(8,128)S(1)}, f32[2,2,2,128,128]{4,3,2,1,0:T(8,128)S(1)}, u32[]{:S(2)}, u32[]{:S(2)}) collective-permute-start(f32[2,2,2,128,128]{4,3,2,1,0:T(8,128)S(1)} %get-tuple-element.52.green), channel_id=1, source_target_pairs={{0,2},{1,3},{2,0},{3,1},{4,6},{5,7},{6,4},{7,5},{8,16},{9,17},{10,... | collective-permute-start | bytes 1572872 | tf_op jit(solution)/shard_map/ppermute | solution.py:40
  7.7 0.0 collective-permute-start.4
  7.7 0.5 %collective-permute-start.2 = (f32[2,2,128,128]{3,2,1,0:T(8,128)S(1)}, f32[2,2,128,128]{3,2,1,0:T(8,128)S(1)}, u32[]{:S(2)}, u32[]{:S(2)}) collective-permute-start(f32[2,2,128,128]{3,2,1,0:T(8,128)S(1)} %get-tuple-element.50.green1), channel_id=1, source_target_pairs={{0,1},{2,3},{4,5},{6,7},{1,0},{3,2},{5,4},{7,6},{8,9},{10,11},{12,... | collective-permute-start | bytes 786440 | tf_op jit(solution)/shard_map/ppermute | solution.py:27
  8.2 3.3 %shard_map.61 = (f32[6,2,128,128]{3,2,1,0:T(8,128)S(1)}, f32[6,2,128,128]{3,2,1,0:T(8,128)S(1)}) custom-call(s32[2,6]{1,0:T(2,128)S(1)} %get-tuple-element.37.neighbours, f32[2,4,6]{2,1,0:T(4,128)S(1)} %get-tuple-element.38.phonon, f32[2,6,128,128]{3,2,1,0:T(8,128)S(1)} %get-tuple-element.39.coupling, f32[2,2,128,128]{3,2,1,0:T(8,128)S(1)} %shard_map.59.green0, ...), custom_call_target="tpu_custom_call" | custom-call | flops 1000000 | bytes 10000 | tf_op jit(solution)/shard_map/pallas_call | solution.py:256
  11.5 0.0 collective-permute-done.ahead
  11.5 2.0 %collective-permute-start.1 = (f32[2,2,128,128]{3,2,1,0:T(8,128)S(1)}, f32[2,2,128,128]{3,2,1,0:T(8,128)S(1)}, u32[]{:S(2)}, u32[]{:S(2)}) collective-permute-start(f32[2,2,128,128]{3,2,1,0:T(8,128)S(1)} %collective-permute-done.ahead), channel_id=1, source_target_pairs={{0,2},{2,4},{4,6},{6,7},{1,0},{3,1},{5,3},{7,5},{8,10},{10,12},{12... | collective-permute-start | bytes 786440 | tf_op jit(solution)/shard_map/ppermute | solution.py:58
  13.5 1.4 %shard_map.62.before = f32[6,2,128,128]{3,2,1,0:T(8,128)S(1)} custom-call(s32[2,6]{1,0:T(2,128)S(1)} %get-tuple-element.37.neighbours, f32[2,4,6]{2,1,0:T(4,128)S(1)} %get-tuple-element.38.phonon, f32[2,6,128,128]{3,2,1,0:T(8,128)S(1)} %get-tuple-element.39.coupling, f32[2,2,128,128]{3,2,1,0:T(8,128)S(1)} %collective-permute-done.ahead, ...), custom_call_target="tpu_custom_call" | custom-call | flops 1000000 | bytes 10000 | tf_op jit(solution)/shard_map/pallas_call | solution.py:256
  14.9 0.7 %collective-permute-start.3 = (f32[2,2,128,128]{3,2,1,0:T(8,128)S(1)}, f32[2,2,128,128]{3,2,1,0:T(8,128)S(1)}, u32[]{:S(2)}, u32[]{:S(2)}) collective-permute-start(f32[2,2,128,128]{3,2,1,0:T(8,128)S(1)} %get-tuple-element.50.green1), channel_id=1, source_target_pairs={{1,2},{3,4},{5,6},{2,1},{4,3},{6,5},{9,10},{11,12},{13,14},{10,9},... | collective-permute-start | bytes 786440 | tf_op jit(solution)/shard_map/ppermute | solution.py:27
  15.6 1.3 %collective-permute-done.2.ahead = f32[2,2,128,128]{3,2,1,0:T(8,128)S(1)} collective-permute-done((f32[2,2,128,128]{3,2,1,0:T(8,128)S(1)}, f32[2,2,128,128]{3,2,1,0:T(8,128)S(1)}, u32[]{:S(2)}, u32[]{:S(2)}) %collective-permute-start.2) | collective-permute-done | bytes 262176 | tf_op jit(solution)/shard_map/ppermute | solution.py:27
  16.8 1.4 %shard_map.63.before = f32[6,2,128,128]{3,2,1,0:T(8,128)S(1)} custom-call(s32[2,6]{1,0:T(2,128)S(1)} %get-tuple-element.37.neighbours, f32[2,4,6]{2,1,0:T(4,128)S(1)} %get-tuple-element.38.phonon, f32[2,6,128,128]{3,2,1,0:T(8,128)S(1)} %get-tuple-element.39.coupling, f32[2,2,128,128]{3,2,1,0:T(8,128)S(1)} %collective-permute-done.2.ahead, ...), custom_call_target="tpu_custom_call" | custom-call | flops 1000000 | bytes 10000 | tf_op jit(solution)/shard_map/pallas_call | solution.py:256
  18.3 3.9 %collective-permute-done.1.across = f32[2,2,128,128]{3,2,1,0:T(8,128)S(1)} collective-permute-done((f32[2,2,128,128]{3,2,1,0:T(8,128)S(1)}, f32[2,2,128,128]{3,2,1,0:T(8,128)S(1)}, u32[]{:S(2)}, u32[]{:S(2)}) %collective-permute-start.1) | collective-permute-done | bytes 262176 | tf_op jit(solution)/shard_map/ppermute | solution.py:58
  22.2 0.7 %shard_map.64 = (f32[6,2,128,128]{3,2,1,0:T(8,128)S(1)}, f32[2,2,128,128]{3,2,1,0:T(8,128)S(1)}, f32[2,2,128,128]{3,2,1,0:T(8,128)S(1)}) custom-call(s32[2,6]{1,0:T(2,128)S(1)} %get-tuple-element.37.neighbours, f32[2,4,6]{2,1,0:T(4,128)S(1)} %get-tuple-element.38.phonon, f32[2,6,128,128]{3,2,1,0:T(8,128)S(1)} %get-tuple-element.39.coupling, ...), custom_call_target="tpu_custom_call" | custom-call | flops 1000000 | bytes 10000 | tf_op jit(solution)/shard_map/pallas_call | solution.py:256
  22.9 1.1 %collective-permute-start.6 = (f32[2,2,128,128]{3,2,1,0:T(8,128)S(1)}, f32[2,2,128,128]{3,2,1,0:T(8,128)S(1)}, u32[]{:S(2)}, u32[]{:S(2)}) collective-permute-start(f32[2,2,128,128]{3,2,1,0:T(8,128)S(1)} %get-tuple-element.56), channel_id=1, source_target_pairs={{0,2},{1,3},{2,0},{3,1},{4,6},{5,7},{6,4},{7,5},{8,16},{9,17},{10,... | collective-permute-start | bytes 786440 | tf_op jit(solution)/shard_map/ppermute | solution.py:40
  24.0 0.8 %collective-permute-start.7 = (f32[2,2,128,128]{3,2,1,0:T(8,128)S(1)}, f32[2,2,128,128]{3,2,1,0:T(8,128)S(1)}, u32[]{:S(2)}, u32[]{:S(2)}) collective-permute-start(f32[2,2,128,128]{3,2,1,0:T(8,128)S(1)} %get-tuple-element.57), channel_id=1, source_target_pairs={{0,8},{16,24},{8,0},{24,16},{1,9},{17,25},{9,1},{25,17},{2,10},{18... | collective-permute-start | bytes 786440 | tf_op jit(solution)/shard_map/ppermute | solution.py:27
  24.8 0.0 collective-permute-done.5.by_cross
  24.8 0.0 collective-permute-done.4.by_core
  24.8 0.6 %shard_map.65 = (f32[2,6,2,128,128]{4,3,2,1,0:T(8,128)S(1)}, f32[2,128,128]{2,1,0:T(8,128)S(1)}) custom-call(f32[6,2,128,128]{3,2,1,0:T(8,128)S(1)} %get-tuple-element.49.total0, f32[2,2,2,128,128]{4,3,2,1,0:T(8,128)S(1)} %get-tuple-element.52.green, f32[2,2,2,128,128]{4,3,2,1,0:T(8,128)S(1)} %collective-permute-done.4.by_core, ...), custom_call_target="tpu_custom_call" | custom-call | flops 1000000 | bytes 10000 | tf_op jit(solution)/shard_map/pallas_call | solution.py:297
  25.4 0.0 collective-permute-done.3.across
  25.4 0.9 %shard_map.66 = (f32[6,2,128,128]{3,2,1,0:T(8,128)S(1)}, f32[2,2,128,128]{3,2,1,0:T(8,128)S(1)}, f32[2,2,128,128]{3,2,1,0:T(8,128)S(1)}, f32[2,128]{1,0:T(2,128)S(1)}) custom-call(s32[2,6]{1,0:T(2,128)S(1)} %get-tuple-element.37.neighbours, f32[2,4,6]{2,1,0:T(4,128)S(1)} %get-tuple-element.38.phonon, f32[2,6,128,128]{3,2,1,0:T(8,128)S(1)} %get-tuple-element.39.coupling, ...), custom_call_target="tpu_custom_call" | custom-call | flops 1000000 | bytes 10000 | tf_op jit(solution)/shard_map/pallas_call | solution.py:256
  26.3 1.2 %collective-permute-start.8 = (f32[2,2,128,128]{3,2,1,0:T(8,128)S(1)}, f32[2,2,128,128]{3,2,1,0:T(8,128)S(1)}, u32[]{:S(2)}, u32[]{:S(2)}) collective-permute-start(f32[2,2,128,128]{3,2,1,0:T(8,128)S(1)} %get-tuple-element.61), channel_id=1, source_target_pairs={{0,2},{1,3},{2,0},{3,1},{4,5},{5,4},{6,7},{7,6},{8,16},{9,17},{10,... | collective-permute-start | bytes 786440 | tf_op jit(solution)/shard_map/ppermute | solution.py:40
  27.5 0.0 collective-permute-start.9
  27.5 1.9 %collective-permute-done.6.cross0 = f32[2,2,128,128]{3,2,1,0:T(8,128)S(1)} collective-permute-done((f32[2,2,128,128]{3,2,1,0:T(8,128)S(1)}, f32[2,2,128,128]{3,2,1,0:T(8,128)S(1)}, u32[]{:S(2)}, u32[]{:S(2)}) %collective-permute-start.6) | collective-permute-done | bytes 262176 | tf_op jit(solution)/shard_map/ppermute | solution.py:40
  29.4 0.0 collective-permute-done.7.core0
  29.4 0.0 collective-permute-start.12
  29.4 1.4 %collective-permute-start.11 = (f32[2,128]{1,0:T(2,128)S(1)}, f32[2,128]{1,0:T(2,128)S(1)}, u32[]{:S(2)}, u32[]{:S(2)}) collective-permute-start(f32[2,128]{1,0:T(2,128)S(1)} %get-tuple-element.63.rest_0_), channel_id=1, source_target_pairs={{0,16},{8,24},{16,0},{24,8},{1,17},{9,25},{17,1},{25,9},{2,18},{10... | collective-permute-start | bytes 3080 | tf_op jit(solution)/shard_map/ppermute | solution.py:235
  30.8 0.4 %collective-permute-start.10 = (f32[2,128]{1,0:T(2,128)S(1)}, f32[2,128]{1,0:T(2,128)S(1)}, u32[]{:S(2)}, u32[]{:S(2)}) collective-permute-start(f32[2,128]{1,0:T(2,128)S(1)} %get-tuple-element.63.rest_0_), channel_id=1, source_target_pairs={{0,8},{8,0},{16,24},{24,16},{1,9},{9,1},{17,25},{25,17},{2,10},{10... | collective-permute-start | bytes 3080 | tf_op jit(solution)/shard_map/ppermute | solution.py:235
  31.2 1.5 %collective-permute-done.8.cross1 = f32[2,2,128,128]{3,2,1,0:T(8,128)S(1)} collective-permute-done((f32[2,2,128,128]{3,2,1,0:T(8,128)S(1)}, f32[2,2,128,128]{3,2,1,0:T(8,128)S(1)}, u32[]{:S(2)}, u32[]{:S(2)}) %collective-permute-start.8) | collective-permute-done | bytes 262176 | tf_op jit(solution)/shard_map/ppermute | solution.py:40
  32.8 0.0 collective-permute-done.9.core1
  32.8 0.0 collective-permute-done.12.rest_3_
  32.8 0.2 collective-permute-done.11.rest_2_
  33.0 0.0 collective-permute-done.10.rest_1_
  33.0 0.9 %shard_map.67 = (f32[2,2,2,128,128]{4,3,2,1,0:T(8,128)}, f32[2,128]{1,0:T(2,128)}) custom-call(f32[6,2,128,128]{3,2,1,0:T(8,128)S(1)} %get-tuple-element.49.total0, f32[6,2,128,128]{3,2,1,0:T(8,128)S(1)} %get-tuple-element.55.total1, f32[2,2,128,128]{3,2,1,0:T(8,128)S(1)} %collective-permute-done.6.cross0, ...), custom_call_target="tpu_custom_call" | custom-call | flops 1000000 | bytes 2000000 | tf_op jit(solution)/shard_map/pallas_call | solution.py:316
Async XLA Ops:
  1.6 9.9 %collective-permute-start = (f32[2,2,128,128]{3,2,1,0:T(8,128)S(1)}, f32[2,2,128,128]{3,2,1,0:T(8,128)S(1)}, u32[]{:S(2)}, u32[]{:S(2)}) collective-permute-start(f32[2,2,128,128]{3,2,1,0:T(8,128)S(1)} %shard_map.59.green0), channel_id=1, source_target_pairs={{0,1},{2,3},{4,5},{6,7},{1,0},{3,2},{5,4},{7,6},{8,9},{10,11},{12,... | collective-permute-start | bytes 786440 | tf_op jit(solution)/shard_map/ppermute | solution.py:27
  6.1 18.8 %collective-permute-start.5 = (f32[2,2,2,128,128]{4,3,2,1,0:T(8,128)S(1)}, f32[2,2,2,128,128]{4,3,2,1,0:T(8,128)S(1)}, u32[]{:S(2)}, u32[]{:S(2)}) collective-permute-start(f32[2,2,2,128,128]{4,3,2,1,0:T(8,128)S(1)} %get-tuple-element.52.green), channel_id=1, source_target_pairs={{0,2},{1,3},{2,0},{3,1},{4,6},{5,7},{6,4},{7,5},{8,16},{9,17},{10,... | collective-permute-start | bytes 1572872 | tf_op jit(solution)/shard_map/ppermute | solution.py:40
  7.7 17.1 %collective-permute-start.4 = (f32[2,2,2,128,128]{4,3,2,1,0:T(8,128)S(1)}, f32[2,2,2,128,128]{4,3,2,1,0:T(8,128)S(1)}, u32[]{:S(2)}, u32[]{:S(2)}) collective-permute-start(f32[2,2,2,128,128]{4,3,2,1,0:T(8,128)S(1)} %get-tuple-element.52.green), channel_id=1, source_target_pairs={{0,8},{16,24},{8,0},{24,16},{1,9},{17,25},{9,1},{25,17},{2,10},{18... | collective-permute-start | bytes 1572872 | tf_op jit(solution)/shard_map/ppermute | solution.py:27
  7.7 9.1 %collective-permute-start.2 = (f32[2,2,128,128]{3,2,1,0:T(8,128)S(1)}, f32[2,2,128,128]{3,2,1,0:T(8,128)S(1)}, u32[]{:S(2)}, u32[]{:S(2)}) collective-permute-start(f32[2,2,128,128]{3,2,1,0:T(8,128)S(1)} %get-tuple-element.50.green1), channel_id=1, source_target_pairs={{0,1},{2,3},{4,5},{6,7},{1,0},{3,2},{5,4},{7,6},{8,9},{10,11},{12,... | collective-permute-start | bytes 786440 | tf_op jit(solution)/shard_map/ppermute | solution.py:27
  11.5 10.6 %collective-permute-start.1 = (f32[2,2,128,128]{3,2,1,0:T(8,128)S(1)}, f32[2,2,128,128]{3,2,1,0:T(8,128)S(1)}, u32[]{:S(2)}, u32[]{:S(2)}) collective-permute-start(f32[2,2,128,128]{3,2,1,0:T(8,128)S(1)} %collective-permute-done.ahead), channel_id=1, source_target_pairs={{0,2},{2,4},{4,6},{6,7},{1,0},{3,1},{5,3},{7,5},{8,10},{10,12},{12... | collective-permute-start | bytes 786440 | tf_op jit(solution)/shard_map/ppermute | solution.py:58
  14.9 10.5 %collective-permute-start.3 = (f32[2,2,128,128]{3,2,1,0:T(8,128)S(1)}, f32[2,2,128,128]{3,2,1,0:T(8,128)S(1)}, u32[]{:S(2)}, u32[]{:S(2)}) collective-permute-start(f32[2,2,128,128]{3,2,1,0:T(8,128)S(1)} %get-tuple-element.50.green1), channel_id=1, source_target_pairs={{1,2},{3,4},{5,6},{2,1},{4,3},{6,5},{9,10},{11,12},{13,14},{10,9},... | collective-permute-start | bytes 786440 | tf_op jit(solution)/shard_map/ppermute | solution.py:27
  22.9 6.4 %collective-permute-start.6 = (f32[2,2,128,128]{3,2,1,0:T(8,128)S(1)}, f32[2,2,128,128]{3,2,1,0:T(8,128)S(1)}, u32[]{:S(2)}, u32[]{:S(2)}) collective-permute-start(f32[2,2,128,128]{3,2,1,0:T(8,128)S(1)} %get-tuple-element.56), channel_id=1, source_target_pairs={{0,2},{1,3},{2,0},{3,1},{4,6},{5,7},{6,4},{7,5},{8,16},{9,17},{10,... | collective-permute-start | bytes 786440 | tf_op jit(solution)/shard_map/ppermute | solution.py:40
  24.0 5.3 %collective-permute-start.7 = (f32[2,2,128,128]{3,2,1,0:T(8,128)S(1)}, f32[2,2,128,128]{3,2,1,0:T(8,128)S(1)}, u32[]{:S(2)}, u32[]{:S(2)}) collective-permute-start(f32[2,2,128,128]{3,2,1,0:T(8,128)S(1)} %get-tuple-element.57), channel_id=1, source_target_pairs={{0,8},{16,24},{8,0},{24,16},{1,9},{17,25},{9,1},{25,17},{2,10},{18... | collective-permute-start | bytes 786440 | tf_op jit(solution)/shard_map/ppermute | solution.py:27
  26.3 6.4 %collective-permute-start.8 = (f32[2,2,128,128]{3,2,1,0:T(8,128)S(1)}, f32[2,2,128,128]{3,2,1,0:T(8,128)S(1)}, u32[]{:S(2)}, u32[]{:S(2)}) collective-permute-start(f32[2,2,128,128]{3,2,1,0:T(8,128)S(1)} %get-tuple-element.61), channel_id=1, source_target_pairs={{0,2},{1,3},{2,0},{3,1},{4,5},{5,4},{6,7},{7,6},{8,16},{9,17},{10,... | collective-permute-start | bytes 786440 | tf_op jit(solution)/shard_map/ppermute | solution.py:40
  27.5 5.3 %collective-permute-start.9 = (f32[2,2,128,128]{3,2,1,0:T(8,128)S(1)}, f32[2,2,128,128]{3,2,1,0:T(8,128)S(1)}, u32[]{:S(2)}, u32[]{:S(2)}) collective-permute-start(f32[2,2,128,128]{3,2,1,0:T(8,128)S(1)} %get-tuple-element.62), channel_id=1, source_target_pairs={{0,8},{16,24},{8,0},{24,16},{1,9},{17,25},{9,1},{25,17},{2,10},{18... | collective-permute-start | bytes 786440 | tf_op jit(solution)/shard_map/ppermute | solution.py:27
  29.4 3.4 %collective-permute-start.12 = (f32[2,128]{1,0:T(2,128)S(1)}, f32[2,128]{1,0:T(2,128)S(1)}, u32[]{:S(2)}, u32[]{:S(2)}) collective-permute-start(f32[2,128]{1,0:T(2,128)S(1)} %get-tuple-element.63.rest_0_), channel_id=1, source_target_pairs={{0,24},{8,16},{16,8},{24,0},{1,25},{9,17},{17,9},{25,1},{2,26},{10... | collective-permute-start | bytes 3080 | tf_op jit(solution)/shard_map/ppermute | solution.py:235
  29.4 3.6 %collective-permute-start.11 = (f32[2,128]{1,0:T(2,128)S(1)}, f32[2,128]{1,0:T(2,128)S(1)}, u32[]{:S(2)}, u32[]{:S(2)}) collective-permute-start(f32[2,128]{1,0:T(2,128)S(1)} %get-tuple-element.63.rest_0_), channel_id=1, source_target_pairs={{0,16},{8,24},{16,0},{24,8},{1,17},{9,25},{17,1},{25,9},{2,18},{10... | collective-permute-start | bytes 3080 | tf_op jit(solution)/shard_map/ppermute | solution.py:235
  30.8 2.2 %collective-permute-start.10 = (f32[2,128]{1,0:T(2,128)S(1)}, f32[2,128]{1,0:T(2,128)S(1)}, u32[]{:S(2)}, u32[]{:S(2)}) collective-permute-start(f32[2,128]{1,0:T(2,128)S(1)} %get-tuple-element.63.rest_0_), channel_id=1, source_target_pairs={{0,8},{8,0},{16,24},{24,16},{1,9},{9,1},{17,25},{25,17},{2,10},{10... | collective-permute-start | bytes 3080 | tf_op jit(solution)/shard_map/ppermute | solution.py:235

commit v8 on v7

--- a/solution.py
+++ b/solution.py
@@ -311,7 +311,7 @@
         (across1, total1, turned, partial),
     )
     core1, cross1 = swap(core1, "energy", 0), cross_swap(cross1, 2, 1)
-    cross0, core0, rate = lax.optimization_barrier((cross0, core0, rate))
+    core0, cross0, rate = lax.optimization_barrier((core0, cross0, rate))
     rates = addends(rate, "energy")
     return pl.pallas_call(
         functools.partial(end_kernel, energies),

time: 34.1 us -> 35 us (1.026)
  starting transfers between devices: 12.8 us -> 13.4 us
    ppermute x3, starting transfers between devices: 3.92 us -> 5.24 us  [exchange(): return lax.ppermute(x, ('energy', 'atom'), perm)]
    ppermute x3, waiting for transfers between devices: 0.21 us -> 1.46 us  [addends(): return [x] + [lax.ppermute(x, axis, turn) for turn in turns]]
    ppermute x3, waiting for transfers between devices: 3.4 us -> 2.45 us  [exchange(): return lax.ppermute(x, ('energy', 'atom'), perm)]
    ppermute x6, starting transfers between devices: 5.03 us -> 4.32 us  [swap(): lax.ppermute(x, axis, [(i, i + 1) for i in low] + [(i + 1, i) for i in low])]
  transfers between devices with their start and end apart: 13 -> 13, of which waited for: 5 -> 5; matrix products, arithmetic and copies ran while one was open for 0% -> 0% of each run, Pallas kernels for 29% -> 28%
where the time goes in v8:
time: 35 us; the launch traced here: 34.8 us
  starting transfers between devices  13.4 us (38%)
  Pallas kernels  11.6 us (33%)
  waiting for transfers between devices  9.08 us (26%)
  between operations  0.73 us (2%)
    pallas_call x5, Pallas kernels, call(): pl.pallas_call(kernel, out_shape=[jax.ShapeDtypeStruct(shape, jnp.float32...  7.74 us
    ppermute x3, starting transfers between devices, exchange(): return lax.ppermute(x, ('energy', 'atom'), perm)  5.24 us
    ppermute x6, starting transfers between devices, swap(): lax.ppermute(x, axis, [(i, i + 1) for i in low] + [(i + 1, i) for i in low])  4.32 us
    ppermute x1, waiting for transfers between devices, forward(): return lax.ppermute(x, axis, [(i, j) for i, j in ups + downs if i != j])  3.9 us
    ppermute x3, waiting for transfers between devices, exchange(): return lax.ppermute(x, ('energy', 'atom'), perm)  2.45 us
    pallas_call x2, Pallas kernels, fetch(): pl.pallas_call(kernel, out_shape=[jax.ShapeDtypeStruct(x.shape, x.dtype)...  2.38 us
    ppermute x1, starting transfers between devices, forward(): return lax.ppermute(x, axis, [(i, j) for i, j in ups + downs if i != j])  1.96 us
    ppermute x3, starting transfers between devices, addends(): return [x] + [lax.ppermute(x, axis, turn) for turn in turns]  1.89 us
  transfers between devices with their start and end apart: 13, of which 5 were waited for; matrix products, arithmetic and copies ran while one was open for 0% of the time, Pallas kernels for 28%

profile of v8, /device:TPU:0, one launch (start us, length us, event | category | flops | bytes accessed | tf_op | source)
XLA Modules:
  0.0 34.8 jit_solution(12378108457214355949)
XLA Ops:
  0.6 1.0 %shard_map.59.green0 = f32[2,2,128,128]{3,2,1,0:T(8,128)S(1)} custom-call(f32[2,2,2,128,128]{4,3,2,1,0:T(8,128)} %green.2), custom_call_target="tpu_custom_call" | custom-call | tf_op jit(solution)/shard_map/pallas_call | solution.py:270
  1.6 3.0 %collective-permute-start = (f32[2,2,128,128]{3,2,1,0:T(8,128)S(1)}, f32[2,2,128,128]{3,2,1,0:T(8,128)S(1)}, u32[]{:S(2)}, u32[]{:S(2)}) collective-permute-start(f32[2,2,128,128]{3,2,1,0:T(8,128)S(1)} %shard_map.59.green0), channel_id=1, source_target_pairs={{0,1},{2,3},{4,5},{6,7},{1,0},{3,2},{5,4},{7,6},{8,9},{10,11},{12,... | collective-permute-start | bytes 786440 | tf_op jit(solution)/shard_map/ppermute | solution.py:27
  4.6 1.4 %shard_map.60 = (f32[2,2,128,128]{3,2,1,0:T(8,128)S(1)}, f32[2,2,2,128,128]{4,3,2,1,0:T(8,128)S(1)}, f32[2,6,128,128]{3,2,1,0:T(8,128)S(1)}, f32[2,4,6]{2,1,0:T(4,128)S(1)}, s32[2,6]{1,0:T(2,128)S(1)}) custom-call(f32[2,2,2,128,128]{4,3,2,1,0:T(8,128)} %green.2, f32[2,6,128,128]{3,2,1,0:T(8,128)} %coupling, f32[2,4,6]{2,1,0:T(4,128)} %bitcast.1, s32[2,6]{1,0:T(2,128)} %neighbours), custom_call_target="tpu_custom_call" | custom-call | tf_op jit(solution)/shard_map/pallas_call | solution.py:270
  6.1 1.6 %collective-permute-start.5 = (f32[2,2,2,128,128]{4,3,2,1,0:T(8,128)S(1)}, f32[2,2,2,128,128]{4,3,2,1,0:T(8,128)S(1)}, u32[]{:S(2)}, u32[]{:S(2)}) collective-permute-start(f32[2,2,2,128,128]{4,3,2,1,0:T(8,128)S(1)} %get-tuple-element.52.green), channel_id=1, source_target_pairs={{0,2},{1,3},{2,0},{3,1},{4,6},{5,7},{6,4},{7,5},{8,16},{9,17},{10,... | collective-permute-start | bytes 1572872 | tf_op jit(solution)/shard_map/ppermute | solution.py:40
  7.7 0.0 collective-permute-start.4
  7.7 0.5 %collective-permute-start.2 = (f32[2,2,128,128]{3,2,1,0:T(8,128)S(1)}, f32[2,2,128,128]{3,2,1,0:T(8,128)S(1)}, u32[]{:S(2)}, u32[]{:S(2)}) collective-permute-start(f32[2,2,128,128]{3,2,1,0:T(8,128)S(1)} %get-tuple-element.50.green1), channel_id=1, source_target_pairs={{0,1},{2,3},{4,5},{6,7},{1,0},{3,2},{5,4},{7,6},{8,9},{10,11},{12,... | collective-permute-start | bytes 786440 | tf_op jit(solution)/shard_map/ppermute | solution.py:27
  8.2 3.3 %shard_map.61 = (f32[6,2,128,128]{3,2,1,0:T(8,128)S(1)}, f32[6,2,128,128]{3,2,1,0:T(8,128)S(1)}) custom-call(s32[2,6]{1,0:T(2,128)S(1)} %get-tuple-element.37.neighbours, f32[2,4,6]{2,1,0:T(4,128)S(1)} %get-tuple-element.38.phonon, f32[2,6,128,128]{3,2,1,0:T(8,128)S(1)} %get-tuple-element.39.coupling, f32[2,2,128,128]{3,2,1,0:T(8,128)S(1)} %shard_map.59.green0, ...), custom_call_target="tpu_custom_call" | custom-call | flops 1000000 | bytes 10000 | tf_op jit(solution)/shard_map/pallas_call | solution.py:256
  11.5 0.0 collective-permute-done.ahead
  11.5 2.0 %collective-permute-start.1 = (f32[2,2,128,128]{3,2,1,0:T(8,128)S(1)}, f32[2,2,128,128]{3,2,1,0:T(8,128)S(1)}, u32[]{:S(2)}, u32[]{:S(2)}) collective-permute-start(f32[2,2,128,128]{3,2,1,0:T(8,128)S(1)} %collective-permute-done.ahead), channel_id=1, source_target_pairs={{0,2},{2,4},{4,6},{6,7},{1,0},{3,1},{5,3},{7,5},{8,10},{10,12},{12... | collective-permute-start | bytes 786440 | tf_op jit(solution)/shard_map/ppermute | solution.py:58
  13.5 1.4 %shard_map.62.before = f32[6,2,128,128]{3,2,1,0:T(8,128)S(1)} custom-call(s32[2,6]{1,0:T(2,128)S(1)} %get-tuple-element.37.neighbours, f32[2,4,6]{2,1,0:T(4,128)S(1)} %get-tuple-element.38.phonon, f32[2,6,128,128]{3,2,1,0:T(8,128)S(1)} %get-tuple-element.39.coupling, f32[2,2,128,128]{3,2,1,0:T(8,128)S(1)} %collective-permute-done.ahead, ...), custom_call_target="tpu_custom_call" | custom-call | flops 1000000 | bytes 10000 | tf_op jit(solution)/shard_map/pallas_call | solution.py:256
  14.9 0.7 %collective-permute-start.3 = (f32[2,2,128,128]{3,2,1,0:T(8,128)S(1)}, f32[2,2,128,128]{3,2,1,0:T(8,128)S(1)}, u32[]{:S(2)}, u32[]{:S(2)}) collective-permute-start(f32[2,2,128,128]{3,2,1,0:T(8,128)S(1)} %get-tuple-element.50.green1), channel_id=1, source_target_pairs={{1,2},{3,4},{5,6},{2,1},{4,3},{6,5},{9,10},{11,12},{13,14},{10,9},... | collective-permute-start | bytes 786440 | tf_op jit(solution)/shard_map/ppermute | solution.py:27
  15.6 1.3 %collective-permute-done.2.ahead = f32[2,2,128,128]{3,2,1,0:T(8,128)S(1)} collective-permute-done((f32[2,2,128,128]{3,2,1,0:T(8,128)S(1)}, f32[2,2,128,128]{3,2,1,0:T(8,128)S(1)}, u32[]{:S(2)}, u32[]{:S(2)}) %collective-permute-start.2) | collective-permute-done | bytes 262176 | tf_op jit(solution)/shard_map/ppermute | solution.py:27
  16.8 1.4 %shard_map.63.before = f32[6,2,128,128]{3,2,1,0:T(8,128)S(1)} custom-call(s32[2,6]{1,0:T(2,128)S(1)} %get-tuple-element.37.neighbours, f32[2,4,6]{2,1,0:T(4,128)S(1)} %get-tuple-element.38.phonon, f32[2,6,128,128]{3,2,1,0:T(8,128)S(1)} %get-tuple-element.39.coupling, f32[2,2,128,128]{3,2,1,0:T(8,128)S(1)} %collective-permute-done.2.ahead, ...), custom_call_target="tpu_custom_call" | custom-call | flops 1000000 | bytes 10000 | tf_op jit(solution)/shard_map/pallas_call | solution.py:256
  18.3 3.9 %collective-permute-done.1.across = f32[2,2,128,128]{3,2,1,0:T(8,128)S(1)} collective-permute-done((f32[2,2,128,128]{3,2,1,0:T(8,128)S(1)}, f32[2,2,128,128]{3,2,1,0:T(8,128)S(1)}, u32[]{:S(2)}, u32[]{:S(2)}) %collective-permute-start.1) | collective-permute-done | bytes 262176 | tf_op jit(solution)/shard_map/ppermute | solution.py:58
  22.2 0.7 %shard_map.64 = (f32[6,2,128,128]{3,2,1,0:T(8,128)S(1)}, f32[2,2,128,128]{3,2,1,0:T(8,128)S(1)}, f32[2,2,128,128]{3,2,1,0:T(8,128)S(1)}) custom-call(s32[2,6]{1,0:T(2,128)S(1)} %get-tuple-element.37.neighbours, f32[2,4,6]{2,1,0:T(4,128)S(1)} %get-tuple-element.38.phonon, f32[2,6,128,128]{3,2,1,0:T(8,128)S(1)} %get-tuple-element.39.coupling, ...), custom_call_target="tpu_custom_call" | custom-call | flops 1000000 | bytes 10000 | tf_op jit(solution)/shard_map/pallas_call | solution.py:256
  22.9 0.1 collective-permute-start.6
  23.0 1.1 %collective-permute-start.7 = (f32[2,2,128,128]{3,2,1,0:T(8,128)S(1)}, f32[2,2,128,128]{3,2,1,0:T(8,128)S(1)}, u32[]{:S(2)}, u32[]{:S(2)}) collective-permute-start(f32[2,2,128,128]{3,2,1,0:T(8,128)S(1)} %get-tuple-element.57), channel_id=1, source_target_pairs={{0,2},{1,3},{2,0},{3,1},{4,6},{5,7},{6,4},{7,5},{8,16},{9,17},{10,... | collective-permute-start | bytes 786440 | tf_op jit(solution)/shard_map/ppermute | solution.py:40
  24.1 0.0 collective-permute-done.5.by_cross
  24.1 0.0 collective-permute-done.4.by_core
  24.1 0.6 %shard_map.65 = (f32[2,6,2,128,128]{4,3,2,1,0:T(8,128)S(1)}, f32[2,128,128]{2,1,0:T(8,128)S(1)}) custom-call(f32[6,2,128,128]{3,2,1,0:T(8,128)S(1)} %get-tuple-element.49.total0, f32[2,2,2,128,128]{4,3,2,1,0:T(8,128)S(1)} %get-tuple-element.52.green, f32[2,2,2,128,128]{4,3,2,1,0:T(8,128)S(1)} %collective-permute-done.4.by_core, ...), custom_call_target="tpu_custom_call" | custom-call | flops 1000000 | bytes 10000 | tf_op jit(solution)/shard_map/pallas_call | solution.py:297
  24.7 0.0 collective-permute-done.3.across
  24.7 0.9 %shard_map.66 = (f32[6,2,128,128]{3,2,1,0:T(8,128)S(1)}, f32[2,2,128,128]{3,2,1,0:T(8,128)S(1)}, f32[2,2,128,128]{3,2,1,0:T(8,128)S(1)}, f32[2,128]{1,0:T(2,128)S(1)}) custom-call(s32[2,6]{1,0:T(2,128)S(1)} %get-tuple-element.37.neighbours, f32[2,4,6]{2,1,0:T(4,128)S(1)} %get-tuple-element.38.phonon, f32[2,6,128,128]{3,2,1,0:T(8,128)S(1)} %get-tuple-element.39.coupling, ...), custom_call_target="tpu_custom_call" | custom-call | flops 1000000 | bytes 10000 | tf_op jit(solution)/shard_map/pallas_call | solution.py:256
  25.6 2.5 %collective-permute-start.8 = (f32[2,2,128,128]{3,2,1,0:T(8,128)S(1)}, f32[2,2,128,128]{3,2,1,0:T(8,128)S(1)}, u32[]{:S(2)}, u32[]{:S(2)}) collective-permute-start(f32[2,2,128,128]{3,2,1,0:T(8,128)S(1)} %get-tuple-element.61), channel_id=1, source_target_pairs={{0,2},{1,3},{2,0},{3,1},{4,5},{5,4},{6,7},{7,6},{8,16},{9,17},{10,... | collective-permute-start | bytes 786440 | tf_op jit(solution)/shard_map/ppermute | solution.py:40
  28.1 0.0 collective-permute-start.9
  28.1 0.0 collective-permute-done.6.core0
  28.1 1.3 %collective-permute-done.7.cross0 = f32[2,2,128,128]{3,2,1,0:T(8,128)S(1)} collective-permute-done((f32[2,2,128,128]{3,2,1,0:T(8,128)S(1)}, f32[2,2,128,128]{3,2,1,0:T(8,128)S(1)}, u32[]{:S(2)}, u32[]{:S(2)}) %collective-permute-start.7) | collective-permute-done | bytes 262176 | tf_op jit(solution)/shard_map/ppermute | solution.py:40
  29.4 0.9 %collective-permute-start.12 = (f32[2,128]{1,0:T(2,128)S(1)}, f32[2,128]{1,0:T(2,128)S(1)}, u32[]{:S(2)}, u32[]{:S(2)}) collective-permute-start(f32[2,128]{1,0:T(2,128)S(1)} %get-tuple-element.63.rest_0_), channel_id=1, source_target_pairs={{0,24},{8,16},{16,8},{24,0},{1,25},{9,17},{17,9},{25,1},{2,26},{10... | collective-permute-start | bytes 3080 | tf_op jit(solution)/shard_map/ppermute | solution.py:235
  30.3 0.9 %collective-permute-start.11 = (f32[2,128]{1,0:T(2,128)S(1)}, f32[2,128]{1,0:T(2,128)S(1)}, u32[]{:S(2)}, u32[]{:S(2)}) collective-permute-start(f32[2,128]{1,0:T(2,128)S(1)} %get-tuple-element.63.rest_0_), channel_id=1, source_target_pairs={{0,16},{8,24},{16,0},{24,8},{1,17},{9,25},{17,1},{25,9},{2,18},{10... | collective-permute-start | bytes 3080 | tf_op jit(solution)/shard_map/ppermute | solution.py:235
  31.2 0.1 collective-permute-start.10
  31.3 1.1 %collective-permute-done.8.cross1 = f32[2,2,128,128]{3,2,1,0:T(8,128)S(1)} collective-permute-done((f32[2,2,128,128]{3,2,1,0:T(8,128)S(1)}, f32[2,2,128,128]{3,2,1,0:T(8,128)S(1)}, u32[]{:S(2)}, u32[]{:S(2)}) %collective-permute-start.8) | collective-permute-done | bytes 262176 | tf_op jit(solution)/shard_map/ppermute | solution.py:40
  32.5 0.0 collective-permute-done.9.core1
  32.5 0.0 collective-permute-done.12.rest_3_
  32.5 1.5 %collective-permute-done.11.rest_2_ = f32[2,128]{1,0:T(2,128)S(1)} collective-permute-done((f32[2,128]{1,0:T(2,128)S(1)}, f32[2,128]{1,0:T(2,128)S(1)}, u32[]{:S(2)}, u32[]{:S(2)}) %collective-permute-start.11) | collective-permute-done | bytes 1056 | tf_op jit(solution)/shard_map/ppermute | solution.py:235
  33.9 0.0 collective-permute-done.10.rest_1_
  33.9 0.9 %shard_map.67 = (f32[2,2,2,128,128]{4,3,2,1,0:T(8,128)}, f32[2,128]{1,0:T(2,128)}) custom-call(f32[6,2,128,128]{3,2,1,0:T(8,128)S(1)} %get-tuple-element.49.total0, f32[6,2,128,128]{3,2,1,0:T(8,128)S(1)} %get-tuple-element.55.total1, f32[2,2,128,128]{3,2,1,0:T(8,128)S(1)} %collective-permute-done.7.cross0, ...), custom_call_target="tpu_custom_call" | custom-call | flops 1000000 | bytes 2000000 | tf_op jit(solution)/shard_map/pallas_call | solution.py:316
Async XLA Ops:
  1.6 9.9 %collective-permute-start = (f32[2,2,128,128]{3,2,1,0:T(8,128)S(1)}, f32[2,2,128,128]{3,2,1,0:T(8,128)S(1)}, u32[]{:S(2)}, u32[]{:S(2)}) collective-permute-start(f32[2,2,128,128]{3,2,1,0:T(8,128)S(1)} %shard_map.59.green0), channel_id=1, source_target_pairs={{0,1},{2,3},{4,5},{6,7},{1,0},{3,2},{5,4},{7,6},{8,9},{10,11},{12,... | collective-permute-start | bytes 786440 | tf_op jit(solution)/shard_map/ppermute | solution.py:27
  6.1 18.1 %collective-permute-start.5 = (f32[2,2,2,128,128]{4,3,2,1,0:T(8,128)S(1)}, f32[2,2,2,128,128]{4,3,2,1,0:T(8,128)S(1)}, u32[]{:S(2)}, u32[]{:S(2)}) collective-permute-start(f32[2,2,2,128,128]{4,3,2,1,0:T(8,128)S(1)} %get-tuple-element.52.green), channel_id=1, source_target_pairs={{0,2},{1,3},{2,0},{3,1},{4,6},{5,7},{6,4},{7,5},{8,16},{9,17},{10,... | collective-permute-start | bytes 1572872 | tf_op jit(solution)/shard_map/ppermute | solution.py:40
  7.7 16.4 %collective-permute-start.4 = (f32[2,2,2,128,128]{4,3,2,1,0:T(8,128)S(1)}, f32[2,2,2,128,128]{4,3,2,1,0:T(8,128)S(1)}, u32[]{:S(2)}, u32[]{:S(2)}) collective-permute-start(f32[2,2,2,128,128]{4,3,2,1,0:T(8,128)S(1)} %get-tuple-element.52.green), channel_id=1, source_target_pairs={{0,8},{16,24},{8,0},{24,16},{1,9},{17,25},{9,1},{25,17},{2,10},{18... | collective-permute-start | bytes 1572872 | tf_op jit(solution)/shard_map/ppermute | solution.py:27
  7.7 9.1 %collective-permute-start.2 = (f32[2,2,128,128]{3,2,1,0:T(8,128)S(1)}, f32[2,2,128,128]{3,2,1,0:T(8,128)S(1)}, u32[]{:S(2)}, u32[]{:S(2)}) collective-permute-start(f32[2,2,128,128]{3,2,1,0:T(8,128)S(1)} %get-tuple-element.50.green1), channel_id=1, source_target_pairs={{0,1},{2,3},{4,5},{6,7},{1,0},{3,2},{5,4},{7,6},{8,9},{10,11},{12,... | collective-permute-start | bytes 786440 | tf_op jit(solution)/shard_map/ppermute | solution.py:27
  11.5 10.6 %collective-permute-start.1 = (f32[2,2,128,128]{3,2,1,0:T(8,128)S(1)}, f32[2,2,128,128]{3,2,1,0:T(8,128)S(1)}, u32[]{:S(2)}, u32[]{:S(2)}) collective-permute-start(f32[2,2,128,128]{3,2,1,0:T(8,128)S(1)} %collective-permute-done.ahead), channel_id=1, source_target_pairs={{0,2},{2,4},{4,6},{6,7},{1,0},{3,1},{5,3},{7,5},{8,10},{10,12},{12... | collective-permute-start | bytes 786440 | tf_op jit(solution)/shard_map/ppermute | solution.py:58
  14.9 9.8 %collective-permute-start.3 = (f32[2,2,128,128]{3,2,1,0:T(8,128)S(1)}, f32[2,2,128,128]{3,2,1,0:T(8,128)S(1)}, u32[]{:S(2)}, u32[]{:S(2)}) collective-permute-start(f32[2,2,128,128]{3,2,1,0:T(8,128)S(1)} %get-tuple-element.50.green1), channel_id=1, source_target_pairs={{1,2},{3,4},{5,6},{2,1},{4,3},{6,5},{9,10},{11,12},{13,14},{10,9},... | collective-permute-start | bytes 786440 | tf_op jit(solution)/shard_map/ppermute | solution.py:27
  22.9 5.2 %collective-permute-start.6 = (f32[2,2,128,128]{3,2,1,0:T(8,128)S(1)}, f32[2,2,128,128]{3,2,1,0:T(8,128)S(1)}, u32[]{:S(2)}, u32[]{:S(2)}) collective-permute-start(f32[2,2,128,128]{3,2,1,0:T(8,128)S(1)} %get-tuple-element.56), channel_id=1, source_target_pairs={{0,8},{16,24},{8,0},{24,16},{1,9},{17,25},{9,1},{25,17},{2,10},{18... | collective-permute-start | bytes 786440 | tf_op jit(solution)/shard_map/ppermute | solution.py:27
  23.0 6.4 %collective-permute-start.7 = (f32[2,2,128,128]{3,2,1,0:T(8,128)S(1)}, f32[2,2,128,128]{3,2,1,0:T(8,128)S(1)}, u32[]{:S(2)}, u32[]{:S(2)}) collective-permute-start(f32[2,2,128,128]{3,2,1,0:T(8,128)S(1)} %get-tuple-element.57), channel_id=1, source_target_pairs={{0,2},{1,3},{2,0},{3,1},{4,6},{5,7},{6,4},{7,5},{8,16},{9,17},{10,... | collective-permute-start | bytes 786440 | tf_op jit(solution)/shard_map/ppermute | solution.py:40
  25.6 6.8 %collective-permute-start.8 = (f32[2,2,128,128]{3,2,1,0:T(8,128)S(1)}, f32[2,2,128,128]{3,2,1,0:T(8,128)S(1)}, u32[]{:S(2)}, u32[]{:S(2)}) collective-permute-start(f32[2,2,128,128]{3,2,1,0:T(8,128)S(1)} %get-tuple-element.61), channel_id=1, source_target_pairs={{0,2},{1,3},{2,0},{3,1},{4,5},{5,4},{6,7},{7,6},{8,16},{9,17},{10,... | collective-permute-start | bytes 786440 | tf_op jit(solution)/shard_map/ppermute | solution.py:40
  28.1 4.4 %collective-permute-start.9 = (f32[2,2,128,128]{3,2,1,0:T(8,128)S(1)}, f32[2,2,128,128]{3,2,1,0:T(8,128)S(1)}, u32[]{:S(2)}, u32[]{:S(2)}) collective-permute-start(f32[2,2,128,128]{3,2,1,0:T(8,128)S(1)} %get-tuple-element.62), channel_id=1, source_target_pairs={{0,8},{16,24},{8,0},{24,16},{1,9},{17,25},{9,1},{25,17},{2,10},{18... | collective-permute-start | bytes 786440 | tf_op jit(solution)/shard_map/ppermute | solution.py:27
  29.4 3.0 %collective-permute-start.12 = (f32[2,128]{1,0:T(2,128)S(1)}, f32[2,128]{1,0:T(2,128)S(1)}, u32[]{:S(2)}, u32[]{:S(2)}) collective-permute-start(f32[2,128]{1,0:T(2,128)S(1)} %get-tuple-element.63.rest_0_), channel_id=1, source_target_pairs={{0,24},{8,16},{16,8},{24,0},{1,25},{9,17},{17,9},{25,1},{2,26},{10... | collective-permute-start | bytes 3080 | tf_op jit(solution)/shard_map/ppermute | solution.py:235
  30.3 3.6 %collective-permute-start.11 = (f32[2,128]{1,0:T(2,128)S(1)}, f32[2,128]{1,0:T(2,128)S(1)}, u32[]{:S(2)}, u32[]{:S(2)}) collective-permute-start(f32[2,128]{1,0:T(2,128)S(1)} %get-tuple-element.63.rest_0_), channel_id=1, source_target_pairs={{0,16},{8,24},{16,0},{24,8},{1,17},{9,25},{17,1},{25,9},{2,18},{10... | collective-permute-start | bytes 3080 | tf_op jit(solution)/shard_map/ppermute | solution.py:235
  31.2 2.7 %collective-permute-start.10 = (f32[2,128]{1,0:T(2,128)S(1)}, f32[2,128]{1,0:T(2,128)S(1)}, u32[]{:S(2)}, u32[]{:S(2)}) collective-permute-start(f32[2,128]{1,0:T(2,128)S(1)} %get-tuple-element.63.rest_0_), channel_id=1, source_target_pairs={{0,8},{8,0},{16,24},{24,16},{1,9},{9,1},{17,25},{25,17},{2,10},{10... | collective-permute-start | bytes 3080 | tf_op jit(solution)/shard_map/ppermute | solution.py:235

commit v9 on v6

--- a/solution.py
+++ b/solution.py
@@ -229,13 +229,18 @@
 
 
 def end_kernel(size, total0, total1, cross0, core0, cross1, core1, *rest):
-    *rates, out, rate = rest
+    *rates, out, rate, work, sems = rest
     e_local = out.shape[1]
     has_core, has_cross = has_partners(size)
+    copies = []
     for c, (total, cross, core) in enumerate(((total0, cross0, core0), (total1, cross1, core1))):
         for e in range(e_local):
-            out[c, e] = total[REACH + e] + core[e] * has_core + cross[e] * has_cross
+            work[c, e] = total[REACH + e] + core[e] * has_core + cross[e] * has_cross
+        copies.append(pltpu.make_async_copy(work.at[c], out.at[c], sems.at[c]))
+        copies[-1].start()
     rate[...] = sum(r[...] for r in rates)
+    for copy in copies:
+        copy.wait()
 
 
 def per_device(green, coupling, phonon, neighbours):
@@ -313,7 +318,11 @@
             jax.ShapeDtypeStruct((a_local, orb), jnp.float32),
         ],
         in_specs=[VMEM] * (6 + len(rates)),
-        out_specs=[VMEM] * 2,
+        out_specs=[ANY, VMEM],
+        scratch_shapes=[
+            pltpu.VMEM(green.shape, jnp.float32),
+            pltpu.SemaphoreType.DMA((2,)),
+        ],
         compiler_params=pltpu.CompilerParams(vmem_limit_bytes=24 * 2**20),
         cost_estimate=pl.CostEstimate(flops=10**6, bytes_accessed=2 * 10**6, transcendentals=0),
     )(total0, total1, cross0, core0, cross1, core1, *rates)

time: 34.1 us -> 34.7 us (1.018)
  starting transfers between devices: 12.9 us -> 14.1 us
  waiting for transfers between devices: 8.66 us -> 7.66 us
  Pallas kernels: 11.6 us -> 12.2 us
    ppermute x3, waiting for transfers between devices: 3.29 us -> 2.48 us  [exchange(): return lax.ppermute(x, ('energy', 'atom'), perm)]
    ppermute x6, starting transfers between devices: 4.31 us -> 5.03 us  [swap(): lax.ppermute(x, axis, [(i, i + 1) for i in low] + [(i + 1, i) for i in low])]
    pallas_call x1, Pallas kernels: 0.92 us -> 1.45 us  [per_device(): pl.pallas_call(functools.partial(end_kernel, energies), out_shape=[jax.Sh...]
    ppermute x3, starting transfers between devices: 4.76 us -> 5.2 us  [exchange(): return lax.ppermute(x, ('energy', 'atom'), perm)]
  transfers between devices with their start and end apart: 13 -> 13, of which waited for: 5 -> 4; matrix products, arithmetic and copies ran while one was open for 0% -> 0% of each run, Pallas kernels for 29% -> 28%
where the time goes in v9:
time: 34.7 us; the launch traced here: 34.6 us
  starting transfers between devices  14.1 us (41%)
  Pallas kernels  12.2 us (35%)
  waiting for transfers between devices  7.66 us (22%)
  between operations  0.73 us (2%)
    pallas_call x5, Pallas kernels, call(): pl.pallas_call(kernel, out_shape=[jax.ShapeDtypeStruct(shape, jnp.float32...  7.74 us
    ppermute x3, starting transfers between devices, exchange(): return lax.ppermute(x, ('energy', 'atom'), perm)  5.2 us
    ppermute x6, starting transfers between devices, swap(): lax.ppermute(x, axis, [(i, i + 1) for i in low] + [(i + 1, i) for i in low])  5.03 us
    ppermute x1, waiting for transfers between devices, forward(): return lax.ppermute(x, axis, [(i, j) for i, j in ups + downs if i != j])  3.9 us
    ppermute x3, waiting for transfers between devices, exchange(): return lax.ppermute(x, ('energy', 'atom'), perm)  2.48 us
    pallas_call x2, Pallas kernels, fetch(): pl.pallas_call(kernel, out_shape=[jax.ShapeDtypeStruct(x.shape, x.dtype)...  2.38 us
    ppermute x1, starting transfers between devices, forward(): return lax.ppermute(x, axis, [(i, j) for i, j in ups + downs if i != j])  1.96 us
    ppermute x3, starting transfers between devices, addends(): return [x] + [lax.ppermute(x, axis, turn) for turn in turns]  1.86 us
  transfers between devices with their start and end apart: 13, of which 4 were waited for; matrix products, arithmetic and copies ran while one was open for 0% of the time, Pallas kernels for 28%

profile of v9, /device:TPU:0, one launch (start us, length us, event | category | flops | bytes accessed | tf_op | source)
XLA Modules:
  0.0 34.6 jit_solution(5703169799090324188)
XLA Ops:
  0.6 1.0 %shard_map.59.green0 = f32[2,2,128,128]{3,2,1,0:T(8,128)S(1)} custom-call(f32[2,2,2,128,128]{4,3,2,1,0:T(8,128)} %green.2), custom_call_target="tpu_custom_call" | custom-call | tf_op jit(solution)/shard_map/pallas_call | solution.py:268
  1.6 3.0 %collective-permute-start = (f32[2,2,128,128]{3,2,1,0:T(8,128)S(1)}, f32[2,2,128,128]{3,2,1,0:T(8,128)S(1)}, u32[]{:S(2)}, u32[]{:S(2)}) collective-permute-start(f32[2,2,128,128]{3,2,1,0:T(8,128)S(1)} %shard_map.59.green0), channel_id=1, source_target_pairs={{0,1},{2,3},{4,5},{6,7},{1,0},{3,2},{5,4},{7,6},{8,9},{10,11},{12,... | collective-permute-start | bytes 786440 | tf_op jit(solution)/shard_map/ppermute | solution.py:27
  4.6 1.4 %shard_map.60 = (f32[2,2,128,128]{3,2,1,0:T(8,128)S(1)}, f32[2,2,2,128,128]{4,3,2,1,0:T(8,128)S(1)}, f32[2,6,128,128]{3,2,1,0:T(8,128)S(1)}, f32[2,4,6]{2,1,0:T(4,128)S(1)}, s32[2,6]{1,0:T(2,128)S(1)}) custom-call(f32[2,2,2,128,128]{4,3,2,1,0:T(8,128)} %green.2, f32[2,6,128,128]{3,2,1,0:T(8,128)} %coupling, f32[2,4,6]{2,1,0:T(4,128)} %bitcast.1, s32[2,6]{1,0:T(2,128)} %neighbours), custom_call_target="tpu_custom_call" | custom-call | tf_op jit(solution)/shard_map/pallas_call | solution.py:268
  6.1 1.6 %collective-permute-start.5 = (f32[2,2,2,128,128]{4,3,2,1,0:T(8,128)S(1)}, f32[2,2,2,128,128]{4,3,2,1,0:T(8,128)S(1)}, u32[]{:S(2)}, u32[]{:S(2)}) collective-permute-start(f32[2,2,2,128,128]{4,3,2,1,0:T(8,128)S(1)} %get-tuple-element.52.green), channel_id=1, source_target_pairs={{0,2},{1,3},{2,0},{3,1},{4,6},{5,7},{6,4},{7,5},{8,16},{9,17},{10,... | collective-permute-start | bytes 1572872 | tf_op jit(solution)/shard_map/ppermute | solution.py:40
  7.7 0.0 collective-permute-start.4
  7.7 0.5 %collective-permute-start.2 = (f32[2,2,128,128]{3,2,1,0:T(8,128)S(1)}, f32[2,2,128,128]{3,2,1,0:T(8,128)S(1)}, u32[]{:S(2)}, u32[]{:S(2)}) collective-permute-start(f32[2,2,128,128]{3,2,1,0:T(8,128)S(1)} %get-tuple-element.50.green1), channel_id=1, source_target_pairs={{0,1},{2,3},{4,5},{6,7},{1,0},{3,2},{5,4},{7,6},{8,9},{10,11},{12,... | collective-permute-start | bytes 786440 | tf_op jit(solution)/shard_map/ppermute | solution.py:27
  8.2 3.3 %shard_map.61 = (f32[6,2,128,128]{3,2,1,0:T(8,128)S(1)}, f32[6,2,128,128]{3,2,1,0:T(8,128)S(1)}) custom-call(s32[2,6]{1,0:T(2,128)S(1)} %get-tuple-element.37.neighbours, f32[2,4,6]{2,1,0:T(4,128)S(1)} %get-tuple-element.38.phonon, f32[2,6,128,128]{3,2,1,0:T(8,128)S(1)} %get-tuple-element.39.coupling, f32[2,2,128,128]{3,2,1,0:T(8,128)S(1)} %shard_map.59.green0, ...), custom_call_target="tpu_custom_call" | custom-call | flops 1000000 | bytes 10000 | tf_op jit(solution)/shard_map/pallas_call | solution.py:254
  11.5 0.0 collective-permute-done.ahead
  11.5 2.0 %collective-permute-start.1 = (f32[2,2,128,128]{3,2,1,0:T(8,128)S(1)}, f32[2,2,128,128]{3,2,1,0:T(8,128)S(1)}, u32[]{:S(2)}, u32[]{:S(2)}) collective-permute-start(f32[2,2,128,128]{3,2,1,0:T(8,128)S(1)} %collective-permute-done.ahead), channel_id=1, source_target_pairs={{0,2},{2,4},{4,6},{6,7},{1,0},{3,1},{5,3},{7,5},{8,10},{10,12},{12... | collective-permute-start | bytes 786440 | tf_op jit(solution)/shard_map/ppermute | solution.py:51
  13.5 1.4 %shard_map.62.before = f32[6,2,128,128]{3,2,1,0:T(8,128)S(1)} custom-call(s32[2,6]{1,0:T(2,128)S(1)} %get-tuple-element.37.neighbours, f32[2,4,6]{2,1,0:T(4,128)S(1)} %get-tuple-element.38.phonon, f32[2,6,128,128]{3,2,1,0:T(8,128)S(1)} %get-tuple-element.39.coupling, f32[2,2,128,128]{3,2,1,0:T(8,128)S(1)} %collective-permute-done.ahead, ...), custom_call_target="tpu_custom_call" | custom-call | flops 1000000 | bytes 10000 | tf_op jit(solution)/shard_map/pallas_call | solution.py:254
  14.9 0.7 %collective-permute-start.3 = (f32[2,2,128,128]{3,2,1,0:T(8,128)S(1)}, f32[2,2,128,128]{3,2,1,0:T(8,128)S(1)}, u32[]{:S(2)}, u32[]{:S(2)}) collective-permute-start(f32[2,2,128,128]{3,2,1,0:T(8,128)S(1)} %get-tuple-element.50.green1), channel_id=1, source_target_pairs={{1,2},{3,4},{5,6},{2,1},{4,3},{6,5},{9,10},{11,12},{13,14},{10,9},... | collective-permute-start | bytes 786440 | tf_op jit(solution)/shard_map/ppermute | solution.py:27
  15.6 1.3 %collective-permute-done.2.ahead = f32[2,2,128,128]{3,2,1,0:T(8,128)S(1)} collective-permute-done((f32[2,2,128,128]{3,2,1,0:T(8,128)S(1)}, f32[2,2,128,128]{3,2,1,0:T(8,128)S(1)}, u32[]{:S(2)}, u32[]{:S(2)}) %collective-permute-start.2) | collective-permute-done | bytes 262176 | tf_op jit(solution)/shard_map/ppermute | solution.py:27
  16.8 1.4 %shard_map.63.before = f32[6,2,128,128]{3,2,1,0:T(8,128)S(1)} custom-call(s32[2,6]{1,0:T(2,128)S(1)} %get-tuple-element.37.neighbours, f32[2,4,6]{2,1,0:T(4,128)S(1)} %get-tuple-element.38.phonon, f32[2,6,128,128]{3,2,1,0:T(8,128)S(1)} %get-tuple-element.39.coupling, f32[2,2,128,128]{3,2,1,0:T(8,128)S(1)} %collective-permute-done.2.ahead, ...), custom_call_target="tpu_custom_call" | custom-call | flops 1000000 | bytes 10000 | tf_op jit(solution)/shard_map/pallas_call | solution.py:254
  18.3 3.9 %collective-permute-done.1.across = f32[2,2,128,128]{3,2,1,0:T(8,128)S(1)} collective-permute-done((f32[2,2,128,128]{3,2,1,0:T(8,128)S(1)}, f32[2,2,128,128]{3,2,1,0:T(8,128)S(1)}, u32[]{:S(2)}, u32[]{:S(2)}) %collective-permute-start.1) | collective-permute-done | bytes 262176 | tf_op jit(solution)/shard_map/ppermute | solution.py:51
  22.2 0.7 %shard_map.64 = (f32[6,2,128,128]{3,2,1,0:T(8,128)S(1)}, f32[2,2,128,128]{3,2,1,0:T(8,128)S(1)}, f32[2,2,128,128]{3,2,1,0:T(8,128)S(1)}) custom-call(s32[2,6]{1,0:T(2,128)S(1)} %get-tuple-element.37.neighbours, f32[2,4,6]{2,1,0:T(4,128)S(1)} %get-tuple-element.38.phonon, f32[2,6,128,128]{3,2,1,0:T(8,128)S(1)} %get-tuple-element.39.coupling, ...), custom_call_target="tpu_custom_call" | custom-call | flops 1000000 | bytes 10000 | tf_op jit(solution)/shard_map/pallas_call | solution.py:254
  22.9 1.1 %collective-permute-start.6 = (f32[2,2,128,128]{3,2,1,0:T(8,128)S(1)}, f32[2,2,128,128]{3,2,1,0:T(8,128)S(1)}, u32[]{:S(2)}, u32[]{:S(2)}) collective-permute-start(f32[2,2,128,128]{3,2,1,0:T(8,128)S(1)} %get-tuple-element.56), channel_id=1, source_target_pairs={{0,2},{1,3},{2,0},{3,1},{4,6},{5,7},{6,4},{7,5},{8,16},{9,17},{10,... | collective-permute-start | bytes 786440 | tf_op jit(solution)/shard_map/ppermute | solution.py:40
  24.0 0.8 %collective-permute-start.7 = (f32[2,2,128,128]{3,2,1,0:T(8,128)S(1)}, f32[2,2,128,128]{3,2,1,0:T(8,128)S(1)}, u32[]{:S(2)}, u32[]{:S(2)}) collective-permute-start(f32[2,2,128,128]{3,2,1,0:T(8,128)S(1)} %get-tuple-element.57), channel_id=1, source_target_pairs={{0,8},{16,24},{8,0},{24,16},{1,9},{17,25},{9,1},{25,17},{2,10},{18... | collective-permute-start | bytes 786440 | tf_op jit(solution)/shard_map/ppermute | solution.py:27
  24.8 0.0 collective-permute-done.5.by_cross
  24.8 0.0 collective-permute-done.4.by_core
  24.8 0.6 %shard_map.65 = (f32[2,6,2,128,128]{4,3,2,1,0:T(8,128)S(1)}, f32[2,128,128]{2,1,0:T(8,128)S(1)}) custom-call(f32[6,2,128,128]{3,2,1,0:T(8,128)S(1)} %get-tuple-element.49.total0, f32[2,2,2,128,128]{4,3,2,1,0:T(8,128)S(1)} %get-tuple-element.52.green, f32[2,2,2,128,128]{4,3,2,1,0:T(8,128)S(1)} %collective-permute-done.4.by_core, ...), custom_call_target="tpu_custom_call" | custom-call | flops 1000000 | bytes 10000 | tf_op jit(solution)/shard_map/pallas_call | solution.py:295
  25.4 0.0 collective-permute-done.3.across
  25.4 0.9 %shard_map.66 = (f32[6,2,128,128]{3,2,1,0:T(8,128)S(1)}, f32[2,2,128,128]{3,2,1,0:T(8,128)S(1)}, f32[2,2,128,128]{3,2,1,0:T(8,128)S(1)}, f32[2,128]{1,0:T(2,128)S(1)}) custom-call(s32[2,6]{1,0:T(2,128)S(1)} %get-tuple-element.37.neighbours, f32[2,4,6]{2,1,0:T(4,128)S(1)} %get-tuple-element.38.phonon, f32[2,6,128,128]{3,2,1,0:T(8,128)S(1)} %get-tuple-element.39.coupling, ...), custom_call_target="tpu_custom_call" | custom-call | flops 1000000 | bytes 10000 | tf_op jit(solution)/shard_map/pallas_call | solution.py:254
  26.3 2.4 %collective-permute-start.8 = (f32[2,2,128,128]{3,2,1,0:T(8,128)S(1)}, f32[2,2,128,128]{3,2,1,0:T(8,128)S(1)}, u32[]{:S(2)}, u32[]{:S(2)}) collective-permute-start(f32[2,2,128,128]{3,2,1,0:T(8,128)S(1)} %get-tuple-element.61), channel_id=1, source_target_pairs={{0,1},{1,0},{2,3},{3,2},{4,5},{5,4},{6,7},{7,6},{8,16},{9,17},{10,... | collective-permute-start | bytes 786440 | tf_op jit(solution)/shard_map/ppermute | solution.py:40
  28.8 0.0 collective-permute-start.9
  28.8 0.6 %collective-permute-done.6.cross0 = f32[2,2,128,128]{3,2,1,0:T(8,128)S(1)} collective-permute-done((f32[2,2,128,128]{3,2,1,0:T(8,128)S(1)}, f32[2,2,128,128]{3,2,1,0:T(8,128)S(1)}, u32[]{:S(2)}, u32[]{:S(2)}) %collective-permute-start.6) | collective-permute-done | bytes 262176 | tf_op jit(solution)/shard_map/ppermute | solution.py:40
  29.4 0.0 collective-permute-done.7.core0
  29.4 0.0 collective-permute-start.12
  29.4 1.6 %collective-permute-start.11 = (f32[2,128]{1,0:T(2,128)S(1)}, f32[2,128]{1,0:T(2,128)S(1)}, u32[]{:S(2)}, u32[]{:S(2)}) collective-permute-start(f32[2,128]{1,0:T(2,128)S(1)} %get-tuple-element.63.rest_0_), channel_id=1, source_target_pairs={{0,16},{8,24},{16,0},{24,8},{1,17},{9,25},{17,1},{25,9},{2,18},{10... | collective-permute-start | bytes 3080 | tf_op jit(solution)/shard_map/ppermute | solution.py:228
  30.9 0.3 collective-permute-start.10
  31.2 1.9 %collective-permute-done.8.cross1 = f32[2,2,128,128]{3,2,1,0:T(8,128)S(1)} collective-permute-done((f32[2,2,128,128]{3,2,1,0:T(8,128)S(1)}, f32[2,2,128,128]{3,2,1,0:T(8,128)S(1)}, u32[]{:S(2)}, u32[]{:S(2)}) %collective-permute-start.8) | collective-permute-done | bytes 262176 | tf_op jit(solution)/shard_map/ppermute | solution.py:40
  33.1 0.0 collective-permute-done.9.core1
  33.1 0.0 collective-permute-done.12.rest_3_
  33.1 0.0 collective-permute-done.11.rest_2_
  33.1 0.0 collective-permute-done.10.rest_1_
  33.2 1.5 %shard_map.67 = (f32[2,2,2,128,128]{4,3,2,1,0:T(8,128)}, f32[2,128]{1,0:T(2,128)}) custom-call(f32[6,2,128,128]{3,2,1,0:T(8,128)S(1)} %get-tuple-element.49.total0, f32[6,2,128,128]{3,2,1,0:T(8,128)S(1)} %get-tuple-element.55.total1, f32[2,2,128,128]{3,2,1,0:T(8,128)S(1)} %collective-permute-done.6.cross0, ...), custom_call_target="tpu_custom_call" | custom-call | flops 1000000 | bytes 2000000 | tf_op jit(solution)/shard_map/pallas_call | solution.py:314
Async XLA Ops:
  1.6 9.9 %collective-permute-start = (f32[2,2,128,128]{3,2,1,0:T(8,128)S(1)}, f32[2,2,128,128]{3,2,1,0:T(8,128)S(1)}, u32[]{:S(2)}, u32[]{:S(2)}) collective-permute-start(f32[2,2,128,128]{3,2,1,0:T(8,128)S(1)} %shard_map.59.green0), channel_id=1, source_target_pairs={{0,1},{2,3},{4,5},{6,7},{1,0},{3,2},{5,4},{7,6},{8,9},{10,11},{12,... | collective-permute-start | bytes 786440 | tf_op jit(solution)/shard_map/ppermute | solution.py:27
  6.1 18.8 %collective-permute-start.5 = (f32[2,2,2,128,128]{4,3,2,1,0:T(8,128)S(1)}, f32[2,2,2,128,128]{4,3,2,1,0:T(8,128)S(1)}, u32[]{:S(2)}, u32[]{:S(2)}) collective-permute-start(f32[2,2,2,128,128]{4,3,2,1,0:T(8,128)S(1)} %get-tuple-element.52.green), channel_id=1, source_target_pairs={{0,2},{1,3},{2,0},{3,1},{4,6},{5,7},{6,4},{7,5},{8,16},{9,17},{10,... | collective-permute-start | bytes 1572872 | tf_op jit(solution)/shard_map/ppermute | solution.py:40
  7.7 17.1 %collective-permute-start.4 = (f32[2,2,2,128,128]{4,3,2,1,0:T(8,128)S(1)}, f32[2,2,2,128,128]{4,3,2,1,0:T(8,128)S(1)}, u32[]{:S(2)}, u32[]{:S(2)}) collective-permute-start(f32[2,2,2,128,128]{4,3,2,1,0:T(8,128)S(1)} %get-tuple-element.52.green), channel_id=1, source_target_pairs={{0,8},{16,24},{8,0},{24,16},{1,9},{17,25},{9,1},{25,17},{2,10},{18... | collective-permute-start | bytes 1572872 | tf_op jit(solution)/shard_map/ppermute | solution.py:27
  7.7 9.1 %collective-permute-start.2 = (f32[2,2,128,128]{3,2,1,0:T(8,128)S(1)}, f32[2,2,128,128]{3,2,1,0:T(8,128)S(1)}, u32[]{:S(2)}, u32[]{:S(2)}) collective-permute-start(f32[2,2,128,128]{3,2,1,0:T(8,128)S(1)} %get-tuple-element.50.green1), channel_id=1, source_target_pairs={{0,1},{2,3},{4,5},{6,7},{1,0},{3,2},{5,4},{7,6},{8,9},{10,11},{12,... | collective-permute-start | bytes 786440 | tf_op jit(solution)/shard_map/ppermute | solution.py:27
  11.5 10.6 %collective-permute-start.1 = (f32[2,2,128,128]{3,2,1,0:T(8,128)S(1)}, f32[2,2,128,128]{3,2,1,0:T(8,128)S(1)}, u32[]{:S(2)}, u32[]{:S(2)}) collective-permute-start(f32[2,2,128,128]{3,2,1,0:T(8,128)S(1)} %collective-permute-done.ahead), channel_id=1, source_target_pairs={{0,2},{2,4},{4,6},{6,7},{1,0},{3,1},{5,3},{7,5},{8,10},{10,12},{12... | collective-permute-start | bytes 786440 | tf_op jit(solution)/shard_map/ppermute | solution.py:51
  14.9 10.5 %collective-permute-start.3 = (f32[2,2,128,128]{3,2,1,0:T(8,128)S(1)}, f32[2,2,128,128]{3,2,1,0:T(8,128)S(1)}, u32[]{:S(2)}, u32[]{:S(2)}) collective-permute-start(f32[2,2,128,128]{3,2,1,0:T(8,128)S(1)} %get-tuple-element.50.green1), channel_id=1, source_target_pairs={{1,2},{3,4},{5,6},{2,1},{4,3},{6,5},{9,10},{11,12},{13,14},{10,9},... | collective-permute-start | bytes 786440 | tf_op jit(solution)/shard_map/ppermute | solution.py:27
  22.9 6.4 %collective-permute-start.6 = (f32[2,2,128,128]{3,2,1,0:T(8,128)S(1)}, f32[2,2,128,128]{3,2,1,0:T(8,128)S(1)}, u32[]{:S(2)}, u32[]{:S(2)}) collective-permute-start(f32[2,2,128,128]{3,2,1,0:T(8,128)S(1)} %get-tuple-element.56), channel_id=1, source_target_pairs={{0,2},{1,3},{2,0},{3,1},{4,6},{5,7},{6,4},{7,5},{8,16},{9,17},{10,... | collective-permute-start | bytes 786440 | tf_op jit(solution)/shard_map/ppermute | solution.py:40
  24.0 5.3 %collective-permute-start.7 = (f32[2,2,128,128]{3,2,1,0:T(8,128)S(1)}, f32[2,2,128,128]{3,2,1,0:T(8,128)S(1)}, u32[]{:S(2)}, u32[]{:S(2)}) collective-permute-start(f32[2,2,128,128]{3,2,1,0:T(8,128)S(1)} %get-tuple-element.57), channel_id=1, source_target_pairs={{0,8},{16,24},{8,0},{24,16},{1,9},{17,25},{9,1},{25,17},{2,10},{18... | collective-permute-start | bytes 786440 | tf_op jit(solution)/shard_map/ppermute | solution.py:27
  26.3 6.8 %collective-permute-start.8 = (f32[2,2,128,128]{3,2,1,0:T(8,128)S(1)}, f32[2,2,128,128]{3,2,1,0:T(8,128)S(1)}, u32[]{:S(2)}, u32[]{:S(2)}) collective-permute-start(f32[2,2,128,128]{3,2,1,0:T(8,128)S(1)} %get-tuple-element.61), channel_id=1, source_target_pairs={{0,1},{1,0},{2,3},{3,2},{4,5},{5,4},{6,7},{7,6},{8,16},{9,17},{10,... | collective-permute-start | bytes 786440 | tf_op jit(solution)/shard_map/ppermute | solution.py:40
  28.8 4.4 %collective-permute-start.9 = (f32[2,2,128,128]{3,2,1,0:T(8,128)S(1)}, f32[2,2,128,128]{3,2,1,0:T(8,128)S(1)}, u32[]{:S(2)}, u32[]{:S(2)}) collective-permute-start(f32[2,2,128,128]{3,2,1,0:T(8,128)S(1)} %get-tuple-element.62), channel_id=1, source_target_pairs={{0,8},{16,24},{8,0},{24,16},{1,9},{17,25},{9,1},{25,17},{2,10},{18... | collective-permute-start | bytes 786440 | tf_op jit(solution)/shard_map/ppermute | solution.py:27
  29.4 3.8 %collective-permute-start.12 = (f32[2,128]{1,0:T(2,128)S(1)}, f32[2,128]{1,0:T(2,128)S(1)}, u32[]{:S(2)}, u32[]{:S(2)}) collective-permute-start(f32[2,128]{1,0:T(2,128)S(1)} %get-tuple-element.63.rest_0_), channel_id=1, source_target_pairs={{0,24},{8,16},{16,8},{24,0},{1,25},{9,17},{17,9},{25,1},{2,26},{10... | collective-permute-start | bytes 3080 | tf_op jit(solution)/shard_map/ppermute | solution.py:228
  29.4 3.8 %collective-permute-start.11 = (f32[2,128]{1,0:T(2,128)S(1)}, f32[2,128]{1,0:T(2,128)S(1)}, u32[]{:S(2)}, u32[]{:S(2)}) collective-permute-start(f32[2,128]{1,0:T(2,128)S(1)} %get-tuple-element.63.rest_0_), channel_id=1, source_target_pairs={{0,16},{8,24},{16,0},{24,8},{1,17},{9,25},{17,1},{25,9},{2,18},{10... | collective-permute-start | bytes 3080 | tf_op jit(solution)/shard_map/ppermute | solution.py:228
  30.9 2.2 %collective-permute-start.10 = (f32[2,128]{1,0:T(2,128)S(1)}, f32[2,128]{1,0:T(2,128)S(1)}, u32[]{:S(2)}, u32[]{:S(2)}) collective-permute-start(f32[2,128]{1,0:T(2,128)S(1)} %get-tuple-element.63.rest_0_), channel_id=1, source_target_pairs={{0,8},{8,0},{16,24},{24,16},{1,9},{9,1},{17,25},{25,17},{2,10},{10... | collective-permute-start | bytes 3080 | tf_op jit(solution)/shard_map/ppermute | solution.py:228

commit v10 on v6

--- a/solution.py
+++ b/solution.py
@@ -304,7 +304,7 @@
         (across1, total1, turned, partial),
     )
     core1, cross1 = swap(core1, "energy", 0), cross_swap(cross1, 1)
-    cross0, core0, rate = lax.optimization_barrier((cross0, core0, rate))
+    core0, cross0, rate = lax.optimization_barrier((core0, cross0, rate))
     rates = addends(rate, "energy")
     return pl.pallas_call(
         functools.partial(end_kernel, energies),

time: 34.1 us -> 35 us (1.026)
  Pallas kernels: 11.6 us -> 12.2 us
    ppermute x3, waiting for transfers between devices: 0.21 us -> 1.3 us  [addends(): return [x] + [lax.ppermute(x, axis, turn) for turn in turns]]
    ppermute x3, waiting for transfers between devices: 3.29 us -> 2.45 us  [exchange(): return lax.ppermute(x, ('energy', 'atom'), perm)]
    ppermute x3, starting transfers between devices: 4.76 us -> 5.4 us  [exchange(): return lax.ppermute(x, ('energy', 'atom'), perm)]
    ppermute x1, starting transfers between devices: 1.96 us -> 1.33 us  [forward(): return lax.ppermute(x, axis, [(i, j) for i, j in ups + downs if i != j])]
    pallas_call x5, Pallas kernels: 7.74 us -> 8.38 us  [call(): pl.pallas_call(kernel, out_shape=[jax.ShapeDtypeStruct(shape, jnp.float32...]
  transfers between devices with their start and end apart: 13 -> 13, of which waited for: 5 -> 5; matrix products, arithmetic and copies ran while one was open for 0% -> 0% of each run, Pallas kernels for 29% -> 30%
where the time goes in v10:
time: 35 us; the launch traced here: 34.8 us
  starting transfers between devices  12.9 us (37%)
  Pallas kernels  12.2 us (35%)
  waiting for transfers between devices  8.91 us (25%)
  between operations  0.73 us (2%)
    pallas_call x5, Pallas kernels, call(): pl.pallas_call(kernel, out_shape=[jax.ShapeDtypeStruct(shape, jnp.float32...  8.38 us
    ppermute x3, starting transfers between devices, exchange(): return lax.ppermute(x, ('energy', 'atom'), perm)  5.4 us
    ppermute x6, starting transfers between devices, swap(): lax.ppermute(x, axis, [(i, i + 1) for i in low] + [(i + 1, i) for i in low])  4.32 us
    ppermute x1, waiting for transfers between devices, forward(): return lax.ppermute(x, axis, [(i, j) for i, j in ups + downs if i != j])  3.9 us
    ppermute x3, waiting for transfers between devices, exchange(): return lax.ppermute(x, ('energy', 'atom'), perm)  2.45 us
    pallas_call x2, Pallas kernels, fetch(): pl.pallas_call(kernel, out_shape=[jax.ShapeDtypeStruct(x.shape, x.dtype)...  2.38 us
    ppermute x3, starting transfers between devices, addends(): return [x] + [lax.ppermute(x, axis, turn) for turn in turns]  1.89 us
    ppermute x1, starting transfers between devices, forward(): return lax.ppermute(x, axis, [(i, j) for i, j in ups + downs if i != j])  1.33 us
  transfers between devices with their start and end apart: 13, of which 5 were waited for; matrix products, arithmetic and copies ran while one was open for 0% of the time, Pallas kernels for 30%

profile of v10, /device:TPU:0, one launch (start us, length us, event | category | flops | bytes accessed | tf_op | source)
XLA Modules:
  0.0 34.8 jit_solution(11337650136087654424)
XLA Ops:
  0.6 1.0 %shard_map.59.green0 = f32[2,2,128,128]{3,2,1,0:T(8,128)S(1)} custom-call(f32[2,2,2,128,128]{4,3,2,1,0:T(8,128)} %green.2), custom_call_target="tpu_custom_call" | custom-call | tf_op jit(solution)/shard_map/pallas_call | solution.py:263
  1.6 3.0 %collective-permute-start = (f32[2,2,128,128]{3,2,1,0:T(8,128)S(1)}, f32[2,2,128,128]{3,2,1,0:T(8,128)S(1)}, u32[]{:S(2)}, u32[]{:S(2)}) collective-permute-start(f32[2,2,128,128]{3,2,1,0:T(8,128)S(1)} %shard_map.59.green0), channel_id=1, source_target_pairs={{0,1},{2,3},{4,5},{6,7},{1,0},{3,2},{5,4},{7,6},{8,9},{10,11},{12,... | collective-permute-start | bytes 786440 | tf_op jit(solution)/shard_map/ppermute | solution.py:27
  4.6 1.4 %shard_map.60 = (f32[2,2,128,128]{3,2,1,0:T(8,128)S(1)}, f32[2,2,2,128,128]{4,3,2,1,0:T(8,128)S(1)}, f32[2,6,128,128]{3,2,1,0:T(8,128)S(1)}, f32[2,4,6]{2,1,0:T(4,128)S(1)}, s32[2,6]{1,0:T(2,128)S(1)}) custom-call(f32[2,2,2,128,128]{4,3,2,1,0:T(8,128)} %green.2, f32[2,6,128,128]{3,2,1,0:T(8,128)} %coupling, f32[2,4,6]{2,1,0:T(4,128)} %bitcast.1, s32[2,6]{1,0:T(2,128)} %neighbours), custom_call_target="tpu_custom_call" | custom-call | tf_op jit(solution)/shard_map/pallas_call | solution.py:263
  6.1 1.6 %collective-permute-start.5 = (f32[2,2,2,128,128]{4,3,2,1,0:T(8,128)S(1)}, f32[2,2,2,128,128]{4,3,2,1,0:T(8,128)S(1)}, u32[]{:S(2)}, u32[]{:S(2)}) collective-permute-start(f32[2,2,2,128,128]{4,3,2,1,0:T(8,128)S(1)} %get-tuple-element.52.green), channel_id=1, source_target_pairs={{0,2},{1,3},{2,0},{3,1},{4,6},{5,7},{6,4},{7,5},{8,16},{9,17},{10,... | collective-permute-start | bytes 1572872 | tf_op jit(solution)/shard_map/ppermute | solution.py:40
  7.7 0.0 collective-permute-start.4
  7.7 0.5 %collective-permute-start.2 = (f32[2,2,128,128]{3,2,1,0:T(8,128)S(1)}, f32[2,2,128,128]{3,2,1,0:T(8,128)S(1)}, u32[]{:S(2)}, u32[]{:S(2)}) collective-permute-start(f32[2,2,128,128]{3,2,1,0:T(8,128)S(1)} %get-tuple-element.50.green1), channel_id=1, source_target_pairs={{0,1},{2,3},{4,5},{6,7},{1,0},{3,2},{5,4},{7,6},{8,9},{10,11},{12,... | collective-permute-start | bytes 786440 | tf_op jit(solution)/shard_map/ppermute | solution.py:27
  8.2 3.9 %shard_map.61 = (f32[6,2,128,128]{3,2,1,0:T(8,128)S(1)}, f32[6,2,128,128]{3,2,1,0:T(8,128)S(1)}) custom-call(s32[2,6]{1,0:T(2,128)S(1)} %get-tuple-element.37.neighbours, f32[2,4,6]{2,1,0:T(4,128)S(1)} %get-tuple-element.38.phonon, f32[2,6,128,128]{3,2,1,0:T(8,128)S(1)} %get-tuple-element.39.coupling, f32[2,2,128,128]{3,2,1,0:T(8,128)S(1)} %shard_map.59.green0, ...), custom_call_target="tpu_custom_call" | custom-call | flops 1000000 | bytes 10000 | tf_op jit(solution)/shard_map/pallas_call | solution.py:249
  12.2 0.0 collective-permute-done.ahead
  12.2 1.3 %collective-permute-start.1 = (f32[2,2,128,128]{3,2,1,0:T(8,128)S(1)}, f32[2,2,128,128]{3,2,1,0:T(8,128)S(1)}, u32[]{:S(2)}, u32[]{:S(2)}) collective-permute-start(f32[2,2,128,128]{3,2,1,0:T(8,128)S(1)} %collective-permute-done.ahead), channel_id=1, source_target_pairs={{0,2},{2,4},{4,6},{6,7},{1,0},{3,1},{5,3},{7,5},{8,10},{10,12},{12... | collective-permute-start | bytes 786440 | tf_op jit(solution)/shard_map/ppermute | solution.py:51
  13.5 1.4 %shard_map.62.before = f32[6,2,128,128]{3,2,1,0:T(8,128)S(1)} custom-call(s32[2,6]{1,0:T(2,128)S(1)} %get-tuple-element.37.neighbours, f32[2,4,6]{2,1,0:T(4,128)S(1)} %get-tuple-element.38.phonon, f32[2,6,128,128]{3,2,1,0:T(8,128)S(1)} %get-tuple-element.39.coupling, f32[2,2,128,128]{3,2,1,0:T(8,128)S(1)} %collective-permute-done.ahead, ...), custom_call_target="tpu_custom_call" | custom-call | flops 1000000 | bytes 10000 | tf_op jit(solution)/shard_map/pallas_call | solution.py:249
  14.9 0.7 %collective-permute-start.3 = (f32[2,2,128,128]{3,2,1,0:T(8,128)S(1)}, f32[2,2,128,128]{3,2,1,0:T(8,128)S(1)}, u32[]{:S(2)}, u32[]{:S(2)}) collective-permute-start(f32[2,2,128,128]{3,2,1,0:T(8,128)S(1)} %get-tuple-element.50.green1), channel_id=1, source_target_pairs={{1,2},{3,4},{5,6},{2,1},{4,3},{6,5},{9,10},{11,12},{13,14},{10,9},... | collective-permute-start | bytes 786440 | tf_op jit(solution)/shard_map/ppermute | solution.py:27
  15.6 1.3 %collective-permute-done.2.ahead = f32[2,2,128,128]{3,2,1,0:T(8,128)S(1)} collective-permute-done((f32[2,2,128,128]{3,2,1,0:T(8,128)S(1)}, f32[2,2,128,128]{3,2,1,0:T(8,128)S(1)}, u32[]{:S(2)}, u32[]{:S(2)}) %collective-permute-start.2) | collective-permute-done | bytes 262176 | tf_op jit(solution)/shard_map/ppermute | solution.py:27
  16.8 1.4 %shard_map.63.before = f32[6,2,128,128]{3,2,1,0:T(8,128)S(1)} custom-call(s32[2,6]{1,0:T(2,128)S(1)} %get-tuple-element.37.neighbours, f32[2,4,6]{2,1,0:T(4,128)S(1)} %get-tuple-element.38.phonon, f32[2,6,128,128]{3,2,1,0:T(8,128)S(1)} %get-tuple-element.39.coupling, f32[2,2,128,128]{3,2,1,0:T(8,128)S(1)} %collective-permute-done.2.ahead, ...), custom_call_target="tpu_custom_call" | custom-call | flops 1000000 | bytes 10000 | tf_op jit(solution)/shard_map/pallas_call | solution.py:249
  18.3 3.9 %collective-permute-done.1.across = f32[2,2,128,128]{3,2,1,0:T(8,128)S(1)} collective-permute-done((f32[2,2,128,128]{3,2,1,0:T(8,128)S(1)}, f32[2,2,128,128]{3,2,1,0:T(8,128)S(1)}, u32[]{:S(2)}, u32[]{:S(2)}) %collective-permute-start.1) | collective-permute-done | bytes 262176 | tf_op jit(solution)/shard_map/ppermute | solution.py:51
  22.2 0.7 %shard_map.64 = (f32[6,2,128,128]{3,2,1,0:T(8,128)S(1)}, f32[2,2,128,128]{3,2,1,0:T(8,128)S(1)}, f32[2,2,128,128]{3,2,1,0:T(8,128)S(1)}) custom-call(s32[2,6]{1,0:T(2,128)S(1)} %get-tuple-element.37.neighbours, f32[2,4,6]{2,1,0:T(4,128)S(1)} %get-tuple-element.38.phonon, f32[2,6,128,128]{3,2,1,0:T(8,128)S(1)} %get-tuple-element.39.coupling, ...), custom_call_target="tpu_custom_call" | custom-call | flops 1000000 | bytes 10000 | tf_op jit(solution)/shard_map/pallas_call | solution.py:249
  22.9 0.1 collective-permute-start.6
  23.0 1.1 %collective-permute-start.7 = (f32[2,2,128,128]{3,2,1,0:T(8,128)S(1)}, f32[2,2,128,128]{3,2,1,0:T(8,128)S(1)}, u32[]{:S(2)}, u32[]{:S(2)}) collective-permute-start(f32[2,2,128,128]{3,2,1,0:T(8,128)S(1)} %get-tuple-element.57), channel_id=1, source_target_pairs={{0,2},{1,3},{2,0},{3,1},{4,6},{5,7},{6,4},{7,5},{8,16},{9,17},{10,... | collective-permute-start | bytes 786440 | tf_op jit(solution)/shard_map/ppermute | solution.py:40
  24.1 0.0 collective-permute-done.5.by_cross
  24.1 0.0 collective-permute-done.4.by_core
  24.1 0.6 %shard_map.65 = (f32[2,6,2,128,128]{4,3,2,1,0:T(8,128)S(1)}, f32[2,128,128]{2,1,0:T(8,128)S(1)}) custom-call(f32[6,2,128,128]{3,2,1,0:T(8,128)S(1)} %get-tuple-element.49.total0, f32[2,2,2,128,128]{4,3,2,1,0:T(8,128)S(1)} %get-tuple-element.52.green, f32[2,2,2,128,128]{4,3,2,1,0:T(8,128)S(1)} %collective-permute-done.4.by_core, ...), custom_call_target="tpu_custom_call" | custom-call | flops 1000000 | bytes 10000 | tf_op jit(solution)/shard_map/pallas_call | solution.py:290
  24.7 0.0 collective-permute-done.3.across
  24.7 0.9 %shard_map.66 = (f32[6,2,128,128]{3,2,1,0:T(8,128)S(1)}, f32[2,2,128,128]{3,2,1,0:T(8,128)S(1)}, f32[2,2,128,128]{3,2,1,0:T(8,128)S(1)}, f32[2,128]{1,0:T(2,128)S(1)}) custom-call(s32[2,6]{1,0:T(2,128)S(1)} %get-tuple-element.37.neighbours, f32[2,4,6]{2,1,0:T(4,128)S(1)} %get-tuple-element.38.phonon, f32[2,6,128,128]{3,2,1,0:T(8,128)S(1)} %get-tuple-element.39.coupling, ...), custom_call_target="tpu_custom_call" | custom-call | flops 1000000 | bytes 10000 | tf_op jit(solution)/shard_map/pallas_call | solution.py:249
  25.6 2.6 %collective-permute-start.8 = (f32[2,2,128,128]{3,2,1,0:T(8,128)S(1)}, f32[2,2,128,128]{3,2,1,0:T(8,128)S(1)}, u32[]{:S(2)}, u32[]{:S(2)}) collective-permute-start(f32[2,2,128,128]{3,2,1,0:T(8,128)S(1)} %get-tuple-element.61), channel_id=1, source_target_pairs={{0,1},{1,0},{2,3},{3,2},{4,5},{5,4},{6,7},{7,6},{8,16},{9,17},{10,... | collective-permute-start | bytes 786440 | tf_op jit(solution)/shard_map/ppermute | solution.py:40
  28.3 0.0 collective-permute-start.9
  28.3 0.0 collective-permute-done.6.core0
  28.3 1.2 %collective-permute-done.7.cross0 = f32[2,2,128,128]{3,2,1,0:T(8,128)S(1)} collective-permute-done((f32[2,2,128,128]{3,2,1,0:T(8,128)S(1)}, f32[2,2,128,128]{3,2,1,0:T(8,128)S(1)}, u32[]{:S(2)}, u32[]{:S(2)}) %collective-permute-start.7) | collective-permute-done | bytes 262176 | tf_op jit(solution)/shard_map/ppermute | solution.py:40
  29.4 0.9 %collective-permute-start.12 = (f32[2,128]{1,0:T(2,128)S(1)}, f32[2,128]{1,0:T(2,128)S(1)}, u32[]{:S(2)}, u32[]{:S(2)}) collective-permute-start(f32[2,128]{1,0:T(2,128)S(1)} %get-tuple-element.63.rest_0_), channel_id=1, source_target_pairs={{0,24},{8,16},{16,8},{24,0},{1,25},{9,17},{17,9},{25,1},{2,26},{10... | collective-permute-start | bytes 3080 | tf_op jit(solution)/shard_map/ppermute | solution.py:228
  30.3 0.9 %collective-permute-start.11 = (f32[2,128]{1,0:T(2,128)S(1)}, f32[2,128]{1,0:T(2,128)S(1)}, u32[]{:S(2)}, u32[]{:S(2)}) collective-permute-start(f32[2,128]{1,0:T(2,128)S(1)} %get-tuple-element.63.rest_0_), channel_id=1, source_target_pairs={{0,16},{8,24},{16,0},{24,8},{1,17},{9,25},{17,1},{25,9},{2,18},{10... | collective-permute-start | bytes 3080 | tf_op jit(solution)/shard_map/ppermute | solution.py:228
  31.2 0.1 collective-permute-start.10
  31.3 1.3 %collective-permute-done.8.cross1 = f32[2,2,128,128]{3,2,1,0:T(8,128)S(1)} collective-permute-done((f32[2,2,128,128]{3,2,1,0:T(8,128)S(1)}, f32[2,2,128,128]{3,2,1,0:T(8,128)S(1)}, u32[]{:S(2)}, u32[]{:S(2)}) %collective-permute-start.8) | collective-permute-done | bytes 262176 | tf_op jit(solution)/shard_map/ppermute | solution.py:40
  32.6 0.0 collective-permute-done.9.core1
  32.6 0.0 collective-permute-done.12.rest_3_
  32.6 1.3 %collective-permute-done.11.rest_2_ = f32[2,128]{1,0:T(2,128)S(1)} collective-permute-done((f32[2,128]{1,0:T(2,128)S(1)}, f32[2,128]{1,0:T(2,128)S(1)}, u32[]{:S(2)}, u32[]{:S(2)}) %collective-permute-start.11) | collective-permute-done | bytes 1056 | tf_op jit(solution)/shard_map/ppermute | solution.py:228
  33.9 0.0 collective-permute-done.10.rest_1_
  33.9 0.9 %shard_map.67 = (f32[2,2,2,128,128]{4,3,2,1,0:T(8,128)}, f32[2,128]{1,0:T(2,128)}) custom-call(f32[6,2,128,128]{3,2,1,0:T(8,128)S(1)} %get-tuple-element.49.total0, f32[6,2,128,128]{3,2,1,0:T(8,128)S(1)} %get-tuple-element.55.total1, f32[2,2,128,128]{3,2,1,0:T(8,128)S(1)} %collective-permute-done.7.cross0, ...), custom_call_target="tpu_custom_call" | custom-call | flops 1000000 | bytes 2000000 | tf_op jit(solution)/shard_map/pallas_call | solution.py:309
Async XLA Ops:
  1.6 10.6 %collective-permute-start = (f32[2,2,128,128]{3,2,1,0:T(8,128)S(1)}, f32[2,2,128,128]{3,2,1,0:T(8,128)S(1)}, u32[]{:S(2)}, u32[]{:S(2)}) collective-permute-start(f32[2,2,128,128]{3,2,1,0:T(8,128)S(1)} %shard_map.59.green0), channel_id=1, source_target_pairs={{0,1},{2,3},{4,5},{6,7},{1,0},{3,2},{5,4},{7,6},{8,9},{10,11},{12,... | collective-permute-start | bytes 786440 | tf_op jit(solution)/shard_map/ppermute | solution.py:27
  6.1 18.1 %collective-permute-start.5 = (f32[2,2,2,128,128]{4,3,2,1,0:T(8,128)S(1)}, f32[2,2,2,128,128]{4,3,2,1,0:T(8,128)S(1)}, u32[]{:S(2)}, u32[]{:S(2)}) collective-permute-start(f32[2,2,2,128,128]{4,3,2,1,0:T(8,128)S(1)} %get-tuple-element.52.green), channel_id=1, source_target_pairs={{0,2},{1,3},{2,0},{3,1},{4,6},{5,7},{6,4},{7,5},{8,16},{9,17},{10,... | collective-permute-start | bytes 1572872 | tf_op jit(solution)/shard_map/ppermute | solution.py:40
  7.7 16.4 %collective-permute-start.4 = (f32[2,2,2,128,128]{4,3,2,1,0:T(8,128)S(1)}, f32[2,2,2,128,128]{4,3,2,1,0:T(8,128)S(1)}, u32[]{:S(2)}, u32[]{:S(2)}) collective-permute-start(f32[2,2,2,128,128]{4,3,2,1,0:T(8,128)S(1)} %get-tuple-element.52.green), channel_id=1, source_target_pairs={{0,8},{16,24},{8,0},{24,16},{1,9},{17,25},{9,1},{25,17},{2,10},{18... | collective-permute-start | bytes 1572872 | tf_op jit(solution)/shard_map/ppermute | solution.py:27
  7.7 9.1 %collective-permute-start.2 = (f32[2,2,128,128]{3,2,1,0:T(8,128)S(1)}, f32[2,2,128,128]{3,2,1,0:T(8,128)S(1)}, u32[]{:S(2)}, u32[]{:S(2)}) collective-permute-start(f32[2,2,128,128]{3,2,1,0:T(8,128)S(1)} %get-tuple-element.50.green1), channel_id=1, source_target_pairs={{0,1},{2,3},{4,5},{6,7},{1,0},{3,2},{5,4},{7,6},{8,9},{10,11},{12,... | collective-permute-start | bytes 786440 | tf_op jit(solution)/shard_map/ppermute | solution.py:27
  12.2 10.0 %collective-permute-start.1 = (f32[2,2,128,128]{3,2,1,0:T(8,128)S(1)}, f32[2,2,128,128]{3,2,1,0:T(8,128)S(1)}, u32[]{:S(2)}, u32[]{:S(2)}) collective-permute-start(f32[2,2,128,128]{3,2,1,0:T(8,128)S(1)} %collective-permute-done.ahead), channel_id=1, source_target_pairs={{0,2},{2,4},{4,6},{6,7},{1,0},{3,1},{5,3},{7,5},{8,10},{10,12},{12... | collective-permute-start | bytes 786440 | tf_op jit(solution)/shard_map/ppermute | solution.py:51
  14.9 9.8 %collective-permute-start.3 = (f32[2,2,128,128]{3,2,1,0:T(8,128)S(1)}, f32[2,2,128,128]{3,2,1,0:T(8,128)S(1)}, u32[]{:S(2)}, u32[]{:S(2)}) collective-permute-start(f32[2,2,128,128]{3,2,1,0:T(8,128)S(1)} %get-tuple-element.50.green1), channel_id=1, source_target_pairs={{1,2},{3,4},{5,6},{2,1},{4,3},{6,5},{9,10},{11,12},{13,14},{10,9},... | collective-permute-start | bytes 786440 | tf_op jit(solution)/shard_map/ppermute | solution.py:27
  22.9 5.3 %collective-permute-start.6 = (f32[2,2,128,128]{3,2,1,0:T(8,128)S(1)}, f32[2,2,128,128]{3,2,1,0:T(8,128)S(1)}, u32[]{:S(2)}, u32[]{:S(2)}) collective-permute-start(f32[2,2,128,128]{3,2,1,0:T(8,128)S(1)} %get-tuple-element.56), channel_id=1, source_target_pairs={{0,8},{16,24},{8,0},{24,16},{1,9},{17,25},{9,1},{25,17},{2,10},{18... | collective-permute-start | bytes 786440 | tf_op jit(solution)/shard_map/ppermute | solution.py:27
  23.0 6.4 %collective-permute-start.7 = (f32[2,2,128,128]{3,2,1,0:T(8,128)S(1)}, f32[2,2,128,128]{3,2,1,0:T(8,128)S(1)}, u32[]{:S(2)}, u32[]{:S(2)}) collective-permute-start(f32[2,2,128,128]{3,2,1,0:T(8,128)S(1)} %get-tuple-element.57), channel_id=1, source_target_pairs={{0,2},{1,3},{2,0},{3,1},{4,6},{5,7},{6,4},{7,5},{8,16},{9,17},{10,... | collective-permute-start | bytes 786440 | tf_op jit(solution)/shard_map/ppermute | solution.py:40
  25.6 7.0 %collective-permute-start.8 = (f32[2,2,128,128]{3,2,1,0:T(8,128)S(1)}, f32[2,2,128,128]{3,2,1,0:T(8,128)S(1)}, u32[]{:S(2)}, u32[]{:S(2)}) collective-permute-start(f32[2,2,128,128]{3,2,1,0:T(8,128)S(1)} %get-tuple-element.61), channel_id=1, source_target_pairs={{0,1},{1,0},{2,3},{3,2},{4,5},{5,4},{6,7},{7,6},{8,16},{9,17},{10,... | collective-permute-start | bytes 786440 | tf_op jit(solution)/shard_map/ppermute | solution.py:40
  28.3 4.4 %collective-permute-start.9 = (f32[2,2,128,128]{3,2,1,0:T(8,128)S(1)}, f32[2,2,128,128]{3,2,1,0:T(8,128)S(1)}, u32[]{:S(2)}, u32[]{:S(2)}) collective-permute-start(f32[2,2,128,128]{3,2,1,0:T(8,128)S(1)} %get-tuple-element.62), channel_id=1, source_target_pairs={{0,8},{16,24},{8,0},{24,16},{1,9},{17,25},{9,1},{25,17},{2,10},{18... | collective-permute-start | bytes 786440 | tf_op jit(solution)/shard_map/ppermute | solution.py:27
  29.4 3.2 %collective-permute-start.12 = (f32[2,128]{1,0:T(2,128)S(1)}, f32[2,128]{1,0:T(2,128)S(1)}, u32[]{:S(2)}, u32[]{:S(2)}) collective-permute-start(f32[2,128]{1,0:T(2,128)S(1)} %get-tuple-element.63.rest_0_), channel_id=1, source_target_pairs={{0,24},{8,16},{16,8},{24,0},{1,25},{9,17},{17,9},{25,1},{2,26},{10... | collective-permute-start | bytes 3080 | tf_op jit(solution)/shard_map/ppermute | solution.py:228
  30.3 3.6 %collective-permute-start.11 = (f32[2,128]{1,0:T(2,128)S(1)}, f32[2,128]{1,0:T(2,128)S(1)}, u32[]{:S(2)}, u32[]{:S(2)}) collective-permute-start(f32[2,128]{1,0:T(2,128)S(1)} %get-tuple-element.63.rest_0_), channel_id=1, source_target_pairs={{0,16},{8,24},{16,0},{24,8},{1,17},{9,25},{17,1},{25,9},{2,18},{10... | collective-permute-start | bytes 3080 | tf_op jit(solution)/shard_map/ppermute | solution.py:228
  31.2 2.7 %collective-permute-start.10 = (f32[2,128]{1,0:T(2,128)S(1)}, f32[2,128]{1,0:T(2,128)S(1)}, u32[]{:S(2)}, u32[]{:S(2)}) collective-permute-start(f32[2,128]{1,0:T(2,128)S(1)} %get-tuple-element.63.rest_0_), channel_id=1, source_target_pairs={{0,8},{8,0},{16,24},{24,16},{1,9},{9,1},{17,25},{25,17},{2,10},{10... | collective-permute-start | bytes 3080 | tf_op jit(solution)/shard_map/ppermute | solution.py:228
